TPU v7x, 256 devices: a whole 4x4x8 slice. The times are simulated.
256 devices in a mesh: blk: 64 (over z, x, y_lo), jac: 4 (over y_hi, core).
Axes of the slice: x: 4, y: 4 (y_hi: 2, y_lo: 2; y = y_hi * 2 + y_lo), z: 8, core: 2. Of those that a mesh axis runs over, the one named last changes fastest.
Arguments:
- coefficients: bfloat16 [16384, 4096], P('blk', 'jac'), may hold values from -0.09375 to 0.09375
- jacobi_matrix: bfloat16 [4096, 4096], P(None, 'jac'), may hold values from -12 to 12, as said below
- jac_limit: int32 [16384], P('blk'), may hold values from 1024 to 4096, as said below
Outputs:
- band_out: float32 [16384, 33, 256], P(('blk', 'jac'))
Inputs may be any that keep to these rules, and one draw needn't show every extreme that they name: `jac_limit`: every value from 1024 to 4096 may occur; both ends occur in every draw. `jacobi_matrix`: Symmetric.
All inputs are finite; a program needn't handle non-finite values.
Results may differ from a plain program's by a relative error of at most 0.0029.
Values may be sent and summed in bfloat16 or wider, within the bound.
No kernel may reach another device: no remote copies, remote signals or barrier semaphores. Data moves between devices by JAX's collectives and lax.ppermute only.
A program may use at most 64 MiB of HBM per device.

v0:
```python
import jax
import jax.numpy as jnp
from jax import lax
from jax.sharding import PartitionSpec as P


def passed_along(block, axis, distance):
    devices = range(lax.axis_size(axis))
    route = [((i - distance) % len(devices), i) for i in devices]
    return lax.ppermute(block, axis, route)


def per_device(coefficients, jacobi_matrix, jac_limit):
    panel_rows, panel_cols = coefficients.shape
    half_cycle = lax.axis_size("blk") // 2
    offset = lax.axis_index("jac") * panel_cols
    columns = offset + lax.broadcasted_iota(jnp.int32, (panel_rows, panel_cols), 1)
    masked = jnp.where(columns < jac_limit[:, None], coefficients, jnp.zeros_like(coefficients))
    folded = jnp.dot(
        lax.all_gather(masked, "jac", axis=1, tiled=True),
        jacobi_matrix,
        preferred_element_type=jnp.float32,
    )
    product = folded.astype(jnp.bfloat16)
    position = lax.axis_index("blk")

    def tile_for(panel_in, step_index):
        result = lax.dot_general(
            product, panel_in, (((1,), (1,)), ((), ())), preferred_element_type=jnp.float32
        )
        keep_tile = jnp.logical_or(step_index < half_cycle, position < half_cycle)
        return jnp.where(keep_tile, result, jnp.zeros_like(result))

    band_out = jnp.zeros((panel_rows, half_cycle + 1, panel_rows), jnp.float32)

    def place_tile(band_in, result, step_index):
        return lax.dynamic_update_slice(band_in, result[:, None, :], (0, step_index, 0))

    band_out = place_tile(band_out, tile_for(masked, 0), 0)

    def forward(step_index, loop_state):
        band_in, panel_in = loop_state
        panel_in = passed_along(panel_in, "blk", -1)
        return (place_tile(band_in, tile_for(panel_in, step_index), step_index), panel_in)

    band_out, _ = lax.fori_loop(1, half_cycle + 1, forward, (band_out, masked))
    band_out = lax.psum_scatter(band_out, "jac", scatter_dimension=0, tiled=True)
    return band_out


def solution(mesh):
    in_specs = (P("blk", "jac"), P(None, "jac"), P("blk"))
    out_specs = P(("blk", "jac"), None, None)
    return jax.shard_map(
        per_device, mesh=mesh, in_specs=in_specs, out_specs=out_specs, check_vma=False
    )
```

profile of v0, /device:TPU:6, one launch (start us, length us, event | category | flops | bytes accessed | tf_op | source)
XLA Modules:
  0.0 681.4 jit_solution(6990821125354048929)
XLA Ops:
  6.5 2.0 compare_select_fusion
  8.7 32.7 %all-gather.2.cloned.1.call-done = bf16[256,4096]{1,0:T(8,128)(2,1)} async-done(((bf16[256,1024]{1,0:T(8,128)(2,1)}), bf16[256,4096]{1,0:T(8,128)(2,1)}) %all-gather.2.cloned.1.call-update) | async-done | bytes 2097168 | tf_op jit(solution)/shard_map/all_gather | solution.py:20
  41.3 6.3 convolution_convert_fusion
  48.0 4.3 dynamic_update_slice.15
  52.4 505.6 %while.19 = (s32[]{:T(128)}, f32[256,33,256]{2,0,1:T(8,128)}, bf16[256,1024]{1,0:T(8,128)(2,1)S(1)}, pred[]{:T(512)}, bf16[256,1024]{1,0:T(8,128)(2,1)S(1)}, /*index=5*/s32[]{:T(128)}, s32[]{:T(128)}, s32[]{:T(128)}, s32[]{:T(128)}) while((s32[]{:T(128)}, f32[256,33,256]{2,0,1:T(8,128)}, bf16[256,1024]{1,0:T(8,128)(2,1)S(1)}, pred[]{:T(512)}, ...), condition=%wide.region_1.2_spmd, body=%wide.region_0.1_spmd.sunk | while | flops 134283264 | bytes 4456632 | solution.py:46
  53.2 13.2 %collective-permute-done = bf16[256,1024]{1,0:T(8,128)(2,1)S(1)} collective-permute-done((bf16[256,1024]{1,0:T(8,128)(2,1)S(1)}, bf16[256,1024]{1,0:T(8,128)(2,1)S(1)}, u32[]{:S(2)}, u32[]{:S(2)}) %collective-permute-start) | collective-permute-done | bytes 524320 | tf_op jit(solution)/shard_map/while/body/eval_jaxpr/ppermute | solution.py:10
  67.5 1.8 collective-permute-start
  69.3 13.3 %collective-permute-done = bf16[256,1024]{1,0:T(8,128)(2,1)S(1)} collective-permute-done((bf16[256,1024]{1,0:T(8,128)(2,1)S(1)}, bf16[256,1024]{1,0:T(8,128)(2,1)S(1)}, u32[]{:S(2)}, u32[]{:S(2)}) %collective-permute-start) | collective-permute-done | bytes 524320 | tf_op jit(solution)/shard_map/while/body/eval_jaxpr/ppermute | solution.py:10
  84.5 14.5 %collective-permute-done = bf16[256,1024]{1,0:T(8,128)(2,1)S(1)} collective-permute-done((bf16[256,1024]{1,0:T(8,128)(2,1)S(1)}, bf16[256,1024]{1,0:T(8,128)(2,1)S(1)}, u32[]{:S(2)}, u32[]{:S(2)}) %collective-permute-start) | collective-permute-done | bytes 524320 | tf_op jit(solution)/shard_map/while/body/eval_jaxpr/ppermute | solution.py:10
  100.1 14.4 %collective-permute-done = bf16[256,1024]{1,0:T(8,128)(2,1)S(1)} collective-permute-done((bf16[256,1024]{1,0:T(8,128)(2,1)S(1)}, bf16[256,1024]{1,0:T(8,128)(2,1)S(1)}, u32[]{:S(2)}, u32[]{:S(2)}) %collective-permute-start) | collective-permute-done | bytes 524320 | tf_op jit(solution)/shard_map/while/body/eval_jaxpr/ppermute | solution.py:10
  115.6 13.5 %collective-permute-done = bf16[256,1024]{1,0:T(8,128)(2,1)S(1)} collective-permute-done((bf16[256,1024]{1,0:T(8,128)(2,1)S(1)}, bf16[256,1024]{1,0:T(8,128)(2,1)S(1)}, u32[]{:S(2)}, u32[]{:S(2)}) %collective-permute-start) | collective-permute-done | bytes 524320 | tf_op jit(solution)/shard_map/while/body/eval_jaxpr/ppermute | solution.py:10
  130.2 12.6 %collective-permute-done = bf16[256,1024]{1,0:T(8,128)(2,1)S(1)} collective-permute-done((bf16[256,1024]{1,0:T(8,128)(2,1)S(1)}, bf16[256,1024]{1,0:T(8,128)(2,1)S(1)}, u32[]{:S(2)}, u32[]{:S(2)}) %collective-permute-start) | collective-permute-done | bytes 524320 | tf_op jit(solution)/shard_map/while/body/eval_jaxpr/ppermute | solution.py:10
  143.9 11.9 %collective-permute-done = bf16[256,1024]{1,0:T(8,128)(2,1)S(1)} collective-permute-done((bf16[256,1024]{1,0:T(8,128)(2,1)S(1)}, bf16[256,1024]{1,0:T(8,128)(2,1)S(1)}, u32[]{:S(2)}, u32[]{:S(2)}) %collective-permute-start) | collective-permute-done | bytes 524320 | tf_op jit(solution)/shard_map/while/body/eval_jaxpr/ppermute | solution.py:10
  156.9 12.6 %collective-permute-done = bf16[256,1024]{1,0:T(8,128)(2,1)S(1)} collective-permute-done((bf16[256,1024]{1,0:T(8,128)(2,1)S(1)}, bf16[256,1024]{1,0:T(8,128)(2,1)S(1)}, u32[]{:S(2)}, u32[]{:S(2)}) %collective-permute-start) | collective-permute-done | bytes 524320 | tf_op jit(solution)/shard_map/while/body/eval_jaxpr/ppermute | solution.py:10
  170.6 14.0 %collective-permute-done = bf16[256,1024]{1,0:T(8,128)(2,1)S(1)} collective-permute-done((bf16[256,1024]{1,0:T(8,128)(2,1)S(1)}, bf16[256,1024]{1,0:T(8,128)(2,1)S(1)}, u32[]{:S(2)}, u32[]{:S(2)}) %collective-permute-start) | collective-permute-done | bytes 524320 | tf_op jit(solution)/shard_map/while/body/eval_jaxpr/ppermute | solution.py:10
  185.7 15.1 %collective-permute-done = bf16[256,1024]{1,0:T(8,128)(2,1)S(1)} collective-permute-done((bf16[256,1024]{1,0:T(8,128)(2,1)S(1)}, bf16[256,1024]{1,0:T(8,128)(2,1)S(1)}, u32[]{:S(2)}, u32[]{:S(2)}) %collective-permute-start) | collective-permute-done | bytes 524320 | tf_op jit(solution)/shard_map/while/body/eval_jaxpr/ppermute | solution.py:10
  201.9 16.1 %collective-permute-done = bf16[256,1024]{1,0:T(8,128)(2,1)S(1)} collective-permute-done((bf16[256,1024]{1,0:T(8,128)(2,1)S(1)}, bf16[256,1024]{1,0:T(8,128)(2,1)S(1)}, u32[]{:S(2)}, u32[]{:S(2)}) %collective-permute-start) | collective-permute-done | bytes 524320 | tf_op jit(solution)/shard_map/while/body/eval_jaxpr/ppermute | solution.py:10
  218.0 1.1 fusion.13
  219.1 17.3 %collective-permute-done = bf16[256,1024]{1,0:T(8,128)(2,1)S(1)} collective-permute-done((bf16[256,1024]{1,0:T(8,128)(2,1)S(1)}, bf16[256,1024]{1,0:T(8,128)(2,1)S(1)}, u32[]{:S(2)}, u32[]{:S(2)}) %collective-permute-start) | collective-permute-done | bytes 524320 | tf_op jit(solution)/shard_map/while/body/eval_jaxpr/ppermute | solution.py:10
  237.5 17.7 %collective-permute-done = bf16[256,1024]{1,0:T(8,128)(2,1)S(1)} collective-permute-done((bf16[256,1024]{1,0:T(8,128)(2,1)S(1)}, bf16[256,1024]{1,0:T(8,128)(2,1)S(1)}, u32[]{:S(2)}, u32[]{:S(2)}) %collective-permute-start) | collective-permute-done | bytes 524320 | tf_op jit(solution)/shard_map/while/body/eval_jaxpr/ppermute | solution.py:10
  256.3 16.3 %collective-permute-done = bf16[256,1024]{1,0:T(8,128)(2,1)S(1)} collective-permute-done((bf16[256,1024]{1,0:T(8,128)(2,1)S(1)}, bf16[256,1024]{1,0:T(8,128)(2,1)S(1)}, u32[]{:S(2)}, u32[]{:S(2)}) %collective-permute-start) | collective-permute-done | bytes 524320 | tf_op jit(solution)/shard_map/while/body/eval_jaxpr/ppermute | solution.py:10
  273.6 15.3 %collective-permute-done = bf16[256,1024]{1,0:T(8,128)(2,1)S(1)} collective-permute-done((bf16[256,1024]{1,0:T(8,128)(2,1)S(1)}, bf16[256,1024]{1,0:T(8,128)(2,1)S(1)}, u32[]{:S(2)}, u32[]{:S(2)}) %collective-permute-start) | collective-permute-done | bytes 524320 | tf_op jit(solution)/shard_map/while/body/eval_jaxpr/ppermute | solution.py:10
  290.1 14.4 %collective-permute-done = bf16[256,1024]{1,0:T(8,128)(2,1)S(1)} collective-permute-done((bf16[256,1024]{1,0:T(8,128)(2,1)S(1)}, bf16[256,1024]{1,0:T(8,128)(2,1)S(1)}, u32[]{:S(2)}, u32[]{:S(2)}) %collective-permute-start) | collective-permute-done | bytes 524320 | tf_op jit(solution)/shard_map/while/body/eval_jaxpr/ppermute | solution.py:10
  305.6 13.5 %collective-permute-done = bf16[256,1024]{1,0:T(8,128)(2,1)S(1)} collective-permute-done((bf16[256,1024]{1,0:T(8,128)(2,1)S(1)}, bf16[256,1024]{1,0:T(8,128)(2,1)S(1)}, u32[]{:S(2)}, u32[]{:S(2)}) %collective-permute-start) | collective-permute-done | bytes 524320 | tf_op jit(solution)/shard_map/while/body/eval_jaxpr/ppermute | solution.py:10
  320.2 12.6 %collective-permute-done = bf16[256,1024]{1,0:T(8,128)(2,1)S(1)} collective-permute-done((bf16[256,1024]{1,0:T(8,128)(2,1)S(1)}, bf16[256,1024]{1,0:T(8,128)(2,1)S(1)}, u32[]{:S(2)}, u32[]{:S(2)}) %collective-permute-start) | collective-permute-done | bytes 524320 | tf_op jit(solution)/shard_map/while/body/eval_jaxpr/ppermute | solution.py:10
  332.8 1.1 fusion.13
  333.9 11.9 %collective-permute-done = bf16[256,1024]{1,0:T(8,128)(2,1)S(1)} collective-permute-done((bf16[256,1024]{1,0:T(8,128)(2,1)S(1)}, bf16[256,1024]{1,0:T(8,128)(2,1)S(1)}, u32[]{:S(2)}, u32[]{:S(2)}) %collective-permute-start) | collective-permute-done | bytes 524320 | tf_op jit(solution)/shard_map/while/body/eval_jaxpr/ppermute | solution.py:10
  346.9 12.6 %collective-permute-done = bf16[256,1024]{1,0:T(8,128)(2,1)S(1)} collective-permute-done((bf16[256,1024]{1,0:T(8,128)(2,1)S(1)}, bf16[256,1024]{1,0:T(8,128)(2,1)S(1)}, u32[]{:S(2)}, u32[]{:S(2)}) %collective-permute-start) | collective-permute-done | bytes 524320 | tf_op jit(solution)/shard_map/while/body/eval_jaxpr/ppermute | solution.py:10
  360.7 14.0 %collective-permute-done = bf16[256,1024]{1,0:T(8,128)(2,1)S(1)} collective-permute-done((bf16[256,1024]{1,0:T(8,128)(2,1)S(1)}, bf16[256,1024]{1,0:T(8,128)(2,1)S(1)}, u32[]{:S(2)}, u32[]{:S(2)}) %collective-permute-start) | collective-permute-done | bytes 524320 | tf_op jit(solution)/shard_map/while/body/eval_jaxpr/ppermute | solution.py:10
  375.7 15.1 %collective-permute-done = bf16[256,1024]{1,0:T(8,128)(2,1)S(1)} collective-permute-done((bf16[256,1024]{1,0:T(8,128)(2,1)S(1)}, bf16[256,1024]{1,0:T(8,128)(2,1)S(1)}, u32[]{:S(2)}, u32[]{:S(2)}) %collective-permute-start) | collective-permute-done | bytes 524320 | tf_op jit(solution)/shard_map/while/body/eval_jaxpr/ppermute | solution.py:10
  391.9 16.2 %collective-permute-done = bf16[256,1024]{1,0:T(8,128)(2,1)S(1)} collective-permute-done((bf16[256,1024]{1,0:T(8,128)(2,1)S(1)}, bf16[256,1024]{1,0:T(8,128)(2,1)S(1)}, u32[]{:S(2)}, u32[]{:S(2)}) %collective-permute-start) | collective-permute-done | bytes 524320 | tf_op jit(solution)/shard_map/while/body/eval_jaxpr/ppermute | solution.py:10
  409.2 17.3 %collective-permute-done = bf16[256,1024]{1,0:T(8,128)(2,1)S(1)} collective-permute-done((bf16[256,1024]{1,0:T(8,128)(2,1)S(1)}, bf16[256,1024]{1,0:T(8,128)(2,1)S(1)}, u32[]{:S(2)}, u32[]{:S(2)}) %collective-permute-start) | collective-permute-done | bytes 524320 | tf_op jit(solution)/shard_map/while/body/eval_jaxpr/ppermute | solution.py:10
  427.6 17.7 %collective-permute-done = bf16[256,1024]{1,0:T(8,128)(2,1)S(1)} collective-permute-done((bf16[256,1024]{1,0:T(8,128)(2,1)S(1)}, bf16[256,1024]{1,0:T(8,128)(2,1)S(1)}, u32[]{:S(2)}, u32[]{:S(2)}) %collective-permute-start) | collective-permute-done | bytes 524320 | tf_op jit(solution)/shard_map/while/body/eval_jaxpr/ppermute | solution.py:10
  445.3 1.1 fusion.13
  446.4 16.3 %collective-permute-done = bf16[256,1024]{1,0:T(8,128)(2,1)S(1)} collective-permute-done((bf16[256,1024]{1,0:T(8,128)(2,1)S(1)}, bf16[256,1024]{1,0:T(8,128)(2,1)S(1)}, u32[]{:S(2)}, u32[]{:S(2)}) %collective-permute-start) | collective-permute-done | bytes 524320 | tf_op jit(solution)/shard_map/while/body/eval_jaxpr/ppermute | solution.py:10
  463.8 15.4 %collective-permute-done = bf16[256,1024]{1,0:T(8,128)(2,1)S(1)} collective-permute-done((bf16[256,1024]{1,0:T(8,128)(2,1)S(1)}, bf16[256,1024]{1,0:T(8,128)(2,1)S(1)}, u32[]{:S(2)}, u32[]{:S(2)}) %collective-permute-start) | collective-permute-done | bytes 524320 | tf_op jit(solution)/shard_map/while/body/eval_jaxpr/ppermute | solution.py:10
  480.2 14.4 %collective-permute-done = bf16[256,1024]{1,0:T(8,128)(2,1)S(1)} collective-permute-done((bf16[256,1024]{1,0:T(8,128)(2,1)S(1)}, bf16[256,1024]{1,0:T(8,128)(2,1)S(1)}, u32[]{:S(2)}, u32[]{:S(2)}) %collective-permute-start) | collective-permute-done | bytes 524320 | tf_op jit(solution)/shard_map/while/body/eval_jaxpr/ppermute | solution.py:10
  495.7 3.2 collective-permute-start
  498.9 11.3 %collective-permute-done = bf16[256,1024]{1,0:T(8,128)(2,1)S(1)} collective-permute-done((bf16[256,1024]{1,0:T(8,128)(2,1)S(1)}, bf16[256,1024]{1,0:T(8,128)(2,1)S(1)}, u32[]{:S(2)}, u32[]{:S(2)}) %collective-permute-start) | collective-permute-done | bytes 524320 | tf_op jit(solution)/shard_map/while/body/eval_jaxpr/ppermute | solution.py:10
  511.3 7.3 %collective-permute-start = (bf16[256,1024]{1,0:T(8,128)(2,1)S(1)}, bf16[256,1024]{1,0:T(8,128)(2,1)S(1)}, u32[]{:S(2)}, u32[]{:S(2)}) collective-permute-start(bf16[256,1024]{1,0:T(8,128)(2,1)S(1)} %get-tuple-element.224), channel_id=1, source_target_pairs={{4,0},{8,4},{12,8},{16,12},{20,16},{24,20},{28,24},{32,28},{36,32}... | collective-permute-start | bytes 1572872 | tf_op jit(solution)/shard_map/while/body/eval_jaxpr/ppermute | solution.py:10
  518.6 10.2 %collective-permute-done = bf16[256,1024]{1,0:T(8,128)(2,1)S(1)} collective-permute-done((bf16[256,1024]{1,0:T(8,128)(2,1)S(1)}, bf16[256,1024]{1,0:T(8,128)(2,1)S(1)}, u32[]{:S(2)}, u32[]{:S(2)}) %collective-permute-start) | collective-permute-done | bytes 524320 | tf_op jit(solution)/shard_map/while/body/eval_jaxpr/ppermute | solution.py:10
  529.8 7.0 %collective-permute-start = (bf16[256,1024]{1,0:T(8,128)(2,1)S(1)}, bf16[256,1024]{1,0:T(8,128)(2,1)S(1)}, u32[]{:S(2)}, u32[]{:S(2)}) collective-permute-start(bf16[256,1024]{1,0:T(8,128)(2,1)S(1)} %get-tuple-element.224), channel_id=1, source_target_pairs={{4,0},{8,4},{12,8},{16,12},{20,16},{24,20},{28,24},{32,28},{36,32}... | collective-permute-start | bytes 1572872 | tf_op jit(solution)/shard_map/while/body/eval_jaxpr/ppermute | solution.py:10
  536.8 6.7 collective-permute-done
  543.6 1.1 fusion.13
  544.7 5.5 collective-permute-start
  550.2 6.7 collective-permute-done
  556.9 1.1 fusion.13
  558.0 116.5 %reduce-scatter.2.cloned.1.call-done = f32[64,33,256]{2,0,1:T(8,128)} async-done(((f32[256,33,256]{2,0,1:T(8,128)}), f32[64,33,256]{2,0,1:T(8,128)}) %reduce-scatter.2.cloned.1.call-update) | async-done | bytes 2162704 | tf_op jit(solution)/shard_map/reduce_scatter | solution.py:47
  (94 shorter events, 31.7 us)
Async XLA Ops:
  6.5 34.8 %all-gather.2.cloned.1.call-start = ((), (), s32[]{:S(2)}) async-start(), calls=%async_computation.1 | async-start | bytes 2621440 | tf_op jit(solution)/shard_map/all_gather | solution.py:20
  8.6 666.0 %reduce-scatter.2.cloned.1.call-start = ((), (), s32[]{:S(2)}) async-start(), calls=%async_computation.2 | async-start | bytes 10813440 | tf_op jit(solution)/shard_map/reduce_scatter | solution.py:47
  8.6 39.0 %copy-start = (bf16[256,1024]{1,0:T(8,128)(2,1)S(1)}, bf16[256,1024]{1,0:T(8,128)(2,1)}, u32[]{:S(2)}) copy-start(bf16[256,1024]{1,0:T(8,128)(2,1)} %compare_select_fusion) | copy-start | bytes 1572868
  52.4 14.1 %collective-permute-start = (bf16[256,1024]{1,0:T(8,128)(2,1)S(1)}, bf16[256,1024]{1,0:T(8,128)(2,1)S(1)}, u32[]{:S(2)}, u32[]{:S(2)}) collective-permute-start(bf16[256,1024]{1,0:T(8,128)(2,1)S(1)} %get-tuple-element.224), channel_id=1, source_target_pairs={{4,0},{8,4},{12,8},{16,12},{20,16},{24,20},{28,24},{32,28},{36,32}... | collective-permute-start | bytes 1572872 | tf_op jit(solution)/shard_map/while/body/eval_jaxpr/ppermute | solution.py:10
  67.5 15.1 %collective-permute-start = (bf16[256,1024]{1,0:T(8,128)(2,1)S(1)}, bf16[256,1024]{1,0:T(8,128)(2,1)S(1)}, u32[]{:S(2)}, u32[]{:S(2)}) collective-permute-start(bf16[256,1024]{1,0:T(8,128)(2,1)S(1)} %get-tuple-element.224), channel_id=1, source_target_pairs={{4,0},{8,4},{12,8},{16,12},{20,16},{24,20},{28,24},{32,28},{36,32}... | collective-permute-start | bytes 1572872 | tf_op jit(solution)/shard_map/while/body/eval_jaxpr/ppermute | solution.py:10
  83.7 15.3 %collective-permute-start = (bf16[256,1024]{1,0:T(8,128)(2,1)S(1)}, bf16[256,1024]{1,0:T(8,128)(2,1)S(1)}, u32[]{:S(2)}, u32[]{:S(2)}) collective-permute-start(bf16[256,1024]{1,0:T(8,128)(2,1)S(1)} %get-tuple-element.224), channel_id=1, source_target_pairs={{4,0},{8,4},{12,8},{16,12},{20,16},{24,20},{28,24},{32,28},{36,32}... | collective-permute-start | bytes 1572872 | tf_op jit(solution)/shard_map/while/body/eval_jaxpr/ppermute | solution.py:10
  100.1 14.4 %collective-permute-start = (bf16[256,1024]{1,0:T(8,128)(2,1)S(1)}, bf16[256,1024]{1,0:T(8,128)(2,1)S(1)}, u32[]{:S(2)}, u32[]{:S(2)}) collective-permute-start(bf16[256,1024]{1,0:T(8,128)(2,1)S(1)} %get-tuple-element.224), channel_id=1, source_target_pairs={{4,0},{8,4},{12,8},{16,12},{20,16},{24,20},{28,24},{32,28},{36,32}... | collective-permute-start | bytes 1572872 | tf_op jit(solution)/shard_map/while/body/eval_jaxpr/ppermute | solution.py:10
  115.6 13.5 %collective-permute-start = (bf16[256,1024]{1,0:T(8,128)(2,1)S(1)}, bf16[256,1024]{1,0:T(8,128)(2,1)S(1)}, u32[]{:S(2)}, u32[]{:S(2)}) collective-permute-start(bf16[256,1024]{1,0:T(8,128)(2,1)S(1)} %get-tuple-element.224), channel_id=1, source_target_pairs={{4,0},{8,4},{12,8},{16,12},{20,16},{24,20},{28,24},{32,28},{36,32}... | collective-permute-start | bytes 1572872 | tf_op jit(solution)/shard_map/while/body/eval_jaxpr/ppermute | solution.py:10
  130.2 12.6 %collective-permute-start = (bf16[256,1024]{1,0:T(8,128)(2,1)S(1)}, bf16[256,1024]{1,0:T(8,128)(2,1)S(1)}, u32[]{:S(2)}, u32[]{:S(2)}) collective-permute-start(bf16[256,1024]{1,0:T(8,128)(2,1)S(1)} %get-tuple-element.224), channel_id=1, source_target_pairs={{4,0},{8,4},{12,8},{16,12},{20,16},{24,20},{28,24},{32,28},{36,32}... | collective-permute-start | bytes 1572872 | tf_op jit(solution)/shard_map/while/body/eval_jaxpr/ppermute | solution.py:10
  143.9 11.9 %collective-permute-start = (bf16[256,1024]{1,0:T(8,128)(2,1)S(1)}, bf16[256,1024]{1,0:T(8,128)(2,1)S(1)}, u32[]{:S(2)}, u32[]{:S(2)}) collective-permute-start(bf16[256,1024]{1,0:T(8,128)(2,1)S(1)} %get-tuple-element.224), channel_id=1, source_target_pairs={{4,0},{8,4},{12,8},{16,12},{20,16},{24,20},{28,24},{32,28},{36,32}... | collective-permute-start | bytes 1572872 | tf_op jit(solution)/shard_map/while/body/eval_jaxpr/ppermute | solution.py:10
  156.9 12.6 %collective-permute-start = (bf16[256,1024]{1,0:T(8,128)(2,1)S(1)}, bf16[256,1024]{1,0:T(8,128)(2,1)S(1)}, u32[]{:S(2)}, u32[]{:S(2)}) collective-permute-start(bf16[256,1024]{1,0:T(8,128)(2,1)S(1)} %get-tuple-element.224), channel_id=1, source_target_pairs={{4,0},{8,4},{12,8},{16,12},{20,16},{24,20},{28,24},{32,28},{36,32}... | collective-permute-start | bytes 1572872 | tf_op jit(solution)/shard_map/while/body/eval_jaxpr/ppermute | solution.py:10
  170.6 14.0 %collective-permute-start = (bf16[256,1024]{1,0:T(8,128)(2,1)S(1)}, bf16[256,1024]{1,0:T(8,128)(2,1)S(1)}, u32[]{:S(2)}, u32[]{:S(2)}) collective-permute-start(bf16[256,1024]{1,0:T(8,128)(2,1)S(1)} %get-tuple-element.224), channel_id=1, source_target_pairs={{4,0},{8,4},{12,8},{16,12},{20,16},{24,20},{28,24},{32,28},{36,32}... | collective-permute-start | bytes 1572872 | tf_op jit(solution)/shard_map/while/body/eval_jaxpr/ppermute | solution.py:10
  185.7 15.1 %collective-permute-start = (bf16[256,1024]{1,0:T(8,128)(2,1)S(1)}, bf16[256,1024]{1,0:T(8,128)(2,1)S(1)}, u32[]{:S(2)}, u32[]{:S(2)}) collective-permute-start(bf16[256,1024]{1,0:T(8,128)(2,1)S(1)} %get-tuple-element.224), channel_id=1, source_target_pairs={{4,0},{8,4},{12,8},{16,12},{20,16},{24,20},{28,24},{32,28},{36,32}... | collective-permute-start | bytes 1572872 | tf_op jit(solution)/shard_map/while/body/eval_jaxpr/ppermute | solution.py:10
  201.8 16.1 %collective-permute-start = (bf16[256,1024]{1,0:T(8,128)(2,1)S(1)}, bf16[256,1024]{1,0:T(8,128)(2,1)S(1)}, u32[]{:S(2)}, u32[]{:S(2)}) collective-permute-start(bf16[256,1024]{1,0:T(8,128)(2,1)S(1)} %get-tuple-element.224), channel_id=1, source_target_pairs={{4,0},{8,4},{12,8},{16,12},{20,16},{24,20},{28,24},{32,28},{36,32}... | collective-permute-start | bytes 1572872 | tf_op jit(solution)/shard_map/while/body/eval_jaxpr/ppermute | solution.py:10
  219.1 17.4 %collective-permute-start = (bf16[256,1024]{1,0:T(8,128)(2,1)S(1)}, bf16[256,1024]{1,0:T(8,128)(2,1)S(1)}, u32[]{:S(2)}, u32[]{:S(2)}) collective-permute-start(bf16[256,1024]{1,0:T(8,128)(2,1)S(1)} %get-tuple-element.224), channel_id=1, source_target_pairs={{4,0},{8,4},{12,8},{16,12},{20,16},{24,20},{28,24},{32,28},{36,32}... | collective-permute-start | bytes 1572872 | tf_op jit(solution)/shard_map/while/body/eval_jaxpr/ppermute | solution.py:10
  237.5 17.7 %collective-permute-start = (bf16[256,1024]{1,0:T(8,128)(2,1)S(1)}, bf16[256,1024]{1,0:T(8,128)(2,1)S(1)}, u32[]{:S(2)}, u32[]{:S(2)}) collective-permute-start(bf16[256,1024]{1,0:T(8,128)(2,1)S(1)} %get-tuple-element.224), channel_id=1, source_target_pairs={{4,0},{8,4},{12,8},{16,12},{20,16},{24,20},{28,24},{32,28},{36,32}... | collective-permute-start | bytes 1572872 | tf_op jit(solution)/shard_map/while/body/eval_jaxpr/ppermute | solution.py:10
  256.3 16.3 %collective-permute-start = (bf16[256,1024]{1,0:T(8,128)(2,1)S(1)}, bf16[256,1024]{1,0:T(8,128)(2,1)S(1)}, u32[]{:S(2)}, u32[]{:S(2)}) collective-permute-start(bf16[256,1024]{1,0:T(8,128)(2,1)S(1)} %get-tuple-element.224), channel_id=1, source_target_pairs={{4,0},{8,4},{12,8},{16,12},{20,16},{24,20},{28,24},{32,28},{36,32}... | collective-permute-start | bytes 1572872 | tf_op jit(solution)/shard_map/while/body/eval_jaxpr/ppermute | solution.py:10
  273.6 15.3 %collective-permute-start = (bf16[256,1024]{1,0:T(8,128)(2,1)S(1)}, bf16[256,1024]{1,0:T(8,128)(2,1)S(1)}, u32[]{:S(2)}, u32[]{:S(2)}) collective-permute-start(bf16[256,1024]{1,0:T(8,128)(2,1)S(1)} %get-tuple-element.224), channel_id=1, source_target_pairs={{4,0},{8,4},{12,8},{16,12},{20,16},{24,20},{28,24},{32,28},{36,32}... | collective-permute-start | bytes 1572872 | tf_op jit(solution)/shard_map/while/body/eval_jaxpr/ppermute | solution.py:10
  290.1 14.4 %collective-permute-start = (bf16[256,1024]{1,0:T(8,128)(2,1)S(1)}, bf16[256,1024]{1,0:T(8,128)(2,1)S(1)}, u32[]{:S(2)}, u32[]{:S(2)}) collective-permute-start(bf16[256,1024]{1,0:T(8,128)(2,1)S(1)} %get-tuple-element.224), channel_id=1, source_target_pairs={{4,0},{8,4},{12,8},{16,12},{20,16},{24,20},{28,24},{32,28},{36,32}... | collective-permute-start | bytes 1572872 | tf_op jit(solution)/shard_map/while/body/eval_jaxpr/ppermute | solution.py:10
  305.6 13.5 %collective-permute-start = (bf16[256,1024]{1,0:T(8,128)(2,1)S(1)}, bf16[256,1024]{1,0:T(8,128)(2,1)S(1)}, u32[]{:S(2)}, u32[]{:S(2)}) collective-permute-start(bf16[256,1024]{1,0:T(8,128)(2,1)S(1)} %get-tuple-element.224), channel_id=1, source_target_pairs={{4,0},{8,4},{12,8},{16,12},{20,16},{24,20},{28,24},{32,28},{36,32}... | collective-permute-start | bytes 1572872 | tf_op jit(solution)/shard_map/while/body/eval_jaxpr/ppermute | solution.py:10
  320.2 12.6 %collective-permute-start = (bf16[256,1024]{1,0:T(8,128)(2,1)S(1)}, bf16[256,1024]{1,0:T(8,128)(2,1)S(1)}, u32[]{:S(2)}, u32[]{:S(2)}) collective-permute-start(bf16[256,1024]{1,0:T(8,128)(2,1)S(1)} %get-tuple-element.224), channel_id=1, source_target_pairs={{4,0},{8,4},{12,8},{16,12},{20,16},{24,20},{28,24},{32,28},{36,32}... | collective-permute-start | bytes 1572872 | tf_op jit(solution)/shard_map/while/body/eval_jaxpr/ppermute | solution.py:10
  333.9 11.9 %collective-permute-start = (bf16[256,1024]{1,0:T(8,128)(2,1)S(1)}, bf16[256,1024]{1,0:T(8,128)(2,1)S(1)}, u32[]{:S(2)}, u32[]{:S(2)}) collective-permute-start(bf16[256,1024]{1,0:T(8,128)(2,1)S(1)} %get-tuple-element.224), channel_id=1, source_target_pairs={{4,0},{8,4},{12,8},{16,12},{20,16},{24,20},{28,24},{32,28},{36,32}... | collective-permute-start | bytes 1572872 | tf_op jit(solution)/shard_map/while/body/eval_jaxpr/ppermute | solution.py:10
  346.9 12.6 %collective-permute-start = (bf16[256,1024]{1,0:T(8,128)(2,1)S(1)}, bf16[256,1024]{1,0:T(8,128)(2,1)S(1)}, u32[]{:S(2)}, u32[]{:S(2)}) collective-permute-start(bf16[256,1024]{1,0:T(8,128)(2,1)S(1)} %get-tuple-element.224), channel_id=1, source_target_pairs={{4,0},{8,4},{12,8},{16,12},{20,16},{24,20},{28,24},{32,28},{36,32}... | collective-permute-start | bytes 1572872 | tf_op jit(solution)/shard_map/while/body/eval_jaxpr/ppermute | solution.py:10
  360.6 14.0 %collective-permute-start = (bf16[256,1024]{1,0:T(8,128)(2,1)S(1)}, bf16[256,1024]{1,0:T(8,128)(2,1)S(1)}, u32[]{:S(2)}, u32[]{:S(2)}) collective-permute-start(bf16[256,1024]{1,0:T(8,128)(2,1)S(1)} %get-tuple-element.224), channel_id=1, source_target_pairs={{4,0},{8,4},{12,8},{16,12},{20,16},{24,20},{28,24},{32,28},{36,32}... | collective-permute-start | bytes 1572872 | tf_op jit(solution)/shard_map/while/body/eval_jaxpr/ppermute | solution.py:10
  375.7 15.1 %collective-permute-start = (bf16[256,1024]{1,0:T(8,128)(2,1)S(1)}, bf16[256,1024]{1,0:T(8,128)(2,1)S(1)}, u32[]{:S(2)}, u32[]{:S(2)}) collective-permute-start(bf16[256,1024]{1,0:T(8,128)(2,1)S(1)} %get-tuple-element.224), channel_id=1, source_target_pairs={{4,0},{8,4},{12,8},{16,12},{20,16},{24,20},{28,24},{32,28},{36,32}... | collective-permute-start | bytes 1572872 | tf_op jit(solution)/shard_map/while/body/eval_jaxpr/ppermute | solution.py:10
  391.9 16.2 %collective-permute-start = (bf16[256,1024]{1,0:T(8,128)(2,1)S(1)}, bf16[256,1024]{1,0:T(8,128)(2,1)S(1)}, u32[]{:S(2)}, u32[]{:S(2)}) collective-permute-start(bf16[256,1024]{1,0:T(8,128)(2,1)S(1)} %get-tuple-element.224), channel_id=1, source_target_pairs={{4,0},{8,4},{12,8},{16,12},{20,16},{24,20},{28,24},{32,28},{36,32}... | collective-permute-start | bytes 1572872 | tf_op jit(solution)/shard_map/while/body/eval_jaxpr/ppermute | solution.py:10
  409.2 17.3 %collective-permute-start = (bf16[256,1024]{1,0:T(8,128)(2,1)S(1)}, bf16[256,1024]{1,0:T(8,128)(2,1)S(1)}, u32[]{:S(2)}, u32[]{:S(2)}) collective-permute-start(bf16[256,1024]{1,0:T(8,128)(2,1)S(1)} %get-tuple-element.224), channel_id=1, source_target_pairs={{4,0},{8,4},{12,8},{16,12},{20,16},{24,20},{28,24},{32,28},{36,32}... | collective-permute-start | bytes 1572872 | tf_op jit(solution)/shard_map/while/body/eval_jaxpr/ppermute | solution.py:10
  427.6 17.7 %collective-permute-start = (bf16[256,1024]{1,0:T(8,128)(2,1)S(1)}, bf16[256,1024]{1,0:T(8,128)(2,1)S(1)}, u32[]{:S(2)}, u32[]{:S(2)}) collective-permute-start(bf16[256,1024]{1,0:T(8,128)(2,1)S(1)} %get-tuple-element.224), channel_id=1, source_target_pairs={{4,0},{8,4},{12,8},{16,12},{20,16},{24,20},{28,24},{32,28},{36,32}... | collective-permute-start | bytes 1572872 | tf_op jit(solution)/shard_map/while/body/eval_jaxpr/ppermute | solution.py:10
  446.4 16.3 %collective-permute-start = (bf16[256,1024]{1,0:T(8,128)(2,1)S(1)}, bf16[256,1024]{1,0:T(8,128)(2,1)S(1)}, u32[]{:S(2)}, u32[]{:S(2)}) collective-permute-start(bf16[256,1024]{1,0:T(8,128)(2,1)S(1)} %get-tuple-element.224), channel_id=1, source_target_pairs={{4,0},{8,4},{12,8},{16,12},{20,16},{24,20},{28,24},{32,28},{36,32}... | collective-permute-start | bytes 1572872 | tf_op jit(solution)/shard_map/while/body/eval_jaxpr/ppermute | solution.py:10
  463.8 15.4 %collective-permute-start = (bf16[256,1024]{1,0:T(8,128)(2,1)S(1)}, bf16[256,1024]{1,0:T(8,128)(2,1)S(1)}, u32[]{:S(2)}, u32[]{:S(2)}) collective-permute-start(bf16[256,1024]{1,0:T(8,128)(2,1)S(1)} %get-tuple-element.224), channel_id=1, source_target_pairs={{4,0},{8,4},{12,8},{16,12},{20,16},{24,20},{28,24},{32,28},{36,32}... | collective-permute-start | bytes 1572872 | tf_op jit(solution)/shard_map/while/body/eval_jaxpr/ppermute | solution.py:10
  480.2 14.4 %collective-permute-start = (bf16[256,1024]{1,0:T(8,128)(2,1)S(1)}, bf16[256,1024]{1,0:T(8,128)(2,1)S(1)}, u32[]{:S(2)}, u32[]{:S(2)}) collective-permute-start(bf16[256,1024]{1,0:T(8,128)(2,1)S(1)} %get-tuple-element.224), channel_id=1, source_target_pairs={{4,0},{8,4},{12,8},{16,12},{20,16},{24,20},{28,24},{32,28},{36,32}... | collective-permute-start | bytes 1572872 | tf_op jit(solution)/shard_map/while/body/eval_jaxpr/ppermute | solution.py:10
  495.7 14.5 %collective-permute-start = (bf16[256,1024]{1,0:T(8,128)(2,1)S(1)}, bf16[256,1024]{1,0:T(8,128)(2,1)S(1)}, u32[]{:S(2)}, u32[]{:S(2)}) collective-permute-start(bf16[256,1024]{1,0:T(8,128)(2,1)S(1)} %get-tuple-element.224), channel_id=1, source_target_pairs={{4,0},{8,4},{12,8},{16,12},{20,16},{24,20},{28,24},{32,28},{36,32}... | collective-permute-start | bytes 1572872 | tf_op jit(solution)/shard_map/while/body/eval_jaxpr/ppermute | solution.py:10
  511.3 17.5 %collective-permute-start = (bf16[256,1024]{1,0:T(8,128)(2,1)S(1)}, bf16[256,1024]{1,0:T(8,128)(2,1)S(1)}, u32[]{:S(2)}, u32[]{:S(2)}) collective-permute-start(bf16[256,1024]{1,0:T(8,128)(2,1)S(1)} %get-tuple-element.224), channel_id=1, source_target_pairs={{4,0},{8,4},{12,8},{16,12},{20,16},{24,20},{28,24},{32,28},{36,32}... | collective-permute-start | bytes 1572872 | tf_op jit(solution)/shard_map/while/body/eval_jaxpr/ppermute | solution.py:10
  529.8 13.7 %collective-permute-start = (bf16[256,1024]{1,0:T(8,128)(2,1)S(1)}, bf16[256,1024]{1,0:T(8,128)(2,1)S(1)}, u32[]{:S(2)}, u32[]{:S(2)}) collective-permute-start(bf16[256,1024]{1,0:T(8,128)(2,1)S(1)} %get-tuple-element.224), channel_id=1, source_target_pairs={{4,0},{8,4},{12,8},{16,12},{20,16},{24,20},{28,24},{32,28},{36,32}... | collective-permute-start | bytes 1572872 | tf_op jit(solution)/shard_map/while/body/eval_jaxpr/ppermute | solution.py:10
  544.7 12.2 %collective-permute-start = (bf16[256,1024]{1,0:T(8,128)(2,1)S(1)}, bf16[256,1024]{1,0:T(8,128)(2,1)S(1)}, u32[]{:S(2)}, u32[]{:S(2)}) collective-permute-start(bf16[256,1024]{1,0:T(8,128)(2,1)S(1)} %get-tuple-element.224), channel_id=1, source_target_pairs={{4,0},{8,4},{12,8},{16,12},{20,16},{24,20},{28,24},{32,28},{36,32}... | collective-permute-start | bytes 1572872 | tf_op jit(solution)/shard_map/while/body/eval_jaxpr/ppermute | solution.py:10
Sparse Core Ops, SparseCore 0:
  9.2 32.0 all-gather.1
  558.1 116.3 reduce-scatter.1
where the time goes:
time: 682 us; the launch traced here: 681 us
  waiting for transfers between devices  593 us (87%)
  matrix products  40.4 us (6%)
  starting transfers between devices  26.6 us (4%)
  between operations  13.4 us (2%)
    ppermute x32, waiting for transfers between devices, passed_along(): return lax.ppermute(block, axis, route)  444 us
    reduce_scatter x1, waiting for transfers between devices, per_device(): lax.psum_scatter(band_out, 'jac', scatter_dimension=0, tiled=True)  117 us
    dot_general x33, matrix products, tile_for(): lax.dot_general(product, panel_in, (((1,), (1,)), ((), ())), preferred_el...  34.1 us
    all_gather x1, waiting for transfers between devices, per_device(): lax.all_gather(masked, 'jac', axis=1, tiled=True)  32.7 us
    ppermute x32, starting transfers between devices, passed_along(): return lax.ppermute(block, axis, route)  26.6 us
  transfers between devices with their start and end apart: 34, of which 34 were waited for; matrix products, arithmetic and copies ran while one was open for 0% of the time, Pallas kernels for 0%

commit v1 on v0

v1 whole, which is shorter than its diff:
```python
import jax
import jax.numpy as jnp
from jax import lax
from jax.experimental import pallas as pl
from jax.experimental.pallas import tpu as pltpu
from jax.sharding import Mesh, PartitionSpec as P

WIDE = 4
VMEM = pl.BlockSpec(memory_space=pltpu.VMEM)
SMEM = pl.BlockSpec(memory_space=pltpu.SMEM)
BF16, F32 = jnp.bfloat16, jnp.float32
TRANSPOSED = (((1,), (1,)), ((), ()))


def shift(block, axis, distance):
    n = lax.axis_size(axis)
    return lax.ppermute(block, axis, [((i + distance) % n, i) for i in range(n)])


def across_and_flip(block):
    return lax.ppermute(block, ("l", "h"), [(i, 3 - i) for i in range(4)])


def call(kernel, out_shape, args, scratch=(), flops=0, limit=20):
    moved = sum(a.size * a.dtype.itemsize for a in args)
    return pl.pallas_call(
        kernel,
        out_shape=out_shape,
        in_specs=[SMEM] + [VMEM] * (len(args) - 1),
        out_specs=jax.tree.map(lambda _: VMEM, out_shape),
        scratch_shapes=list(scratch),
        compiler_params=pltpu.CompilerParams(vmem_limit_bytes=limit * 2**20),
        cost_estimate=pl.CostEstimate(flops=flops, bytes_accessed=moved, transcendentals=0),
    )(*args)


def like(rows, columns, dtype):
    return jax.ShapeDtypeStruct((rows, columns), dtype)


def own_product(place, total, across, across_beside, slab):
    rows, width = total.shape
    share = rows // 4

    def kernel(place_ref, total_ref, a_ref, b_ref, slab_ref, send_ref, keep_ref, sum_ref):
        core, quarter = place_ref[0], place_ref[1]
        mine = slab_ref[pl.ds(pl.multiple_of(core * width, width), width), :]
        theirs = slab_ref[pl.ds(pl.multiple_of((1 - core) * width, width), width), :]
        sum_ref[...] = (
            total_ref[...]
            + jnp.dot(a_ref[...], mine, preferred_element_type=F32)
            + jnp.dot(b_ref[...], theirs, preferred_element_type=F32)
        )
        for ref, others in ((send_ref, (3, 1)), (keep_ref, (2, 0))):
            for to, other in enumerate(others):
                start = pl.multiple_of((quarter ^ other) * share, share)
                ref[to * share : (to + 1) * share, :] = sum_ref[pl.ds(start, share), :].astype(BF16)

    return call(
        kernel,
        [like(rows // 2, width, BF16)] * 2,
        (place, total, across, across_beside, slab),
        scratch=(pltpu.VMEM((rows, width), F32),),
        flops=4 * rows * width * width,
    )


def tiles(late, products, panels, blocks, same, flipped, weight):
    tile, depth = products[0][1].shape
    half, share, n = tile // 2, tile // 4, len(products)
    first = min(steps[0] for _, steps in blocks)
    used = [p for p in range(first, len(panels))]
    flat = [a for _, a in products] + [a for p in used for a in panels[p]]
    most = max(len(members) for members, _ in blocks)
    widest = max(len(steps) for _, steps in blocks) + 1
    n_out = 2 * bool(same) + 2 * bool(flipped)

    def kernel(late_ref, *refs):
        product_refs = {key: refs[i] for i, (key, _) in enumerate(products)}
        panel_refs = {p: refs[n + 2 * i : n + 2 * i + 2] for i, p in enumerate(used)}
        out_refs, (stack_ref, held_ref) = refs[len(flat) : len(flat) + n_out], refs[-2:]
        for members, steps in blocks:
            rows = len(members) * half
            for i, key in enumerate(members):
                for part in range(2):
                    stack_ref[part, i * half : (i + 1) * half, :] = product_refs[key][
                        part * half : (part + 1) * half, :
                    ]
            for i, step in enumerate((*steps, steps[-1] + 1)):
                held_ref[:rows, i * tile : (i + 1) * tile] = sum(
                    lax.dot_general(
                        stack_ref[part, :rows, :],
                        panel_refs[step][part][...],
                        TRANSPOSED,
                        preferred_element_type=F32,
                    )
                    for part in range(2)
                )
            for into, (names, kinds) in enumerate(((same, (BF16, F32)), (flipped, (BF16, BF16)))):
                for slot, (key, step) in enumerate(names):
                    if key not in members or not (step in steps or step == WIDE):
                        continue
                    i = members.index(key)
                    column = step - steps[0]
                    if step < WIDE:
                        column = column + late_ref[key]
                    at = pl.ds(pl.multiple_of(column * tile, tile), tile)
                    theirs = held_ref[i * half : i * half + share, at]
                    ours = held_ref[i * half + share : (i + 1) * half, at]
                    pair = (ours, theirs) if into else (theirs, ours)
                    for ref, value, kind in zip(out_refs[2 * into * bool(same) :], pair, kinds):
                        ref[:, slot * tile : (slot + 1) * tile] = value.astype(kind)

    out = []
    if same:
        out += [like(share, len(same) * tile, BF16), like(share, len(same) * tile, F32)]
    if flipped:
        out += [like(share, len(flipped) * tile, BF16)] * 2
    flops = weight * 2 * half * 2 * depth * tile * (len(same) + len(flipped))
    return call(
        kernel,
        out,
        (late, *flat),
        scratch=(
            pltpu.VMEM((2, most * half, depth), BF16),
            pltpu.VMEM((most * half, widest * tile), F32),
        ),
        flops=flops,
    )


def split(same, flipped, groups, tile):
    share = same[0].shape[0]

    def kernel(_, *refs):
        pairs, out_refs = (refs[:2], refs[2:4]), refs[4:]
        for ref, group in zip(out_refs, groups):
            for to, (which, slot) in enumerate(group):
                left, right = pairs[which]
                at = slice(slot * tile, (slot + 1) * tile)
                value = left[:, at].astype(F32) + right[:, at].astype(F32)
                ref[:, to * tile : (to + 1) * tile] = value.astype(ref.dtype)

    return call(
        kernel,
        [
            like(share, len(group) * tile, BF16 if index else F32)
            for index, group in enumerate(groups)
        ],
        (jnp.zeros((1,), jnp.int32), *same, *flipped),
    )


def assemble(place, arrays, plan, band, share, tile):
    def kernel(place_ref, *refs):
        *refs, out_ref = refs
        low, keep_last = place_ref[0], place_ref[1]
        for ref, entries in zip(refs, plan):
            for slot, entry in enumerate(entries):
                value = ref[:, slot * tile : (slot + 1) * tile].astype(F32)
                if entry is None:
                    out_ref[band - 1] = jnp.where(keep_last > 0, value, jnp.zeros_like(value))
                    continue
                flipped, distance, step = entry
                offset = 2 * distance
                if flipped:
                    offset = (offset + 1 - 2 * low) & 7
                out_ref[offset + 8 * step] = value

    return call(kernel, jax.ShapeDtypeStruct((band, share, tile), F32), (place, *arrays))


def per_device(coefficients, jacobi_matrix, jac_limit):
    tile, width = coefficients.shape
    share = tile // 4
    z, x, l, h, c = (lax.axis_index(name) for name in "zxlhc")
    quarter = 2 * h + c
    hold = lax.optimization_barrier

    columns = quarter * width + lax.broadcasted_iota(jnp.int32, (tile, width), 1)
    masked = jnp.where(columns < jac_limit[:, None], coefficients, jnp.zeros_like(coefficients))

    across = shift(masked, "h", 1)
    panels = [masked, shift(masked, "z", 1)]
    beside = shift(masked, "c", 1)

    def rows_of(index):
        return lax.dynamic_slice_in_dim(jacobi_matrix, index * width, width, 0)

    total = jnp.dot(masked, rows_of(quarter), preferred_element_type=F32)
    total = total + jnp.dot(beside, rows_of(quarter ^ 1), preferred_element_type=F32)
    slab = lax.dynamic_slice_in_dim(jacobi_matrix, (1 - h) * 2 * width, 2 * width, 0)
    total, across, slab, panels[1] = hold((total, across, slab, panels[1]))
    across_beside = shift(across, "c", 1)
    place = jnp.stack([c, quarter]).astype(jnp.int32)
    send, keep = own_product(place, total, across, across_beside, slab)
    product = jnp.concatenate([keep, shift(send, "c", 1)])

    def late(dx, flipped):
        return (2 * ((x + dx) % 4) + (l ^ flipped) > 2 * x + l).astype(jnp.int32)

    distances = (0, 1, -1, 2)
    lates = jnp.stack([late(dx, f) for f in (0, 1) for dx in distances])

    def start(products, panels, blocks, same, flipped, weight):
        flipped = [(4 + d, e) for d, e in flipped]
        return tiles(lates, list(products.items()), panels, blocks, same, flipped, weight)

    def finish(same, flipped, names):
        groups = [
            [(f, s) for f in (0, 1) for s, (d, _) in enumerate(names[f]) if d == to]
            for to in range(4)
        ]
        pieces = split(same, flipped, groups, tile)
        arrays, plan = [], []
        for to, (piece, group) in enumerate(zip(pieces, groups)):
            if to:
                piece = shift(piece, "x", -distances[to])
            arrays.append(piece)
            entries = [(f, names[f][s][1]) for f, s in group]
            plan.append([None if e == WIDE else (f, -distances[to] % 4, e) for f, e in entries])
        return arrays, plan

    panels.append(shift(panels[-1], "z", 1))
    flip = shift(product, "l", 1)
    up, down = shift(product, "x", 1), shift(product, "x", -1)

    flip, up, down, panels[2] = hold((flip, up, down, panels[2]))
    panels.append(shift(panels[-1], "z", 1))
    up_flip, down_flip = shift(up, "l", 1), shift(flip, "x", -1)
    far = shift(up, "x", 1)
    both = [(masked, beside)] + [(p, shift(p, "c", 1)) for p in panels[1:3]]

    up_flip, down_flip, far, panels[3] = hold((up_flip, down_flip, far, panels[3]))
    far_flip = shift(down_flip, "x", -1)
    fourth = shift(panels[3], "z", 1)
    both.append((panels[3], shift(panels[3], "c", 1)))
    same_1 = [(d, e) for d in range(4) for e in range(3)]
    products = {0: product, 1: up, 2: down, 3: far}
    other, own = start(products, both, [((0, 1, 2, 3), (0, 1, 2))], same_1, [], 8)

    flipped_1 = [(d, e) for d in range(3) for e in range(3)]
    flip, _ = hold((flip, other))
    other = shift(other, "h", 1)
    products = {4: flip, 5: up_flip, 6: down_flip}
    by_l, by_both = start(products, both, [((4, 5, 6), (0, 1, 2))], [], flipped_1, 8)
    by_l, by_both = shift(by_l, "l", 1), across_and_flip(by_both)

    both.append(hold((fourth, shift(fourth, "c", 1), other))[:2])
    same_2 = [(0, 3), (1, 3), (2, 3), (3, 3), (0, 4)]
    flipped_2 = [(0, 3), (1, 3), (2, 3), (3, 3), (3, 0), (3, 1), (3, 2)]
    products = {0: product, 1: up, 2: down, 3: far, **products, 7: far_flip}
    blocks = [(tuple(range(8)), (3,)), ((7,), (0, 1, 2))]
    other_2, own_2, by_l_2, by_both_2 = start(products, both, blocks, same_2, flipped_2, 8)
    by_l, by_both, other_2, by_l_2, by_both_2 = hold((by_l, by_both, other_2, by_l_2, by_both_2))
    other_2 = shift(other_2, "h", 1)
    by_l_2, by_both_2 = shift(by_l_2, "l", 1), across_and_flip(by_both_2)
    arrays, plan = finish((own, other), (by_l, by_both), (same_1, flipped_1))
    more, more_plan = finish((own_2, other_2), (by_l_2, by_both_2), (same_2, flipped_2))

    where = jnp.stack([l, (z < lax.axis_size("z") // 2)]).astype(jnp.int32)
    band = 8 * WIDE + 1
    out = assemble(where, arrays + more, plan + more_plan, band, share, tile)
    return jnp.transpose(out, (1, 0, 2))


def solution(mesh):
    fine = Mesh(mesh.devices.reshape(8, 4, 2, 2, 2), ("z", "x", "l", "h", "c"))
    blk, jac = ("z", "x", "l"), ("h", "c")
    in_specs = (P(blk, jac), P(None, jac), P(blk))
    out_specs = P(blk + jac, None, None)
    return jax.shard_map(
        per_device, mesh=fine, in_specs=in_specs, out_specs=out_specs, check_vma=False
    )
```

time: 682 us -> 118 us (0.17)
  waiting for transfers between devices: 593 us -> 45.8 us
  matrix products: 40.4 us -> 1.46 us
  Pallas kernels: 0 us -> 16.9 us
  starting transfers between devices: 26.6 us -> 41.4 us
  between operations: 13.4 us -> 0.25 us
    ppermute x32 -> x31, waiting for transfers between devices: 444 us -> 45.8 us  [the longest x29 44.9 us: shift(): lax.ppermute(block, axis, [((i + distance) % n, i) for i in range(n)])]
    reduce_scatter x1 -> x0, waiting for transfers between devices: 117 us -> none  [per_device(): lax.psum_scatter(band_out, 'jac', scatter_dimension=0, tiled=True)]
    dot_general x34 -> x2, matrix products: 40.4 us -> 1.46 us  [the longest x1 0.74 us: per_device(): jnp.dot(beside, rows_of(quarter ^ 1), preferred_element_type=F32)]
    all_gather x1 -> x0, waiting for transfers between devices: 32.7 us -> none  [per_device(): lax.all_gather(masked, 'jac', axis=1, tiled=True)]
    pallas_call x0 -> x7, Pallas kernels: none -> 16.9 us  [call(): pl.pallas_call(kernel, out_shape=out_shape, in_specs=[SMEM] + [VMEM] * (l...]
    ppermute x32 -> x31, starting transfers between devices: 26.6 us -> 41.4 us  [the longest x29 37 us: shift(): lax.ppermute(block, axis, [((i + distance) % n, i) for i in range(n)])]
    unnamed x2 -> x27, local copies, waits for them, and re-layouts: 0.01 us -> 7.15 us
  transfers between devices with their start and end apart: 34 -> 31, of which waited for: 34 -> 17; matrix products, arithmetic and copies ran while one was open for 0% -> 4% of each run, Pallas kernels for 0% -> 11%
where the time goes in v1:
time: 118 us; the launch traced here: 117 us
  waiting for transfers between devices  45.8 us (39%)
  starting transfers between devices  41.4 us (35%)
  Pallas kernels  16.9 us (14%)
  local copies, waits for them, and re-layouts  10.1 us (9%)
  matrix products  1.46 us (1%)
  other arithmetic  1.39 us (1%)
    ppermute x29, waiting for transfers between devices, shift(): lax.ppermute(block, axis, [((i + distance) % n, i) for i in range(n)])  44.9 us
    ppermute x29, starting transfers between devices, shift(): lax.ppermute(block, axis, [((i + distance) % n, i) for i in range(n)])  37 us
    pallas_call x7, Pallas kernels, call(): pl.pallas_call(kernel, out_shape=out_shape, in_specs=[SMEM] + [VMEM] * (l...  16.9 us
    unnamed x27, local copies, waits for them, and re-layouts  7.15 us
    ppermute x2, starting transfers between devices, across_and_flip(): return lax.ppermute(block, ('l', 'h'), [(i, 3 - i) for i in range(4)])  4.34 us
    dynamic_slice x1, local copies, waits for them, and re-layouts, per_device(): lax.dynamic_slice_in_dim(jacobi_matrix, (1 - h) * 2 * width, 2 * width, 0)  2.8 us
  transfers between devices with their start and end apart: 31, of which 17 were waited for; matrix products, arithmetic and copies ran while one was open for 4% of the time, Pallas kernels for 11%

profile of v1, /device:TPU:6, one launch (start us, length us, event | category | flops | bytes accessed | tf_op | source)
XLA Modules:
  0.0 117.3 jit_solution(5547381985825202410)
XLA Ops:
  0.0 1.2 %compare_select_fusion.refs_4_.refs_3_.refs_8_ = bf16[256,1024]{1,0:T(8,128)(2,1)S(1)} fusion(bf16[256,1024]{1,0:T(8,128)(2,1)} %param.3, s32[1024]{0:T(1024)S(1)} %iota_add_fusion, s32[256]{0:T(256)} %param.5), kind=kLoop, calls=%fused_computation.5 | loop fusion | flops 524288 | bytes 1053696 | tf_op jit(solution)/shard_map/jit(_where)/select_n | solution.py:181
  1.2 5.9 %collective-permute-start.2 = (bf16[256,1024]{1,0:T(8,128)(2,1)S(1)}, bf16[256,1024]{1,0:T(8,128)(2,1)S(1)}, u32[]{:S(2)}, u32[]{:S(2)}) collective-permute-start(bf16[256,1024]{1,0:T(8,128)(2,1)S(1)} %compare_select_fusion.refs_4_.refs_3_.refs_8_), channel_id=1, source_target_pairs={{32,0},{64,32},{96,64},{128,96},{160,128},{192,160},{224,192},{0,2... | collective-permute-start | bytes 1572872 | tf_op jit(solution)/shard_map/ppermute | solution.py:17
  7.2 3.2 %collective-permute-start.1 = (bf16[256,1024]{1,0:T(8,128)(2,1)S(1)}, bf16[256,1024]{1,0:T(8,128)(2,1)S(1)}, u32[]{:S(2)}, u32[]{:S(2)}) collective-permute-start(bf16[256,1024]{1,0:T(8,128)(2,1)S(1)} %compare_select_fusion.refs_4_.refs_3_.refs_8_), channel_id=1, source_target_pairs={{2,0},{0,2},{3,1},{1,3},{6,4},{4,6},{7,5},{5,7},{10,8},{8,10},{11,... | collective-permute-start | bytes 1572872 | tf_op jit(solution)/shard_map/ppermute | solution.py:17
  10.4 2.8 %constant_dynamic-slice_fusion.slab_ref = bf16[2048,1024]{1,0:T(8,128)(2,1)S(1)} fusion(bf16[4096,1024]{1,0:T(8,128)(2,1)} %param.4, s32[]{:T(128)S(6)} %select_n.47), kind=kLoop, calls=%fused_computation.9 | loop fusion | bytes 8388612 | tf_op jit(solution)/shard_map/dynamic_slice | solution.py:192
  13.2 1.8 %copy-done.12 = bf16[4096,1024]{1,0:T(8,128)(2,1)S(1)} copy-done((bf16[4096,1024]{1,0:T(8,128)(2,1)S(1)}, bf16[4096,1024]{1,0:T(8,128)(2,1)}, u32[]{:S(2)}) %copy-start.12) | copy-done | bytes 8388632
  15.0 0.7 fusion.2
  15.8 0.7 fusion.4.total_ref
  16.5 1.9 %collective-permute-done.2.refs_6_.refs_5_.refs_10_ = bf16[256,1024]{1,0:T(8,128)(2,1)S(1)} collective-permute-done((bf16[256,1024]{1,0:T(8,128)(2,1)S(1)}, bf16[256,1024]{1,0:T(8,128)(2,1)S(1)}, u32[]{:S(2)}, u32[]{:S(2)}) %collective-permute-start.2) | collective-permute-done | bytes 524320 | tf_op jit(solution)/shard_map/ppermute | solution.py:17
  18.4 3.7 %collective-permute-done.1.a_ref = bf16[256,1024]{1,0:T(8,128)(2,1)S(1)} collective-permute-done((bf16[256,1024]{1,0:T(8,128)(2,1)S(1)}, bf16[256,1024]{1,0:T(8,128)(2,1)S(1)}, u32[]{:S(2)}, u32[]{:S(2)}) %collective-permute-start.1) | collective-permute-done | bytes 524320 | tf_op jit(solution)/shard_map/ppermute | solution.py:17
  22.1 1.8 %collective-permute-done.3.b_ref = bf16[256,1024]{1,0:T(8,128)(2,1)S(1)} collective-permute-done((bf16[256,1024]{1,0:T(8,128)(2,1)S(1)}, bf16[256,1024]{1,0:T(8,128)(2,1)S(1)}, u32[]{:S(2)}, u32[]{:S(2)}) %collective-permute-start.3) | collective-permute-done | bytes 524320 | tf_op jit(solution)/shard_map/ppermute | solution.py:17
  24.0 1.9 %shard_map.37 = (bf16[128,1024]{1,0:T(8,128)(2,1)S(1)}, bf16[128,1024]{1,0:T(8,128)(2,1)S(1)}) custom-call(s32[2]{0:T(128)S(1)} %pad_add_fusion.1.place_ref, f32[256,1024]{1,0:T(8,128)S(1)} %fusion.4.total_ref, bf16[256,1024]{1,0:T(8,128)(2,1)S(1)} %collective-permute-done.1.a_ref, bf16[256,1024]{1,0:T(8,128)(2,1)S(1)} %collective-permute-done.3.b_ref, ...), custom_call_target="tpu_custom_call" | custom-call | flops 1073741824 | bytes 6291464 | tf_op jit(solution)/shard_map/pallas_call | solution.py:26
  26.1 1.0 collective-permute-start.8
  28.0 1.5 %collective-permute-start.6 = (bf16[256,1024]{1,0:T(8,128)(2,1)S(1)}, bf16[256,1024]{1,0:T(8,128)(2,1)S(1)}, u32[]{:S(2)}, u32[]{:S(2)}) collective-permute-start(bf16[256,1024]{1,0:T(8,128)(2,1)S(1)} %constant_dynamic-update-slice_fusion.refs_0_), channel_id=1, source_target_pairs={{8,0},{16,8},{24,16},{0,24},{9,1},{17,9},{25,17},{1,25},{10,2},{18... | collective-permute-start | bytes 1572872 | tf_op jit(solution)/shard_map/ppermute | solution.py:17
  29.6 1.6 %collective-permute-start.5 = (bf16[256,1024]{1,0:T(8,128)(2,1)S(1)}, bf16[256,1024]{1,0:T(8,128)(2,1)S(1)}, u32[]{:S(2)}, u32[]{:S(2)}) collective-permute-start(bf16[256,1024]{1,0:T(8,128)(2,1)S(1)} %constant_dynamic-update-slice_fusion.refs_0_), channel_id=1, source_target_pairs={{4,0},{0,4},{5,1},{1,5},{6,2},{2,6},{7,3},{3,7},{12,8},{8,12},{13,... | collective-permute-start | bytes 1572872 | tf_op jit(solution)/shard_map/ppermute | solution.py:17
  31.2 9.1 %collective-permute-done.8.refs_8_.refs_7_.refs_12_ = bf16[256,1024]{1,0:T(8,128)(2,1)S(1)} collective-permute-done((bf16[256,1024]{1,0:T(8,128)(2,1)S(1)}, bf16[256,1024]{1,0:T(8,128)(2,1)S(1)}, u32[]{:S(2)}, u32[]{:S(2)}) %collective-permute-start.8) | collective-permute-done | bytes 524320 | tf_op jit(solution)/shard_map/ppermute | solution.py:17
  40.3 1.3 %collective-permute-done.7.refs_2_ = bf16[256,1024]{1,0:T(8,128)(2,1)S(1)} collective-permute-done((bf16[256,1024]{1,0:T(8,128)(2,1)S(1)}, bf16[256,1024]{1,0:T(8,128)(2,1)S(1)}, u32[]{:S(2)}, u32[]{:S(2)}) %collective-permute-start.7) | collective-permute-done | bytes 524320 | tf_op jit(solution)/shard_map/ppermute | solution.py:17
  41.5 1.4 %collective-permute-done.6.refs_1_ = bf16[256,1024]{1,0:T(8,128)(2,1)S(1)} collective-permute-done((bf16[256,1024]{1,0:T(8,128)(2,1)S(1)}, bf16[256,1024]{1,0:T(8,128)(2,1)S(1)}, u32[]{:S(2)}, u32[]{:S(2)}) %collective-permute-start.6) | collective-permute-done | bytes 524320 | tf_op jit(solution)/shard_map/ppermute | solution.py:17
  43.0 1.7 %collective-permute-start.10 = (bf16[256,1024]{1,0:T(8,128)(2,1)S(1)}, bf16[256,1024]{1,0:T(8,128)(2,1)S(1)}, u32[]{:S(2)}, u32[]{:S(2)}) collective-permute-start(bf16[256,1024]{1,0:T(8,128)(2,1)S(1)} %collective-permute-done.5.refs_0_.refs_4_), channel_id=1, source_target_pairs={{24,0},{0,8},{8,16},{16,24},{25,1},{1,9},{9,17},{17,25},{26,2},{2,... | collective-permute-start | bytes 1572872 | tf_op jit(solution)/shard_map/ppermute | solution.py:17
  44.7 0.8 copy-done.3
  45.8 1.6 %collective-permute-start.9 = (bf16[256,1024]{1,0:T(8,128)(2,1)S(1)}, bf16[256,1024]{1,0:T(8,128)(2,1)S(1)}, u32[]{:S(2)}, u32[]{:S(2)}) collective-permute-start(bf16[256,1024]{1,0:T(8,128)(2,1)S(1)} %collective-permute-done.6.refs_1_), channel_id=1, source_target_pairs={{4,0},{0,4},{5,1},{1,5},{6,2},{2,6},{7,3},{3,7},{12,8},{8,12},{13,... | collective-permute-start | bytes 1572872 | tf_op jit(solution)/shard_map/ppermute | solution.py:17
  47.4 0.8 copy-done
  48.2 1.0 collective-permute-start.12
  49.2 6.5 %collective-permute-done.10.refs_2_.refs_6_ = bf16[256,1024]{1,0:T(8,128)(2,1)S(1)} collective-permute-done((bf16[256,1024]{1,0:T(8,128)(2,1)S(1)}, bf16[256,1024]{1,0:T(8,128)(2,1)S(1)}, u32[]{:S(2)}, u32[]{:S(2)}) %collective-permute-start.10) | collective-permute-done | bytes 524320 | tf_op jit(solution)/shard_map/ppermute | solution.py:17
  55.8 3.1 %collective-permute-done.11.refs_3_ = bf16[256,1024]{1,0:T(8,128)(2,1)S(1)} collective-permute-done((bf16[256,1024]{1,0:T(8,128)(2,1)S(1)}, bf16[256,1024]{1,0:T(8,128)(2,1)S(1)}, u32[]{:S(2)}, u32[]{:S(2)}) %collective-permute-start.11) | collective-permute-done | bytes 524320 | tf_op jit(solution)/shard_map/ppermute | solution.py:17
  58.9 0.8 copy-done.7
  59.7 0.8 copy-done.10
  60.7 1.9 %collective-permute-start.20 = (bf16[256,1024]{1,0:T(8,128)(2,1)}, bf16[256,1024]{1,0:T(8,128)(2,1)S(1)}, u32[]{:S(2)}, u32[]{:S(2)}) collective-permute-start(bf16[256,1024]{1,0:T(8,128)(2,1)} %collective-permute-done.12.refs_10_.refs_9_.refs_14_), channel_id=1, source_target_pairs={{32,0},{64,32},{96,64},{128,96},{160,128},{192,160},{224,192},{0,2... | collective-permute-start | bytes 1572872 | tf_op jit(solution)/shard_map/ppermute | solution.py:17
  62.6 2.6 %collective-permute-start.19 = (bf16[256,1024]{1,0:T(8,128)(2,1)}, bf16[256,1024]{1,0:T(8,128)(2,1)S(1)}, u32[]{:S(2)}, u32[]{:S(2)}) collective-permute-start(bf16[256,1024]{1,0:T(8,128)(2,1)} %copy-done.5), channel_id=1, source_target_pairs={{24,0},{0,8},{8,16},{16,24},{25,1},{1,9},{9,17},{17,25},{26,2},{2,... | collective-permute-start | bytes 1572872 | tf_op jit(solution)/shard_map/ppermute | solution.py:17
  65.3 1.0 copy-done.1
  66.3 1.0 copy-done.8
  67.4 4.1 %shard_map.38 = (bf16[64,3072]{1,0:T(8,128)(2,1)S(1)}, f32[64,3072]{1,0:T(8,128)S(1)}) custom-call(s32[8]{0:T(128)S(1)} %stack.71.late_ref, bf16[256,1024]{1,0:T(8,128)(2,1)S(1)} %constant_dynamic-update-slice_fusion.refs_0_, bf16[256,1024]{1,0:T(8,128)(2,1)S(1)} %copy-done.1, bf16[256,1024]{1,0:T(8,128)(2,1)S(1)} %collective-permute-done.7.refs_2_, ...), custom_call_target="tpu_custom_call" | custom-call | flops 12884901888 | bytes 6291488 | tf_op jit(solution)/shard_map/pallas_call | solution.py:26
  71.5 3.0 %collective-permute-start.16 = (bf16[64,3072]{1,0:T(8,128)(2,1)S(1)}, bf16[64,3072]{1,0:T(8,128)(2,1)S(1)}, u32[]{:S(2)}, u32[]{:S(2)}) collective-permute-start(bf16[64,3072]{1,0:T(8,128)(2,1)S(1)} %get-tuple-element.56), channel_id=1, source_target_pairs={{2,0},{0,2},{3,1},{1,3},{6,4},{4,6},{7,5},{5,7},{10,8},{8,10},{11,... | collective-permute-start | bytes 1179656 | tf_op jit(solution)/shard_map/ppermute | solution.py:17
  74.5 0.7 collective-permute-done.20.refs_16_
  75.3 3.5 %shard_map.39 = (bf16[64,2304]{1,0:T(8,128)(2,1)S(1)}, bf16[64,2304]{1,0:T(8,128)(2,1)S(1)}) custom-call(s32[8]{0:T(128)S(1)} %stack.71.late_ref, bf16[256,1024]{1,0:T(8,128)(2,1)S(1)} %copy-done.4, bf16[256,1024]{1,0:T(8,128)(2,1)S(1)} %copy-done.11, bf16[256,1024]{1,0:T(8,128)(2,1)S(1)} %copy-done.6, ...), custom_call_target="tpu_custom_call" | custom-call | flops 9663676416 | bytes 5767200 | tf_op jit(solution)/shard_map/pallas_call | solution.py:26
  78.7 1.7 %collective-permute-start.17 = (bf16[64,2304]{1,0:T(8,128)(2,1)S(1)}, bf16[64,2304]{1,0:T(8,128)(2,1)S(1)}, u32[]{:S(2)}, u32[]{:S(2)}) collective-permute-start(bf16[64,2304]{1,0:T(8,128)(2,1)S(1)} %get-tuple-element.60), channel_id=1, source_target_pairs={{4,0},{0,4},{5,1},{1,5},{6,2},{2,6},{7,3},{3,7},{12,8},{8,12},{13,... | collective-permute-start | bytes 884744 | tf_op jit(solution)/shard_map/ppermute | solution.py:17
  80.4 2.2 %collective-permute-start.18 = (bf16[64,2304]{1,0:T(8,128)(2,1)S(1)}, bf16[64,2304]{1,0:T(8,128)(2,1)S(1)}, u32[]{:S(2)}, u32[]{:S(2)}) collective-permute-start(bf16[64,2304]{1,0:T(8,128)(2,1)S(1)} %get-tuple-element.61), channel_id=1, source_target_pairs={{0,6},{2,4},{4,2},{6,0},{1,7},{3,5},{5,3},{7,1},{8,14},{10,12},{12... | collective-permute-start | bytes 884744 | tf_op jit(solution)/shard_map/ppermute | solution.py:21
  82.6 1.5 %collective-permute-done.16.refs_1_ = bf16[64,3072]{1,0:T(8,128)(2,1)S(1)} collective-permute-done((bf16[64,3072]{1,0:T(8,128)(2,1)S(1)}, bf16[64,3072]{1,0:T(8,128)(2,1)S(1)}, u32[]{:S(2)}, u32[]{:S(2)}) %collective-permute-start.16) | collective-permute-done | bytes 393248 | tf_op jit(solution)/shard_map/ppermute | solution.py:17
  84.1 5.3 %shard_map.40 = (bf16[64,1280]{1,0:T(8,128)(2,1)S(1)}, f32[64,1280]{1,0:T(8,128)S(1)}, bf16[64,1792]{1,0:T(8,128)(2,1)S(1)}, bf16[64,1792]{1,0:T(8,128)(2,1)S(1)}) custom-call(s32[8]{0:T(128)S(1)} %stack.71.late_ref, bf16[256,1024]{1,0:T(8,128)(2,1)S(1)} %constant_dynamic-update-slice_fusion.refs_0_, bf16[256,1024]{1,0:T(8,128)(2,1)S(1)} %copy-done.2, ...), custom_call_target="tpu_custom_call" | custom-call | flops 12884901888 | bytes 9437216 | tf_op jit(solution)/shard_map/pallas_call | solution.py:26
  89.9 0.8 collective-permute-done.18.refs_3_
  90.7 1.1 collective-permute-start.26
  91.8 2.2 %collective-permute-start.27 = (bf16[64,1792]{1,0:T(8,128)(2,1)S(1)}, bf16[64,1792]{1,0:T(8,128)(2,1)S(1)}, u32[]{:S(2)}, u32[]{:S(2)}) collective-permute-start(bf16[64,1792]{1,0:T(8,128)(2,1)S(1)} %get-tuple-element.76), channel_id=1, source_target_pairs={{0,6},{2,4},{4,2},{6,0},{1,7},{3,5},{5,3},{7,1},{8,14},{10,12},{12... | collective-permute-start | bytes 688136 | tf_op jit(solution)/shard_map/ppermute | solution.py:21
  94.0 0.9 collective-permute-start.25
  95.2 2.0 %collective-permute-start.22 = (bf16[64,1536]{1,0:T(8,128)(2,1)S(1)}, bf16[64,1536]{1,0:T(8,128)(2,1)S(1)}, u32[]{:S(2)}, u32[]{:S(2)}) collective-permute-start(bf16[64,1536]{1,0:T(8,128)(2,1)S(1)} %get-tuple-element.70), channel_id=1, source_target_pairs={{24,0},{0,8},{8,16},{16,24},{25,1},{1,9},{9,17},{17,25},{26,2},{2,... | collective-permute-start | bytes 589832 | tf_op jit(solution)/shard_map/ppermute | solution.py:17
  97.3 6.2 %collective-permute-done.25.refs_1_ = bf16[64,1280]{1,0:T(8,128)(2,1)S(1)} collective-permute-done((bf16[64,1280]{1,0:T(8,128)(2,1)S(1)}, bf16[64,1280]{1,0:T(8,128)(2,1)S(1)}, u32[]{:S(2)}, u32[]{:S(2)}) %collective-permute-start.25) | collective-permute-done | bytes 163872 | tf_op jit(solution)/shard_map/ppermute | solution.py:17
  103.6 2.9 %collective-permute-start.30 = (bf16[64,1280]{1,0:T(8,128)(2,1)S(1)}, bf16[64,1280]{1,0:T(8,128)(2,1)S(1)}, u32[]{:S(2)}, u32[]{:S(2)}) collective-permute-start(bf16[64,1280]{1,0:T(8,128)(2,1)S(1)} %get-tuple-element.80), channel_id=1, source_target_pairs={{16,0},{24,8},{0,16},{8,24},{17,1},{25,9},{1,17},{9,25},{18,2},{26... | collective-permute-start | bytes 491528 | tf_op jit(solution)/shard_map/ppermute | solution.py:17
  107.0 1.5 %collective-permute-start.29 = (bf16[64,512]{1,0:T(8,128)(2,1)S(1)}, bf16[64,512]{1,0:T(8,128)(2,1)S(1)}, u32[]{:S(2)}, u32[]{:S(2)}) collective-permute-start(bf16[64,512]{1,0:T(8,128)(2,1)S(1)} %get-tuple-element.79), channel_id=1, source_target_pairs={{8,0},{16,8},{24,16},{0,24},{9,1},{17,9},{25,17},{1,25},{10,2},{18... | collective-permute-start | bytes 196616 | tf_op jit(solution)/shard_map/ppermute | solution.py:17
  108.6 6.0 %collective-permute-done.23.refs_2_ = bf16[64,1536]{1,0:T(8,128)(2,1)S(1)} collective-permute-done((bf16[64,1536]{1,0:T(8,128)(2,1)S(1)}, bf16[64,1536]{1,0:T(8,128)(2,1)S(1)}, u32[]{:S(2)}, u32[]{:S(2)}) %collective-permute-start.23) | collective-permute-done | bytes 196640 | tf_op jit(solution)/shard_map/ppermute | solution.py:17
  115.2 2.0 %shard_map.43 = f32[33,64,256]{2,1,0:T(8,128)} custom-call(s32[2]{0:T(128)S(1)} %pad_add_fusion.place_ref, f32[64,1536]{1,0:T(8,128)S(1)} %get-tuple-element.69.refs_0_, bf16[64,1536]{1,0:T(8,128)(2,1)S(1)} %collective-permute-done.22.refs_1_, bf16[64,1536]{1,0:T(8,128)(2,1)S(1)} %collective-permute-done.23.refs_2_, ...), custom_call_target="tpu_custom_call" | custom-call | bytes 1376264 | tf_op jit(solution)/shard_map/pallas_call | solution.py:26
  (58 shorter events, 4.1 us)
Async XLA Ops:
  1.2 17.1 %collective-permute-start.2 = (bf16[256,1024]{1,0:T(8,128)(2,1)S(1)}, bf16[256,1024]{1,0:T(8,128)(2,1)S(1)}, u32[]{:S(2)}, u32[]{:S(2)}) collective-permute-start(bf16[256,1024]{1,0:T(8,128)(2,1)S(1)} %compare_select_fusion.refs_4_.refs_3_.refs_8_), channel_id=1, source_target_pairs={{32,0},{64,32},{96,64},{128,96},{160,128},{192,160},{224,192},{0,2... | collective-permute-start | bytes 1572872 | tf_op jit(solution)/shard_map/ppermute | solution.py:17
  7.2 14.9 %collective-permute-start.1 = (bf16[256,1024]{1,0:T(8,128)(2,1)S(1)}, bf16[256,1024]{1,0:T(8,128)(2,1)S(1)}, u32[]{:S(2)}, u32[]{:S(2)}) collective-permute-start(bf16[256,1024]{1,0:T(8,128)(2,1)S(1)} %compare_select_fusion.refs_4_.refs_3_.refs_8_), channel_id=1, source_target_pairs={{2,0},{0,2},{3,1},{1,3},{6,4},{4,6},{7,5},{5,7},{10,8},{8,10},{11,... | collective-permute-start | bytes 1572872 | tf_op jit(solution)/shard_map/ppermute | solution.py:17
  10.4 5.4 %collective-permute-start = (bf16[256,1024]{1,0:T(8,128)(2,1)S(1)}, bf16[256,1024]{1,0:T(8,128)(2,1)S(1)}, u32[]{:S(2)}, u32[]{:S(2)}) collective-permute-start(bf16[256,1024]{1,0:T(8,128)(2,1)S(1)} %compare_select_fusion.refs_4_.refs_3_.refs_8_), channel_id=1, source_target_pairs={{1,0},{0,1},{3,2},{2,3},{5,4},{4,5},{7,6},{6,7},{9,8},{8,9},{11,10... | collective-permute-start | bytes 1572872 | tf_op jit(solution)/shard_map/ppermute | solution.py:17
  10.4 4.6 %copy-start.12 = (bf16[4096,1024]{1,0:T(8,128)(2,1)S(1)}, bf16[4096,1024]{1,0:T(8,128)(2,1)}, u32[]{:S(2)}) copy-start(bf16[4096,1024]{1,0:T(8,128)(2,1)} %param.4) | copy-start | bytes 25165828
  22.1 1.9 %collective-permute-start.3 = (bf16[256,1024]{1,0:T(8,128)(2,1)S(1)}, bf16[256,1024]{1,0:T(8,128)(2,1)S(1)}, u32[]{:S(2)}, u32[]{:S(2)}) collective-permute-start(bf16[256,1024]{1,0:T(8,128)(2,1)S(1)} %collective-permute-done.1.a_ref), channel_id=1, source_target_pairs={{1,0},{0,1},{3,2},{2,3},{5,4},{4,5},{7,6},{6,7},{9,8},{8,9},{11,10... | collective-permute-start | bytes 1572872 | tf_op jit(solution)/shard_map/ppermute | solution.py:17
  25.8 1.6 %collective-permute-start.4 = (bf16[128,1024]{1,0:T(8,128)(2,1)S(1)}, bf16[128,1024]{1,0:T(8,128)(2,1)S(1)}, u32[]{:S(2)}, u32[]{:S(2)}) collective-permute-start(bf16[128,1024]{1,0:T(8,128)(2,1)S(1)} %get-tuple-element.47), channel_id=1, source_target_pairs={{1,0},{0,1},{3,2},{2,3},{5,4},{4,5},{7,6},{6,7},{9,8},{8,9},{11,10... | collective-permute-start | bytes 786440 | tf_op jit(solution)/shard_map/ppermute | solution.py:17
  26.1 14.2 %collective-permute-start.8 = (bf16[256,1024]{1,0:T(8,128)(2,1)S(1)}, bf16[256,1024]{1,0:T(8,128)(2,1)S(1)}, u32[]{:S(2)}, u32[]{:S(2)}) collective-permute-start(bf16[256,1024]{1,0:T(8,128)(2,1)S(1)} %collective-permute-done.2.refs_6_.refs_5_.refs_10_), channel_id=1, source_target_pairs={{32,0},{64,32},{96,64},{128,96},{160,128},{192,160},{224,192},{0,2... | collective-permute-start | bytes 1572872 | tf_op jit(solution)/shard_map/ppermute | solution.py:17
  27.5 14.0 %collective-permute-start.7 = (bf16[256,1024]{1,0:T(8,128)(2,1)S(1)}, bf16[256,1024]{1,0:T(8,128)(2,1)S(1)}, u32[]{:S(2)}, u32[]{:S(2)}) collective-permute-start(bf16[256,1024]{1,0:T(8,128)(2,1)S(1)} %constant_dynamic-update-slice_fusion.refs_0_), channel_id=1, source_target_pairs={{24,0},{0,8},{8,16},{16,24},{25,1},{1,9},{9,17},{17,25},{26,2},{2,... | collective-permute-start | bytes 1572872 | tf_op jit(solution)/shard_map/ppermute | solution.py:17
  28.0 14.9 %collective-permute-start.6 = (bf16[256,1024]{1,0:T(8,128)(2,1)S(1)}, bf16[256,1024]{1,0:T(8,128)(2,1)S(1)}, u32[]{:S(2)}, u32[]{:S(2)}) collective-permute-start(bf16[256,1024]{1,0:T(8,128)(2,1)S(1)} %constant_dynamic-update-slice_fusion.refs_0_), channel_id=1, source_target_pairs={{8,0},{16,8},{24,16},{0,24},{9,1},{17,9},{25,17},{1,25},{10,2},{18... | collective-permute-start | bytes 1572872 | tf_op jit(solution)/shard_map/ppermute | solution.py:17
  29.6 13.4 %collective-permute-start.5 = (bf16[256,1024]{1,0:T(8,128)(2,1)S(1)}, bf16[256,1024]{1,0:T(8,128)(2,1)S(1)}, u32[]{:S(2)}, u32[]{:S(2)}) collective-permute-start(bf16[256,1024]{1,0:T(8,128)(2,1)S(1)} %constant_dynamic-update-slice_fusion.refs_0_), channel_id=1, source_target_pairs={{4,0},{0,4},{5,1},{1,5},{6,2},{2,6},{7,3},{3,7},{12,8},{8,12},{13,... | collective-permute-start | bytes 1572872 | tf_op jit(solution)/shard_map/ppermute | solution.py:17
  43.0 12.8 %collective-permute-start.10 = (bf16[256,1024]{1,0:T(8,128)(2,1)S(1)}, bf16[256,1024]{1,0:T(8,128)(2,1)S(1)}, u32[]{:S(2)}, u32[]{:S(2)}) collective-permute-start(bf16[256,1024]{1,0:T(8,128)(2,1)S(1)} %collective-permute-done.5.refs_0_.refs_4_), channel_id=1, source_target_pairs={{24,0},{0,8},{8,16},{16,24},{25,1},{1,9},{9,17},{17,25},{26,2},{2,... | collective-permute-start | bytes 1572872 | tf_op jit(solution)/shard_map/ppermute | solution.py:17
  44.7 0.8 copy-start.3
  45.5 13.4 %collective-permute-start.11 = (bf16[256,1024]{1,0:T(8,128)(2,1)S(1)}, bf16[256,1024]{1,0:T(8,128)(2,1)S(1)}, u32[]{:S(2)}, u32[]{:S(2)}) collective-permute-start(bf16[256,1024]{1,0:T(8,128)(2,1)S(1)} %collective-permute-done.6.refs_1_), channel_id=1, source_target_pairs={{8,0},{16,8},{24,16},{0,24},{9,1},{17,9},{25,17},{1,25},{10,2},{18... | collective-permute-start | bytes 1572872 | tf_op jit(solution)/shard_map/ppermute | solution.py:17
  45.8 13.9 %collective-permute-start.9 = (bf16[256,1024]{1,0:T(8,128)(2,1)S(1)}, bf16[256,1024]{1,0:T(8,128)(2,1)S(1)}, u32[]{:S(2)}, u32[]{:S(2)}) collective-permute-start(bf16[256,1024]{1,0:T(8,128)(2,1)S(1)} %collective-permute-done.6.refs_1_), channel_id=1, source_target_pairs={{4,0},{0,4},{5,1},{1,5},{6,2},{2,6},{7,3},{3,7},{12,8},{8,12},{13,... | collective-permute-start | bytes 1572872 | tf_op jit(solution)/shard_map/ppermute | solution.py:17
  47.4 0.8 copy-start
  48.2 12.3 %collective-permute-start.12 = (bf16[256,1024]{1,0:T(8,128)(2,1)S(1)}, bf16[256,1024]{1,0:T(8,128)(2,1)}, u32[]{:S(2)}, u32[]{:S(2)}) collective-permute-start(bf16[256,1024]{1,0:T(8,128)(2,1)S(1)} %collective-permute-done.8.refs_8_.refs_7_.refs_12_), channel_id=1, source_target_pairs={{32,0},{64,32},{96,64},{128,96},{160,128},{192,160},{224,192},{0,2... | collective-permute-start | bytes 1572872 | tf_op jit(solution)/shard_map/ppermute | solution.py:17
  49.2 16.1 %collective-permute-start.13 = (bf16[256,1024]{1,0:T(8,128)(2,1)S(1)}, bf16[256,1024]{1,0:T(8,128)(2,1)}, u32[]{:S(2)}, u32[]{:S(2)}) collective-permute-start(bf16[256,1024]{1,0:T(8,128)(2,1)S(1)} %collective-permute-done.2.refs_6_.refs_5_.refs_10_), channel_id=1, source_target_pairs={{1,0},{0,1},{3,2},{2,3},{5,4},{4,5},{7,6},{6,7},{9,8},{8,9},{11,10... | collective-permute-start | bytes 1572872 | tf_op jit(solution)/shard_map/ppermute | solution.py:17
  55.8 4.8 %copy-start.5 = (bf16[256,1024]{1,0:T(8,128)(2,1)}, bf16[256,1024]{1,0:T(8,128)(2,1)S(1)}, u32[]{:S(2)}) copy-start(bf16[256,1024]{1,0:T(8,128)(2,1)S(1)} %collective-permute-done.10.refs_2_.refs_6_) | copy-start | bytes 1572868
  55.8 9.5 %collective-permute-start.14 = (bf16[256,1024]{1,0:T(8,128)(2,1)S(1)}, bf16[256,1024]{1,0:T(8,128)(2,1)}, u32[]{:S(2)}, u32[]{:S(2)}) collective-permute-start(bf16[256,1024]{1,0:T(8,128)(2,1)S(1)} %collective-permute-done.8.refs_8_.refs_7_.refs_12_), channel_id=1, source_target_pairs={{1,0},{0,1},{3,2},{2,3},{5,4},{4,5},{7,6},{6,7},{9,8},{8,9},{11,10... | collective-permute-start | bytes 1572872 | tf_op jit(solution)/shard_map/ppermute | solution.py:17
  58.9 0.8 copy-start.7
  59.7 0.8 copy-start.10
  60.5 4.7 %collective-permute-start.15 = (bf16[256,1024]{1,0:T(8,128)(2,1)}, bf16[256,1024]{1,0:T(8,128)(2,1)}, u32[]{:S(2)}, u32[]{:S(2)}) collective-permute-start(bf16[256,1024]{1,0:T(8,128)(2,1)} %collective-permute-done.12.refs_10_.refs_9_.refs_14_), channel_id=1, source_target_pairs={{1,0},{0,1},{3,2},{2,3},{5,4},{4,5},{7,6},{6,7},{9,8},{8,9},{11,10... | collective-permute-start | bytes 1572872 | tf_op jit(solution)/shard_map/ppermute | solution.py:17
  60.7 14.6 %collective-permute-start.20 = (bf16[256,1024]{1,0:T(8,128)(2,1)}, bf16[256,1024]{1,0:T(8,128)(2,1)S(1)}, u32[]{:S(2)}, u32[]{:S(2)}) collective-permute-start(bf16[256,1024]{1,0:T(8,128)(2,1)} %collective-permute-done.12.refs_10_.refs_9_.refs_14_), channel_id=1, source_target_pairs={{32,0},{64,32},{96,64},{128,96},{160,128},{192,160},{224,192},{0,2... | collective-permute-start | bytes 1572872 | tf_op jit(solution)/shard_map/ppermute | solution.py:17
  62.6 21.5 %collective-permute-start.19 = (bf16[256,1024]{1,0:T(8,128)(2,1)}, bf16[256,1024]{1,0:T(8,128)(2,1)S(1)}, u32[]{:S(2)}, u32[]{:S(2)}) collective-permute-start(bf16[256,1024]{1,0:T(8,128)(2,1)} %copy-done.5), channel_id=1, source_target_pairs={{24,0},{0,8},{8,16},{16,24},{25,1},{1,9},{9,17},{17,25},{26,2},{2,... | collective-permute-start | bytes 1572872 | tf_op jit(solution)/shard_map/ppermute | solution.py:17
  65.3 1.0 copy-start.1
  66.3 1.0 copy-start.8
  67.4 7.9 %copy-start.4 = (bf16[256,1024]{1,0:T(8,128)(2,1)S(1)}, bf16[256,1024]{1,0:T(8,128)(2,1)}, u32[]{:S(2)}) copy-start(bf16[256,1024]{1,0:T(8,128)(2,1)} %copy-done.3) | copy-start | bytes 1572868
  67.4 7.9 %copy-start.6 = (bf16[256,1024]{1,0:T(8,128)(2,1)S(1)}, bf16[256,1024]{1,0:T(8,128)(2,1)}, u32[]{:S(2)}) copy-start(bf16[256,1024]{1,0:T(8,128)(2,1)} %copy-done.5) | copy-start | bytes 1572868
  67.4 7.9 %copy-start.11 = (bf16[256,1024]{1,0:T(8,128)(2,1)S(1)}, bf16[256,1024]{1,0:T(8,128)(2,1)}, u32[]{:S(2)}) copy-start(bf16[256,1024]{1,0:T(8,128)(2,1)} %copy-done.10) | copy-start | bytes 1572868
  71.5 12.6 %copy-start.2 = (bf16[256,1024]{1,0:T(8,128)(2,1)S(1)}, bf16[256,1024]{1,0:T(8,128)(2,1)}, u32[]{:S(2)}) copy-start(bf16[256,1024]{1,0:T(8,128)(2,1)} %copy-done) | copy-start | bytes 1572868
  71.5 12.6 %copy-start.9 = (bf16[256,1024]{1,0:T(8,128)(2,1)S(1)}, bf16[256,1024]{1,0:T(8,128)(2,1)}, u32[]{:S(2)}) copy-start(bf16[256,1024]{1,0:T(8,128)(2,1)} %copy-done.7) | copy-start | bytes 1572868
  71.5 12.6 %collective-permute-start.16 = (bf16[64,3072]{1,0:T(8,128)(2,1)S(1)}, bf16[64,3072]{1,0:T(8,128)(2,1)S(1)}, u32[]{:S(2)}, u32[]{:S(2)}) collective-permute-start(bf16[64,3072]{1,0:T(8,128)(2,1)S(1)} %get-tuple-element.56), channel_id=1, source_target_pairs={{2,0},{0,2},{3,1},{1,3},{6,4},{4,6},{7,5},{5,7},{10,8},{8,10},{11,... | collective-permute-start | bytes 1179656 | tf_op jit(solution)/shard_map/ppermute | solution.py:17
  75.3 8.8 %collective-permute-start.21 = (bf16[256,1024]{1,0:T(8,128)(2,1)S(1)}, bf16[256,1024]{1,0:T(8,128)(2,1)S(1)}, u32[]{:S(2)}, u32[]{:S(2)}) collective-permute-start(bf16[256,1024]{1,0:T(8,128)(2,1)S(1)} %collective-permute-done.20.refs_16_), channel_id=1, source_target_pairs={{1,0},{0,1},{3,2},{2,3},{5,4},{4,5},{7,6},{6,7},{9,8},{8,9},{11,10... | collective-permute-start | bytes 1572872 | tf_op jit(solution)/shard_map/ppermute | solution.py:17
  78.7 11.2 %collective-permute-start.17 = (bf16[64,2304]{1,0:T(8,128)(2,1)S(1)}, bf16[64,2304]{1,0:T(8,128)(2,1)S(1)}, u32[]{:S(2)}, u32[]{:S(2)}) collective-permute-start(bf16[64,2304]{1,0:T(8,128)(2,1)S(1)} %get-tuple-element.60), channel_id=1, source_target_pairs={{4,0},{0,4},{5,1},{1,5},{6,2},{2,6},{7,3},{3,7},{12,8},{8,12},{13,... | collective-permute-start | bytes 884744 | tf_op jit(solution)/shard_map/ppermute | solution.py:17
  80.4 10.3 %collective-permute-start.18 = (bf16[64,2304]{1,0:T(8,128)(2,1)S(1)}, bf16[64,2304]{1,0:T(8,128)(2,1)S(1)}, u32[]{:S(2)}, u32[]{:S(2)}) collective-permute-start(bf16[64,2304]{1,0:T(8,128)(2,1)S(1)} %get-tuple-element.61), channel_id=1, source_target_pairs={{0,6},{2,4},{4,2},{6,0},{1,7},{3,5},{5,3},{7,1},{8,14},{10,12},{12... | collective-permute-start | bytes 884744 | tf_op jit(solution)/shard_map/ppermute | solution.py:21
  90.7 12.7 %collective-permute-start.26 = (bf16[64,1792]{1,0:T(8,128)(2,1)S(1)}, bf16[64,1792]{1,0:T(8,128)(2,1)S(1)}, u32[]{:S(2)}, u32[]{:S(2)}) collective-permute-start(bf16[64,1792]{1,0:T(8,128)(2,1)S(1)} %get-tuple-element.75), channel_id=1, source_target_pairs={{4,0},{0,4},{5,1},{1,5},{6,2},{2,6},{7,3},{3,7},{12,8},{8,12},{13,... | collective-permute-start | bytes 688136 | tf_op jit(solution)/shard_map/ppermute | solution.py:17
  91.8 11.7 %collective-permute-start.27 = (bf16[64,1792]{1,0:T(8,128)(2,1)S(1)}, bf16[64,1792]{1,0:T(8,128)(2,1)S(1)}, u32[]{:S(2)}, u32[]{:S(2)}) collective-permute-start(bf16[64,1792]{1,0:T(8,128)(2,1)S(1)} %get-tuple-element.76), channel_id=1, source_target_pairs={{0,6},{2,4},{4,2},{6,0},{1,7},{3,5},{5,3},{7,1},{8,14},{10,12},{12... | collective-permute-start | bytes 688136 | tf_op jit(solution)/shard_map/ppermute | solution.py:21
  94.0 9.5 %collective-permute-start.25 = (bf16[64,1280]{1,0:T(8,128)(2,1)S(1)}, bf16[64,1280]{1,0:T(8,128)(2,1)S(1)}, u32[]{:S(2)}, u32[]{:S(2)}) collective-permute-start(bf16[64,1280]{1,0:T(8,128)(2,1)S(1)} %get-tuple-element.74), channel_id=1, source_target_pairs={{2,0},{0,2},{3,1},{1,3},{6,4},{4,6},{7,5},{5,7},{10,8},{8,10},{11,... | collective-permute-start | bytes 491528 | tf_op jit(solution)/shard_map/ppermute | solution.py:17
  95.0 12.0 %collective-permute-start.24 = (bf16[64,768]{1,0:T(8,128)(2,1)S(1)}, bf16[64,768]{1,0:T(8,128)(2,1)S(1)}, u32[]{:S(2)}, u32[]{:S(2)}) collective-permute-start(bf16[64,768]{1,0:T(8,128)(2,1)S(1)} %get-tuple-element.72), channel_id=1, source_target_pairs={{16,0},{24,8},{0,16},{8,24},{17,1},{25,9},{1,17},{9,25},{18,2},{26... | collective-permute-start | bytes 294920 | tf_op jit(solution)/shard_map/ppermute | solution.py:17
  95.2 13.3 %collective-permute-start.22 = (bf16[64,1536]{1,0:T(8,128)(2,1)S(1)}, bf16[64,1536]{1,0:T(8,128)(2,1)S(1)}, u32[]{:S(2)}, u32[]{:S(2)}) collective-permute-start(bf16[64,1536]{1,0:T(8,128)(2,1)S(1)} %get-tuple-element.70), channel_id=1, source_target_pairs={{24,0},{0,8},{8,16},{16,24},{25,1},{1,9},{9,17},{17,25},{26,2},{2,... | collective-permute-start | bytes 589832 | tf_op jit(solution)/shard_map/ppermute | solution.py:17
  103.5 11.1 %collective-permute-start.23 = (bf16[64,1536]{1,0:T(8,128)(2,1)S(1)}, bf16[64,1536]{1,0:T(8,128)(2,1)S(1)}, u32[]{:S(2)}, u32[]{:S(2)}) collective-permute-start(bf16[64,1536]{1,0:T(8,128)(2,1)S(1)} %get-tuple-element.71), channel_id=1, source_target_pairs={{8,0},{16,8},{24,16},{0,24},{9,1},{17,9},{25,17},{1,25},{10,2},{18... | collective-permute-start | bytes 589832 | tf_op jit(solution)/shard_map/ppermute | solution.py:17
  103.6 11.7 %collective-permute-start.30 = (bf16[64,1280]{1,0:T(8,128)(2,1)S(1)}, bf16[64,1280]{1,0:T(8,128)(2,1)S(1)}, u32[]{:S(2)}, u32[]{:S(2)}) collective-permute-start(bf16[64,1280]{1,0:T(8,128)(2,1)S(1)} %get-tuple-element.80), channel_id=1, source_target_pairs={{16,0},{24,8},{0,16},{8,24},{17,1},{25,9},{1,17},{9,25},{18,2},{26... | collective-permute-start | bytes 491528 | tf_op jit(solution)/shard_map/ppermute | solution.py:17
  106.5 8.1 %collective-permute-start.28 = (bf16[64,512]{1,0:T(8,128)(2,1)S(1)}, bf16[64,512]{1,0:T(8,128)(2,1)S(1)}, u32[]{:S(2)}, u32[]{:S(2)}) collective-permute-start(bf16[64,512]{1,0:T(8,128)(2,1)S(1)} %get-tuple-element.78), channel_id=1, source_target_pairs={{24,0},{0,8},{8,16},{16,24},{25,1},{1,9},{9,17},{17,25},{26,2},{2,... | collective-permute-start | bytes 196616 | tf_op jit(solution)/shard_map/ppermute | solution.py:17
  107.0 8.3 %collective-permute-start.29 = (bf16[64,512]{1,0:T(8,128)(2,1)S(1)}, bf16[64,512]{1,0:T(8,128)(2,1)S(1)}, u32[]{:S(2)}, u32[]{:S(2)}) collective-permute-start(bf16[64,512]{1,0:T(8,128)(2,1)S(1)} %get-tuple-element.79), channel_id=1, source_target_pairs={{8,0},{16,8},{24,16},{0,24},{9,1},{17,9},{25,17},{1,25},{10,2},{18... | collective-permute-start | bytes 196616 | tf_op jit(solution)/shard_map/ppermute | solution.py:17

commit v2 on v1

--- a/solution.py
+++ b/solution.py
@@ -70,14 +70,18 @@
     half, share, n = tile // 2, tile // 4, len(products)
     first = min(steps[0] for _, steps in blocks)
     used = [p for p in range(first, len(panels))]
-    flat = [a for _, a in products] + [a for p in used for a in panels[p]]
+    parts = [p if isinstance(p, tuple) else (p,) for at in used for p in panels[at]]
+    flat = [a for _, a in products] + [a for p in parts for a in p]
     most = max(len(members) for members, _ in blocks)
     widest = max(len(steps) for _, steps in blocks) + 1
     n_out = 2 * bool(same) + 2 * bool(flipped)
 
     def kernel(late_ref, *refs):
         product_refs = {key: refs[i] for i, (key, _) in enumerate(products)}
-        panel_refs = {p: refs[n + 2 * i : n + 2 * i + 2] for i, p in enumerate(used)}
+        rest, panel_refs = list(refs[n : len(flat)]), []
+        for part in parts:
+            panel_refs.append(rest[: len(part)])
+            rest = rest[len(part) :]
         out_refs, (stack_ref, held_ref) = refs[len(flat) : len(flat) + n_out], refs[-2:]
         for members, steps in blocks:
             rows = len(members) * half
@@ -87,14 +91,17 @@
                         part * half : (part + 1) * half, :
                     ]
             for i, step in enumerate((*steps, steps[-1] + 1)):
+                halves = [panel_refs[2 * (step - first) + part] for part in range(2)]
                 held_ref[:rows, i * tile : (i + 1) * tile] = sum(
                     lax.dot_general(
                         stack_ref[part, :rows, :],
-                        panel_refs[step][part][...],
+                        half_refs[0][...]
+                        if len(half_refs) == 1
+                        else jnp.concatenate([ref[...] for ref in half_refs]),
                         TRANSPOSED,
                         preferred_element_type=F32,
                     )
-                    for part in range(2)
+                    for part, half_refs in enumerate(halves)
                 )
             for into, (names, kinds) in enumerate(((same, (BF16, F32)), (flipped, (BF16, BF16)))):
                 for slot, (key, step) in enumerate(names):
@@ -129,14 +136,14 @@
     )
 
 
-def split(same, flipped, groups, tile):
-    share = same[0].shape[0]
+def split(sums, groups, tile):
+    share = sums[0][0].shape[0]
+    flat = [a for pair in sums for a in pair]
 
     def kernel(_, *refs):
-        pairs, out_refs = (refs[:2], refs[2:4]), refs[4:]
-        for ref, group in zip(out_refs, groups):
+        for ref, group in zip(refs[len(flat) :], groups):
             for to, (which, slot) in enumerate(group):
-                left, right = pairs[which]
+                left, right = refs[2 * which : 2 * which + 2]
                 at = slice(slot * tile, (slot + 1) * tile)
                 value = left[:, at].astype(F32) + right[:, at].astype(F32)
                 ref[:, to * tile : (to + 1) * tile] = value.astype(ref.dtype)
@@ -147,27 +154,61 @@
             like(share, len(group) * tile, BF16 if index else F32)
             for index, group in enumerate(groups)
         ],
-        (jnp.zeros((1,), jnp.int32), *same, *flipped),
-    )
-
-
-def assemble(place, arrays, plan, band, share, tile):
-    def kernel(place_ref, *refs):
-        *refs, out_ref = refs
+        (jnp.zeros((1,), jnp.int32), *flat),
+    )
+
+
+def assemble(place, arrays, plan, band, share, tile, base=None):
+    count = sum(len(entries) for entries in plan)
+
+    def tiles_of(place_ref, refs):
         low, keep_last = place_ref[0], place_ref[1]
         for ref, entries in zip(refs, plan):
             for slot, entry in enumerate(entries):
                 value = ref[:, slot * tile : (slot + 1) * tile].astype(F32)
                 if entry is None:
-                    out_ref[band - 1] = jnp.where(keep_last > 0, value, jnp.zeros_like(value))
+                    yield band - 1, jnp.where(keep_last > 0, value, jnp.zeros_like(value))
                     continue
                 flipped, distance, step = entry
                 offset = 2 * distance
                 if flipped:
                     offset = (offset + 1 - 2 * low) & 7
-                out_ref[offset + 8 * step] = value
-
-    return call(kernel, jax.ShapeDtypeStruct((band, share, tile), F32), (place, *arrays))
+                yield offset + 8 * step, value
+
+    out = jax.ShapeDtypeStruct((band, share, tile), F32)
+    if base is None:
+
+        def first_kernel(place_ref, *refs):
+            for offset, value in tiles_of(place_ref, refs[:-1]):
+                refs[-1][offset] = value
+
+        return call(first_kernel, out, (place, *arrays))
+
+    def kernel(place_ref, *refs):
+        out_ref, stage_ref, sems = refs[-3:]
+        copies = []
+        for index, (offset, value) in enumerate(tiles_of(place_ref, refs[:-4])):
+            stage_ref[index] = value
+            copies.append(
+                pltpu.make_async_copy(stage_ref.at[index], out_ref.at[offset], sems.at[index])
+            )
+            copies[-1].start()
+        for copy in copies:
+            copy.wait()
+
+    anywhere = pl.BlockSpec(memory_space=pl.ANY)
+    return pl.pallas_call(
+        kernel,
+        out_shape=out,
+        in_specs=[SMEM] + [VMEM] * len(arrays) + [anywhere],
+        out_specs=anywhere,
+        input_output_aliases={len(arrays) + 1: 0},
+        scratch_shapes=[
+            pltpu.VMEM((count, share, tile), F32),
+            pltpu.SemaphoreType.DMA((count,)),
+        ],
+        compiler_params=pltpu.CompilerParams(vmem_limit_bytes=16 * 2**20),
+    )(place, *arrays, base)
 
 
 def per_device(coefficients, jacobi_matrix, jac_limit):
@@ -206,18 +247,18 @@
         flipped = [(4 + d, e) for d, e in flipped]
         return tiles(lates, list(products.items()), panels, blocks, same, flipped, weight)
 
-    def finish(same, flipped, names):
+    def finish(sums, names, targets):
         groups = [
-            [(f, s) for f in (0, 1) for s, (d, _) in enumerate(names[f]) if d == to]
-            for to in range(4)
+            [(n, s) for n, (_, name) in enumerate(names) for s, (d, _) in enumerate(name) if d == to]
+            for to in targets
         ]
-        pieces = split(same, flipped, groups, tile)
+        pieces = split(sums, groups, tile)
         arrays, plan = [], []
-        for to, (piece, group) in enumerate(zip(pieces, groups)):
+        for to, piece, group in zip(targets, pieces, groups):
             if to:
                 piece = shift(piece, "x", -distances[to])
             arrays.append(piece)
-            entries = [(f, names[f][s][1]) for f, s in group]
+            entries = [(names[n][0], names[n][1][s][1]) for n, s in group]
             plan.append([None if e == WIDE else (f, -distances[to] % 4, e) for f, e in entries])
         return arrays, plan
 
@@ -231,7 +272,7 @@
     far = shift(up, "x", 1)
     both = [(masked, beside)] + [(p, shift(p, "c", 1)) for p in panels[1:3]]
 
-    up_flip, down_flip, far, panels[3] = hold((up_flip, down_flip, far, panels[3]))
+    up_flip, down_flip, far = hold((up_flip, down_flip, far))
     far_flip = shift(down_flip, "x", -1)
     fourth = shift(panels[3], "z", 1)
     both.append((panels[3], shift(panels[3], "c", 1)))
@@ -246,21 +287,29 @@
     by_l, by_both = start(products, both, [((4, 5, 6), (0, 1, 2))], [], flipped_1, 8)
     by_l, by_both = shift(by_l, "l", 1), across_and_flip(by_both)
 
-    both.append(hold((fourth, shift(fourth, "c", 1), other))[:2])
+    both.append((fourth, tuple(shift(rows, "c", 1) for rows in jnp.split(fourth, 2))))
     same_2 = [(0, 3), (1, 3), (2, 3), (3, 3), (0, 4)]
     flipped_2 = [(0, 3), (1, 3), (2, 3), (3, 3), (3, 0), (3, 1), (3, 2)]
     products = {0: product, 1: up, 2: down, 3: far, **products, 7: far_flip}
     blocks = [(tuple(range(8)), (3,)), ((7,), (0, 1, 2))]
-    other_2, own_2, by_l_2, by_both_2 = start(products, both, blocks, same_2, flipped_2, 8)
-    by_l, by_both, other_2, by_l_2, by_both_2 = hold((by_l, by_both, other_2, by_l_2, by_both_2))
+    other_2, own_2, by_l_2, by_both_2 = start(products, both, blocks, same_2, flipped_2, 0)
+    other, by_l, by_both, other_2, by_l_2, by_both_2 = hold(
+        (other, by_l, by_both, other_2, by_l_2, by_both_2)
+    )
     other_2 = shift(other_2, "h", 1)
     by_l_2, by_both_2 = shift(by_l_2, "l", 1), across_and_flip(by_both_2)
-    arrays, plan = finish((own, other), (by_l, by_both), (same_1, flipped_1))
-    more, more_plan = finish((own_2, other_2), (by_l_2, by_both_2), (same_2, flipped_2))
+    sums, names = [(own, other), (by_l, by_both)], [(0, same_1), (1, flipped_1)]
+    arrays, plan = finish(sums, names, (0, 1, 2))
+    other_2, by_l_2, by_both_2, *arrays = hold((other_2, by_l_2, by_both_2, *arrays))
+    sums += [(own_2, other_2), (by_l_2, by_both_2)]
+    names = [(f, [(d if d == 3 else -1, e) for d, e in name]) for f, name in names]
+    names += [(0, same_2), (1, flipped_2)]
+    more, more_plan = finish(sums, names, (0, 1, 2, 3))
 
     where = jnp.stack([l, (z < lax.axis_size("z") // 2)]).astype(jnp.int32)
     band = 8 * WIDE + 1
-    out = assemble(where, arrays + more, plan + more_plan, band, share, tile)
+    out = assemble(where, arrays, plan, band, share, tile)
+    out = assemble(where, more, more_plan, band, share, tile, out)
     return jnp.transpose(out, (1, 0, 2))
 
 

time: 118 us -> 111 us (0.941)
  local copies, waits for them, and re-layouts: 10.1 us -> 5.61 us
  starting transfers between devices: 41.4 us -> 37.9 us
  waiting for transfers between devices: 45.8 us -> 43.2 us
  Pallas kernels: 16.9 us -> 19.3 us
    unnamed x27 -> x11, local copies, waits for them, and re-layouts: 7.15 us -> 2.66 us
    ppermute x29, waiting for transfers between devices: 44.9 us -> 43.1 us  [shift(): lax.ppermute(block, axis, [((i + distance) % n, i) for i in range(n)])]
    ppermute x2, starting transfers between devices: 4.34 us -> 2.54 us  [across_and_flip(): return lax.ppermute(block, ('l', 'h'), [(i, 3 - i) for i in range(4)])]
    ppermute x29, starting transfers between devices: 37 us -> 35.4 us  [shift(): lax.ppermute(block, axis, [((i + distance) % n, i) for i in range(n)])]
    pallas_call x0 -> x1, Pallas kernels: none -> 1.6 us  [assemble(): pl.pallas_call(kernel, out_shape=out, in_specs=[SMEM] + [VMEM] * len(arra...]
  transfers between devices with their start and end apart: 31 -> 31, of which waited for: 17 -> 17; matrix products, arithmetic and copies ran while one was open for 4% -> 4% of each run, Pallas kernels for 11% -> 14%
where the time goes in v2:
time: 111 us; the launch traced here: 109 us
  waiting for transfers between devices  43.2 us (39%)
  starting transfers between devices  37.9 us (34%)
  Pallas kernels  19.3 us (17%)
  local copies, waits for them, and re-layouts  5.61 us (5%)
  matrix products  1.46 us (1%)
  other arithmetic  1.39 us (1%)
    ppermute x29, waiting for transfers between devices, shift(): lax.ppermute(block, axis, [((i + distance) % n, i) for i in range(n)])  43.1 us
    ppermute x29, starting transfers between devices, shift(): lax.ppermute(block, axis, [((i + distance) % n, i) for i in range(n)])  35.4 us
    pallas_call x7, Pallas kernels, call(): pl.pallas_call(kernel, out_shape=out_shape, in_specs=[SMEM] + [VMEM] * (l...  17.7 us
    dynamic_slice x1, local copies, waits for them, and re-layouts, per_device(): lax.dynamic_slice_in_dim(jacobi_matrix, (1 - h) * 2 * width, 2 * width, 0)  2.8 us
    unnamed x11, local copies, waits for them, and re-layouts  2.66 us
    ppermute x2, starting transfers between devices, across_and_flip(): return lax.ppermute(block, ('l', 'h'), [(i, 3 - i) for i in range(4)])  2.54 us
  transfers between devices with their start and end apart: 31, of which 17 were waited for; matrix products, arithmetic and copies ran while one was open for 4% of the time, Pallas kernels for 14%

profile of v2, /device:TPU:6, one launch (start us, length us, event | category | flops | bytes accessed | tf_op | source)
XLA Modules:
  0.0 109.2 jit_solution(2035076603123612003)
XLA Ops:
  0.0 1.2 %compare_select_fusion.refs_4_.refs_3_.refs_8_ = bf16[256,1024]{1,0:T(8,128)(2,1)S(1)} fusion(bf16[256,1024]{1,0:T(8,128)(2,1)} %param.3, s32[1024]{0:T(1024)S(1)} %iota_add_fusion, s32[256]{0:T(256)} %param.5), kind=kLoop, calls=%fused_computation.5 | loop fusion | flops 524288 | bytes 1053696 | tf_op jit(solution)/shard_map/jit(_where)/select_n | solution.py:222
  1.2 5.9 %collective-permute-start.2 = (bf16[256,1024]{1,0:T(8,128)(2,1)S(1)}, bf16[256,1024]{1,0:T(8,128)(2,1)S(1)}, u32[]{:S(2)}, u32[]{:S(2)}) collective-permute-start(bf16[256,1024]{1,0:T(8,128)(2,1)S(1)} %compare_select_fusion.refs_4_.refs_3_.refs_8_), channel_id=1, source_target_pairs={{32,0},{64,32},{96,64},{128,96},{160,128},{192,160},{224,192},{0,2... | collective-permute-start | bytes 1572872 | tf_op jit(solution)/shard_map/ppermute | solution.py:17
  7.2 3.2 %collective-permute-start.1 = (bf16[256,1024]{1,0:T(8,128)(2,1)S(1)}, bf16[256,1024]{1,0:T(8,128)(2,1)S(1)}, u32[]{:S(2)}, u32[]{:S(2)}) collective-permute-start(bf16[256,1024]{1,0:T(8,128)(2,1)S(1)} %compare_select_fusion.refs_4_.refs_3_.refs_8_), channel_id=1, source_target_pairs={{2,0},{0,2},{3,1},{1,3},{6,4},{4,6},{7,5},{5,7},{10,8},{8,10},{11,... | collective-permute-start | bytes 1572872 | tf_op jit(solution)/shard_map/ppermute | solution.py:17
  10.4 2.8 %constant_dynamic-slice_fusion.slab_ref = bf16[2048,1024]{1,0:T(8,128)(2,1)S(1)} fusion(bf16[4096,1024]{1,0:T(8,128)(2,1)} %param.4, s32[]{:T(128)S(6)} %select_n.47), kind=kLoop, calls=%fused_computation.9 | loop fusion | bytes 8388612 | tf_op jit(solution)/shard_map/dynamic_slice | solution.py:233
  13.2 1.8 %copy-done.4 = bf16[4096,1024]{1,0:T(8,128)(2,1)S(1)} copy-done((bf16[4096,1024]{1,0:T(8,128)(2,1)S(1)}, bf16[4096,1024]{1,0:T(8,128)(2,1)}, u32[]{:S(2)}) %copy-start.4) | copy-done | bytes 8388632
  15.0 0.7 fusion.2
  15.8 0.7 fusion.4.total_ref
  16.5 1.9 %collective-permute-done.2.refs_6_.refs_5_.refs_10_ = bf16[256,1024]{1,0:T(8,128)(2,1)S(1)} collective-permute-done((bf16[256,1024]{1,0:T(8,128)(2,1)S(1)}, bf16[256,1024]{1,0:T(8,128)(2,1)S(1)}, u32[]{:S(2)}, u32[]{:S(2)}) %collective-permute-start.2) | collective-permute-done | bytes 524320 | tf_op jit(solution)/shard_map/ppermute | solution.py:17
  18.4 3.7 %collective-permute-done.1.a_ref = bf16[256,1024]{1,0:T(8,128)(2,1)S(1)} collective-permute-done((bf16[256,1024]{1,0:T(8,128)(2,1)S(1)}, bf16[256,1024]{1,0:T(8,128)(2,1)S(1)}, u32[]{:S(2)}, u32[]{:S(2)}) %collective-permute-start.1) | collective-permute-done | bytes 524320 | tf_op jit(solution)/shard_map/ppermute | solution.py:17
  22.1 1.8 %collective-permute-done.3.b_ref = bf16[256,1024]{1,0:T(8,128)(2,1)S(1)} collective-permute-done((bf16[256,1024]{1,0:T(8,128)(2,1)S(1)}, bf16[256,1024]{1,0:T(8,128)(2,1)S(1)}, u32[]{:S(2)}, u32[]{:S(2)}) %collective-permute-start.3) | collective-permute-done | bytes 524320 | tf_op jit(solution)/shard_map/ppermute | solution.py:17
  24.0 1.9 %shard_map.37 = (bf16[128,1024]{1,0:T(8,128)(2,1)S(1)}, bf16[128,1024]{1,0:T(8,128)(2,1)S(1)}) custom-call(s32[2]{0:T(128)S(1)} %pad_add_fusion.1.place_ref, f32[256,1024]{1,0:T(8,128)S(1)} %fusion.4.total_ref, bf16[256,1024]{1,0:T(8,128)(2,1)S(1)} %collective-permute-done.1.a_ref, bf16[256,1024]{1,0:T(8,128)(2,1)S(1)} %collective-permute-done.3.b_ref, ...), custom_call_target="tpu_custom_call" | custom-call | flops 1073741824 | bytes 6291464 | tf_op jit(solution)/shard_map/pallas_call | solution.py:26
  26.1 1.0 collective-permute-start.8
  27.5 0.6 collective-permute-start.7
  28.0 1.5 %collective-permute-start.6 = (bf16[256,1024]{1,0:T(8,128)(2,1)S(1)}, bf16[256,1024]{1,0:T(8,128)(2,1)}, u32[]{:S(2)}, u32[]{:S(2)}) collective-permute-start(bf16[256,1024]{1,0:T(8,128)(2,1)S(1)} %constant_dynamic-update-slice_fusion.refs_0_), channel_id=1, source_target_pairs={{8,0},{16,8},{24,16},{0,24},{9,1},{17,9},{25,17},{1,25},{10,2},{18... | collective-permute-start | bytes 1572872 | tf_op jit(solution)/shard_map/ppermute | solution.py:17
  29.6 1.6 %collective-permute-start.5 = (bf16[256,1024]{1,0:T(8,128)(2,1)S(1)}, bf16[256,1024]{1,0:T(8,128)(2,1)S(1)}, u32[]{:S(2)}, u32[]{:S(2)}) collective-permute-start(bf16[256,1024]{1,0:T(8,128)(2,1)S(1)} %constant_dynamic-update-slice_fusion.refs_0_), channel_id=1, source_target_pairs={{4,0},{0,4},{5,1},{1,5},{6,2},{2,6},{7,3},{3,7},{12,8},{8,12},{13,... | collective-permute-start | bytes 1572872 | tf_op jit(solution)/shard_map/ppermute | solution.py:17
  31.2 9.1 %collective-permute-done.8.refs_8_.refs_7_.refs_12_ = bf16[256,1024]{1,0:T(8,128)(2,1)S(1)} collective-permute-done((bf16[256,1024]{1,0:T(8,128)(2,1)S(1)}, bf16[256,1024]{1,0:T(8,128)(2,1)S(1)}, u32[]{:S(2)}, u32[]{:S(2)}) %collective-permute-start.8) | collective-permute-done | bytes 524320 | tf_op jit(solution)/shard_map/ppermute | solution.py:17
  40.3 1.3 %collective-permute-done.7.refs_2_ = bf16[256,1024]{1,0:T(8,128)(2,1)S(1)} collective-permute-done((bf16[256,1024]{1,0:T(8,128)(2,1)S(1)}, bf16[256,1024]{1,0:T(8,128)(2,1)S(1)}, u32[]{:S(2)}, u32[]{:S(2)}) %collective-permute-start.7) | collective-permute-done | bytes 524320 | tf_op jit(solution)/shard_map/ppermute | solution.py:17
  41.5 1.5 %collective-permute-done.6.refs_1_ = bf16[256,1024]{1,0:T(8,128)(2,1)} collective-permute-done((bf16[256,1024]{1,0:T(8,128)(2,1)S(1)}, bf16[256,1024]{1,0:T(8,128)(2,1)}, u32[]{:S(2)}, u32[]{:S(2)}) %collective-permute-start.6) | collective-permute-done | bytes 524320 | tf_op jit(solution)/shard_map/ppermute | solution.py:17
  43.0 1.6 %collective-permute-start.10 = (bf16[256,1024]{1,0:T(8,128)(2,1)S(1)}, bf16[256,1024]{1,0:T(8,128)(2,1)S(1)}, u32[]{:S(2)}, u32[]{:S(2)}) collective-permute-start(bf16[256,1024]{1,0:T(8,128)(2,1)S(1)} %collective-permute-done.5.refs_0_.refs_4_), channel_id=1, source_target_pairs={{24,0},{0,8},{8,16},{16,24},{25,1},{1,9},{9,17},{17,25},{26,2},{2,... | collective-permute-start | bytes 1572872 | tf_op jit(solution)/shard_map/ppermute | solution.py:17
  44.7 0.8 copy-done
  45.5 1.0 collective-permute-start.14
  46.9 1.6 %collective-permute-start.9 = (bf16[256,1024]{1,0:T(8,128)(2,1)}, bf16[256,1024]{1,0:T(8,128)(2,1)}, u32[]{:S(2)}, u32[]{:S(2)}) collective-permute-start(bf16[256,1024]{1,0:T(8,128)(2,1)} %collective-permute-done.6.refs_1_), channel_id=1, source_target_pairs={{4,0},{0,4},{5,1},{1,5},{6,2},{2,6},{7,3},{3,7},{12,8},{8,12},{13,... | collective-permute-start | bytes 1572872 | tf_op jit(solution)/shard_map/ppermute | solution.py:17
  48.5 7.4 %collective-permute-done.10.refs_2_.refs_6_ = bf16[256,1024]{1,0:T(8,128)(2,1)S(1)} collective-permute-done((bf16[256,1024]{1,0:T(8,128)(2,1)S(1)}, bf16[256,1024]{1,0:T(8,128)(2,1)S(1)}, u32[]{:S(2)}, u32[]{:S(2)}) %collective-permute-start.10) | collective-permute-done | bytes 524320 | tf_op jit(solution)/shard_map/ppermute | solution.py:17
  55.9 2.0 %collective-permute-done.14.refs_10_.refs_9_.refs_14_ = bf16[256,1024]{1,0:T(8,128)(2,1)} collective-permute-done((bf16[256,1024]{1,0:T(8,128)(2,1)S(1)}, bf16[256,1024]{1,0:T(8,128)(2,1)}, u32[]{:S(2)}, u32[]{:S(2)}) %collective-permute-start.14) | collective-permute-done | bytes 524320 | tf_op jit(solution)/shard_map/ppermute | solution.py:17
  58.0 2.0 %collective-permute-done.11.refs_3_ = bf16[256,1024]{1,0:T(8,128)(2,1)} collective-permute-done((bf16[256,1024]{1,0:T(8,128)(2,1)}, bf16[256,1024]{1,0:T(8,128)(2,1)}, u32[]{:S(2)}, u32[]{:S(2)}) %collective-permute-start.11) | collective-permute-done | bytes 524320 | tf_op jit(solution)/shard_map/ppermute | solution.py:17
  60.0 1.7 %collective-permute-start.19 = (bf16[256,1024]{1,0:T(8,128)(2,1)}, bf16[256,1024]{1,0:T(8,128)(2,1)S(1)}, u32[]{:S(2)}, u32[]{:S(2)}) collective-permute-start(bf16[256,1024]{1,0:T(8,128)(2,1)} %copy-done.2), channel_id=1, source_target_pairs={{24,0},{0,8},{8,16},{16,24},{25,1},{1,9},{9,17},{17,25},{26,2},{2,... | collective-permute-start | bytes 1572872 | tf_op jit(solution)/shard_map/ppermute | solution.py:17
  61.8 1.0 collective-permute-start.20
  62.8 4.3 %shard_map.38 = (bf16[64,3072]{1,0:T(8,128)(2,1)S(1)}, f32[64,3072]{1,0:T(8,128)S(1)}) custom-call(s32[8]{0:T(128)S(1)} %stack.71.late_ref, bf16[256,1024]{1,0:T(8,128)(2,1)S(1)} %constant_dynamic-update-slice_fusion.refs_0_, bf16[256,1024]{1,0:T(8,128)(2,1)} %collective-permute-done.6.refs_1_, bf16[256,1024]{1,0:T(8,128)(2,1)S(1)} %collective-permute-done.7.refs_2_, ...), custom_call_target="tpu_custom_call" | custom-call | flops 12884901888 | bytes 6291488 | tf_op jit(solution)/shard_map/pallas_call | solution.py:26
  67.1 3.3 %collective-permute-start.16 = (bf16[64,3072]{1,0:T(8,128)(2,1)S(1)}, bf16[64,3072]{1,0:T(8,128)(2,1)S(1)}, u32[]{:S(2)}, u32[]{:S(2)}) collective-permute-start(bf16[64,3072]{1,0:T(8,128)(2,1)S(1)} %get-tuple-element.58), channel_id=1, source_target_pairs={{2,0},{0,2},{3,1},{1,3},{6,4},{4,6},{7,5},{5,7},{10,8},{8,10},{11,... | collective-permute-start | bytes 1179656 | tf_op jit(solution)/shard_map/ppermute | solution.py:17
  70.4 3.6 %shard_map.39 = (bf16[64,2304]{1,0:T(8,128)(2,1)S(1)}, bf16[64,2304]{1,0:T(8,128)(2,1)S(1)}) custom-call(s32[8]{0:T(128)S(1)} %stack.71.late_ref, bf16[256,1024]{1,0:T(8,128)(2,1)S(1)} %copy-done.1, bf16[256,1024]{1,0:T(8,128)(2,1)} %collective-permute-done.9.refs_1_.refs_5_, bf16[256,1024]{1,0:T(8,128)(2,1)S(1)} %copy-done.3, ...), custom_call_target="tpu_custom_call" | custom-call | flops 9663676416 | bytes 5767200 | tf_op jit(solution)/shard_map/pallas_call | solution.py:26
  74.0 0.8 collective-permute-start.17
  74.8 0.5 collective-permute-start.18
  75.4 0.5 collective-permute-start.21
  75.9 1.0 collective-permute-done.22.refs_18_
  77.3 5.7 %shard_map.40 = (bf16[64,1280]{1,0:T(8,128)(2,1)S(1)}, f32[64,1280]{1,0:T(8,128)S(1)}, bf16[64,1792]{1,0:T(8,128)(2,1)S(1)}, bf16[64,1792]{1,0:T(8,128)(2,1)S(1)}) custom-call(s32[8]{0:T(128)S(1)} %stack.71.late_ref, bf16[256,1024]{1,0:T(8,128)(2,1)S(1)} %constant_dynamic-update-slice_fusion.refs_0_, bf16[256,1024]{1,0:T(8,128)(2,1)} %collective-permute-done.6.refs_1_, ...), custom_call_target="tpu_custom_call" | custom-call | bytes 9437216 | tf_op jit(solution)/shard_map/pallas_call | solution.py:26
  83.0 1.2 %collective-permute-done.17.refs_2_ = bf16[64,2304]{1,0:T(8,128)(2,1)S(1)} collective-permute-done((bf16[64,2304]{1,0:T(8,128)(2,1)S(1)}, bf16[64,2304]{1,0:T(8,128)(2,1)S(1)}, u32[]{:S(2)}, u32[]{:S(2)}) %collective-permute-start.17) | collective-permute-done | bytes 294944 | tf_op jit(solution)/shard_map/ppermute | solution.py:17
  84.5 1.2 %collective-permute-start.24 = (bf16[64,1792]{1,0:T(8,128)(2,1)S(1)}, bf16[64,1792]{1,0:T(8,128)(2,1)S(1)}, u32[]{:S(2)}, u32[]{:S(2)}) collective-permute-start(bf16[64,1792]{1,0:T(8,128)(2,1)S(1)} %get-tuple-element.72), channel_id=1, source_target_pairs={{4,0},{0,4},{5,1},{1,5},{6,2},{2,6},{7,3},{3,7},{12,8},{8,12},{13,... | collective-permute-start | bytes 688136 | tf_op jit(solution)/shard_map/ppermute | solution.py:17
  85.6 2.1 %collective-permute-start.25 = (bf16[64,1792]{1,0:T(8,128)(2,1)S(1)}, bf16[64,1792]{1,0:T(8,128)(2,1)S(1)}, u32[]{:S(2)}, u32[]{:S(2)}) collective-permute-start(bf16[64,1792]{1,0:T(8,128)(2,1)S(1)} %get-tuple-element.73), channel_id=1, source_target_pairs={{0,6},{2,4},{4,2},{6,0},{1,7},{3,5},{5,3},{7,1},{8,14},{10,12},{12... | collective-permute-start | bytes 688136 | tf_op jit(solution)/shard_map/ppermute | solution.py:21
  87.8 1.5 %collective-permute-start.26 = (bf16[64,1536]{1,0:T(8,128)(2,1)S(1)}, bf16[64,1536]{1,0:T(8,128)(2,1)S(1)}, u32[]{:S(2)}, u32[]{:S(2)}) collective-permute-start(bf16[64,1536]{1,0:T(8,128)(2,1)S(1)} %get-tuple-element.75), channel_id=1, source_target_pairs={{24,0},{0,8},{8,16},{16,24},{25,1},{1,9},{9,17},{17,25},{26,2},{2,... | collective-permute-start | bytes 589832 | tf_op jit(solution)/shard_map/ppermute | solution.py:17
  89.3 0.6 collective-permute-start.27
  89.9 0.9 collective-permute-start.23
  90.8 6.0 %collective-permute-done.23.refs_5_ = bf16[64,1280]{1,0:T(8,128)(2,1)S(1)} collective-permute-done((bf16[64,1280]{1,0:T(8,128)(2,1)S(1)}, bf16[64,1280]{1,0:T(8,128)(2,1)S(1)}, u32[]{:S(2)}, u32[]{:S(2)}) %collective-permute-start.23) | collective-permute-done | bytes 163872 | tf_op jit(solution)/shard_map/ppermute | solution.py:17
  96.9 3.1 %collective-permute-start.30 = (bf16[64,2048]{1,0:T(8,128)(2,1)S(1)}, bf16[64,2048]{1,0:T(8,128)(2,1)S(1)}, u32[]{:S(2)}, u32[]{:S(2)}) collective-permute-start(bf16[64,2048]{1,0:T(8,128)(2,1)S(1)} %get-tuple-element.83), channel_id=1, source_target_pairs={{16,0},{24,8},{0,16},{8,24},{17,1},{25,9},{1,17},{9,25},{18,2},{26... | collective-permute-start | bytes 786440 | tf_op jit(solution)/shard_map/ppermute | solution.py:17
  100.0 2.0 %collective-permute-start.28 = (bf16[64,512]{1,0:T(8,128)(2,1)S(1)}, bf16[64,512]{1,0:T(8,128)(2,1)S(1)}, u32[]{:S(2)}, u32[]{:S(2)}) collective-permute-start(bf16[64,512]{1,0:T(8,128)(2,1)S(1)} %get-tuple-element.81), channel_id=1, source_target_pairs={{24,0},{0,8},{8,16},{16,24},{25,1},{1,9},{9,17},{17,25},{26,2},{2,... | collective-permute-start | bytes 196616 | tf_op jit(solution)/shard_map/ppermute | solution.py:17
  102.1 2.0 %shard_map.43.refs_4_ = f32[33,64,256]{2,1,0:T(8,128)} custom-call(s32[2]{0:T(128)S(1)} %pad_add_fusion.place_ref, f32[64,1536]{1,0:T(8,128)S(1)} %get-tuple-element.84.refs_0_, bf16[64,1536]{1,0:T(8,128)(2,1)S(1)} %collective-permute-done.26.refs_1_, bf16[64,1536]{1,0:T(8,128)(2,1)S(1)} %collective-permute-done.27.refs_2_), custom_call_target="tpu_custom_call" | custom-call | bytes 786440 | tf_op jit(solution)/shard_map/pallas_call | solution.py:26
  104.1 2.1 %collective-permute-done.28.refs_1_ = bf16[64,512]{1,0:T(8,128)(2,1)S(1)} collective-permute-done((bf16[64,512]{1,0:T(8,128)(2,1)S(1)}, bf16[64,512]{1,0:T(8,128)(2,1)S(1)}, u32[]{:S(2)}, u32[]{:S(2)}) %collective-permute-start.28) | collective-permute-done | bytes 65568 | tf_op jit(solution)/shard_map/ppermute | solution.py:17
  106.1 1.3 %collective-permute-done.29.refs_2_ = bf16[64,512]{1,0:T(8,128)(2,1)S(1)} collective-permute-done((bf16[64,512]{1,0:T(8,128)(2,1)S(1)}, bf16[64,512]{1,0:T(8,128)(2,1)S(1)}, u32[]{:S(2)}, u32[]{:S(2)}) %collective-permute-start.29) | collective-permute-done | bytes 65568 | tf_op jit(solution)/shard_map/ppermute | solution.py:17
  107.4 1.6 %shard_map.44 = f32[33,64,256]{2,1,0:T(8,128)} custom-call(s32[2]{0:T(128)S(1)} %pad_add_fusion.place_ref, f32[64,768]{1,0:T(8,128)S(1)} %get-tuple-element.80.refs_0_, bf16[64,512]{1,0:T(8,128)(2,1)S(1)} %collective-permute-done.28.refs_1_, bf16[64,512]{1,0:T(8,128)(2,1)S(1)} %collective-permute-done.29.refs_2_, ...), custom_call_target="tpu_custom_call", output_to_operand_aliasing={{}: (5, {})} | custom-call | tf_op jit(solution)/shard_map/pallas_call | solution.py:200
  (44 shorter events, 2.3 us)
Async XLA Ops:
  1.2 17.1 %collective-permute-start.2 = (bf16[256,1024]{1,0:T(8,128)(2,1)S(1)}, bf16[256,1024]{1,0:T(8,128)(2,1)S(1)}, u32[]{:S(2)}, u32[]{:S(2)}) collective-permute-start(bf16[256,1024]{1,0:T(8,128)(2,1)S(1)} %compare_select_fusion.refs_4_.refs_3_.refs_8_), channel_id=1, source_target_pairs={{32,0},{64,32},{96,64},{128,96},{160,128},{192,160},{224,192},{0,2... | collective-permute-start | bytes 1572872 | tf_op jit(solution)/shard_map/ppermute | solution.py:17
  7.2 14.9 %collective-permute-start.1 = (bf16[256,1024]{1,0:T(8,128)(2,1)S(1)}, bf16[256,1024]{1,0:T(8,128)(2,1)S(1)}, u32[]{:S(2)}, u32[]{:S(2)}) collective-permute-start(bf16[256,1024]{1,0:T(8,128)(2,1)S(1)} %compare_select_fusion.refs_4_.refs_3_.refs_8_), channel_id=1, source_target_pairs={{2,0},{0,2},{3,1},{1,3},{6,4},{4,6},{7,5},{5,7},{10,8},{8,10},{11,... | collective-permute-start | bytes 1572872 | tf_op jit(solution)/shard_map/ppermute | solution.py:17
  10.4 5.4 %collective-permute-start = (bf16[256,1024]{1,0:T(8,128)(2,1)S(1)}, bf16[256,1024]{1,0:T(8,128)(2,1)S(1)}, u32[]{:S(2)}, u32[]{:S(2)}) collective-permute-start(bf16[256,1024]{1,0:T(8,128)(2,1)S(1)} %compare_select_fusion.refs_4_.refs_3_.refs_8_), channel_id=1, source_target_pairs={{1,0},{0,1},{3,2},{2,3},{5,4},{4,5},{7,6},{6,7},{9,8},{8,9},{11,10... | collective-permute-start | bytes 1572872 | tf_op jit(solution)/shard_map/ppermute | solution.py:17
  10.4 4.6 %copy-start.4 = (bf16[4096,1024]{1,0:T(8,128)(2,1)S(1)}, bf16[4096,1024]{1,0:T(8,128)(2,1)}, u32[]{:S(2)}) copy-start(bf16[4096,1024]{1,0:T(8,128)(2,1)} %param.4) | copy-start | bytes 25165828
  22.1 1.9 %collective-permute-start.3 = (bf16[256,1024]{1,0:T(8,128)(2,1)S(1)}, bf16[256,1024]{1,0:T(8,128)(2,1)S(1)}, u32[]{:S(2)}, u32[]{:S(2)}) collective-permute-start(bf16[256,1024]{1,0:T(8,128)(2,1)S(1)} %collective-permute-done.1.a_ref), channel_id=1, source_target_pairs={{1,0},{0,1},{3,2},{2,3},{5,4},{4,5},{7,6},{6,7},{9,8},{8,9},{11,10... | collective-permute-start | bytes 1572872 | tf_op jit(solution)/shard_map/ppermute | solution.py:17
  25.8 1.6 %collective-permute-start.4 = (bf16[128,1024]{1,0:T(8,128)(2,1)S(1)}, bf16[128,1024]{1,0:T(8,128)(2,1)S(1)}, u32[]{:S(2)}, u32[]{:S(2)}) collective-permute-start(bf16[128,1024]{1,0:T(8,128)(2,1)S(1)} %get-tuple-element.50), channel_id=1, source_target_pairs={{1,0},{0,1},{3,2},{2,3},{5,4},{4,5},{7,6},{6,7},{9,8},{8,9},{11,10... | collective-permute-start | bytes 786440 | tf_op jit(solution)/shard_map/ppermute | solution.py:17
  26.1 14.2 %collective-permute-start.8 = (bf16[256,1024]{1,0:T(8,128)(2,1)S(1)}, bf16[256,1024]{1,0:T(8,128)(2,1)S(1)}, u32[]{:S(2)}, u32[]{:S(2)}) collective-permute-start(bf16[256,1024]{1,0:T(8,128)(2,1)S(1)} %collective-permute-done.2.refs_6_.refs_5_.refs_10_), channel_id=1, source_target_pairs={{32,0},{64,32},{96,64},{128,96},{160,128},{192,160},{224,192},{0,2... | collective-permute-start | bytes 1572872 | tf_op jit(solution)/shard_map/ppermute | solution.py:17
  27.5 14.0 %collective-permute-start.7 = (bf16[256,1024]{1,0:T(8,128)(2,1)S(1)}, bf16[256,1024]{1,0:T(8,128)(2,1)S(1)}, u32[]{:S(2)}, u32[]{:S(2)}) collective-permute-start(bf16[256,1024]{1,0:T(8,128)(2,1)S(1)} %constant_dynamic-update-slice_fusion.refs_0_), channel_id=1, source_target_pairs={{24,0},{0,8},{8,16},{16,24},{25,1},{1,9},{9,17},{17,25},{26,2},{2,... | collective-permute-start | bytes 1572872 | tf_op jit(solution)/shard_map/ppermute | solution.py:17
  28.0 15.0 %collective-permute-start.6 = (bf16[256,1024]{1,0:T(8,128)(2,1)S(1)}, bf16[256,1024]{1,0:T(8,128)(2,1)}, u32[]{:S(2)}, u32[]{:S(2)}) collective-permute-start(bf16[256,1024]{1,0:T(8,128)(2,1)S(1)} %constant_dynamic-update-slice_fusion.refs_0_), channel_id=1, source_target_pairs={{8,0},{16,8},{24,16},{0,24},{9,1},{17,9},{25,17},{1,25},{10,2},{18... | collective-permute-start | bytes 1572872 | tf_op jit(solution)/shard_map/ppermute | solution.py:17
  29.6 13.5 %collective-permute-start.5 = (bf16[256,1024]{1,0:T(8,128)(2,1)S(1)}, bf16[256,1024]{1,0:T(8,128)(2,1)S(1)}, u32[]{:S(2)}, u32[]{:S(2)}) collective-permute-start(bf16[256,1024]{1,0:T(8,128)(2,1)S(1)} %constant_dynamic-update-slice_fusion.refs_0_), channel_id=1, source_target_pairs={{4,0},{0,4},{5,1},{1,5},{6,2},{2,6},{7,3},{3,7},{12,8},{8,12},{13,... | collective-permute-start | bytes 1572872 | tf_op jit(solution)/shard_map/ppermute | solution.py:17
  43.0 12.8 %collective-permute-start.10 = (bf16[256,1024]{1,0:T(8,128)(2,1)S(1)}, bf16[256,1024]{1,0:T(8,128)(2,1)S(1)}, u32[]{:S(2)}, u32[]{:S(2)}) collective-permute-start(bf16[256,1024]{1,0:T(8,128)(2,1)S(1)} %collective-permute-done.5.refs_0_.refs_4_), channel_id=1, source_target_pairs={{24,0},{0,8},{8,16},{16,24},{25,1},{1,9},{9,17},{17,25},{26,2},{2,... | collective-permute-start | bytes 1572872 | tf_op jit(solution)/shard_map/ppermute | solution.py:17
  44.7 0.8 copy-start
  45.5 12.4 %collective-permute-start.14 = (bf16[256,1024]{1,0:T(8,128)(2,1)S(1)}, bf16[256,1024]{1,0:T(8,128)(2,1)}, u32[]{:S(2)}, u32[]{:S(2)}) collective-permute-start(bf16[256,1024]{1,0:T(8,128)(2,1)S(1)} %collective-permute-done.8.refs_8_.refs_7_.refs_12_), channel_id=1, source_target_pairs={{32,0},{64,32},{96,64},{128,96},{160,128},{192,160},{224,192},{0,2... | collective-permute-start | bytes 1572872 | tf_op jit(solution)/shard_map/ppermute | solution.py:17
  46.5 13.5 %collective-permute-start.11 = (bf16[256,1024]{1,0:T(8,128)(2,1)}, bf16[256,1024]{1,0:T(8,128)(2,1)}, u32[]{:S(2)}, u32[]{:S(2)}) collective-permute-start(bf16[256,1024]{1,0:T(8,128)(2,1)} %collective-permute-done.6.refs_1_), channel_id=1, source_target_pairs={{8,0},{16,8},{24,16},{0,24},{9,1},{17,9},{25,17},{1,25},{10,2},{18... | collective-permute-start | bytes 1572872 | tf_op jit(solution)/shard_map/ppermute | solution.py:17
  46.9 13.2 %collective-permute-start.9 = (bf16[256,1024]{1,0:T(8,128)(2,1)}, bf16[256,1024]{1,0:T(8,128)(2,1)}, u32[]{:S(2)}, u32[]{:S(2)}) collective-permute-start(bf16[256,1024]{1,0:T(8,128)(2,1)} %collective-permute-done.6.refs_1_), channel_id=1, source_target_pairs={{4,0},{0,4},{5,1},{1,5},{6,2},{2,6},{7,3},{3,7},{12,8},{8,12},{13,... | collective-permute-start | bytes 1572872 | tf_op jit(solution)/shard_map/ppermute | solution.py:17
  48.4 14.3 %collective-permute-start.12 = (bf16[256,1024]{1,0:T(8,128)(2,1)S(1)}, bf16[256,1024]{1,0:T(8,128)(2,1)}, u32[]{:S(2)}, u32[]{:S(2)}) collective-permute-start(bf16[256,1024]{1,0:T(8,128)(2,1)S(1)} %collective-permute-done.2.refs_6_.refs_5_.refs_10_), channel_id=1, source_target_pairs={{1,0},{0,1},{3,2},{2,3},{5,4},{4,5},{7,6},{6,7},{9,8},{8,9},{11,10... | collective-permute-start | bytes 1572872 | tf_op jit(solution)/shard_map/ppermute | solution.py:17
  55.9 2.0 %copy-start.2 = (bf16[256,1024]{1,0:T(8,128)(2,1)}, bf16[256,1024]{1,0:T(8,128)(2,1)S(1)}, u32[]{:S(2)}) copy-start(bf16[256,1024]{1,0:T(8,128)(2,1)S(1)} %collective-permute-done.10.refs_2_.refs_6_) | copy-start | bytes 1572868
  55.9 6.9 %collective-permute-start.13 = (bf16[256,1024]{1,0:T(8,128)(2,1)S(1)}, bf16[256,1024]{1,0:T(8,128)(2,1)}, u32[]{:S(2)}, u32[]{:S(2)}) collective-permute-start(bf16[256,1024]{1,0:T(8,128)(2,1)S(1)} %collective-permute-done.8.refs_8_.refs_7_.refs_12_), channel_id=1, source_target_pairs={{1,0},{0,1},{3,2},{2,3},{5,4},{4,5},{7,6},{6,7},{9,8},{8,9},{11,10... | collective-permute-start | bytes 1572872 | tf_op jit(solution)/shard_map/ppermute | solution.py:17
  57.9 4.9 %collective-permute-start.15 = (bf16[256,1024]{1,0:T(8,128)(2,1)}, bf16[256,1024]{1,0:T(8,128)(2,1)}, u32[]{:S(2)}, u32[]{:S(2)}) collective-permute-start(bf16[256,1024]{1,0:T(8,128)(2,1)} %collective-permute-done.14.refs_10_.refs_9_.refs_14_), channel_id=1, source_target_pairs={{1,0},{0,1},{3,2},{2,3},{5,4},{4,5},{7,6},{6,7},{9,8},{8,9},{11,10... | collective-permute-start | bytes 1572872 | tf_op jit(solution)/shard_map/ppermute | solution.py:17
  58.0 12.4 %copy-start.1 = (bf16[256,1024]{1,0:T(8,128)(2,1)S(1)}, bf16[256,1024]{1,0:T(8,128)(2,1)}, u32[]{:S(2)}) copy-start(bf16[256,1024]{1,0:T(8,128)(2,1)} %copy-done) | copy-start | bytes 1572868
  58.0 12.4 %copy-start.3 = (bf16[256,1024]{1,0:T(8,128)(2,1)S(1)}, bf16[256,1024]{1,0:T(8,128)(2,1)}, u32[]{:S(2)}) copy-start(bf16[256,1024]{1,0:T(8,128)(2,1)} %copy-done.2) | copy-start | bytes 1572868
  60.0 15.4 %collective-permute-start.19 = (bf16[256,1024]{1,0:T(8,128)(2,1)}, bf16[256,1024]{1,0:T(8,128)(2,1)S(1)}, u32[]{:S(2)}, u32[]{:S(2)}) collective-permute-start(bf16[256,1024]{1,0:T(8,128)(2,1)} %copy-done.2), channel_id=1, source_target_pairs={{24,0},{0,8},{8,16},{16,24},{25,1},{1,9},{9,17},{17,25},{26,2},{2,... | collective-permute-start | bytes 1572872 | tf_op jit(solution)/shard_map/ppermute | solution.py:17
  61.8 13.5 %collective-permute-start.20 = (bf16[256,1024]{1,0:T(8,128)(2,1)}, bf16[256,1024]{1,0:T(8,128)(2,1)S(1)}, u32[]{:S(2)}, u32[]{:S(2)}) collective-permute-start(bf16[256,1024]{1,0:T(8,128)(2,1)} %collective-permute-done.14.refs_10_.refs_9_.refs_14_), channel_id=1, source_target_pairs={{32,0},{64,32},{96,64},{128,96},{160,128},{192,160},{224,192},{0,2... | collective-permute-start | bytes 1572872 | tf_op jit(solution)/shard_map/ppermute | solution.py:17
  67.1 17.3 %collective-permute-start.16 = (bf16[64,3072]{1,0:T(8,128)(2,1)S(1)}, bf16[64,3072]{1,0:T(8,128)(2,1)S(1)}, u32[]{:S(2)}, u32[]{:S(2)}) collective-permute-start(bf16[64,3072]{1,0:T(8,128)(2,1)S(1)} %get-tuple-element.58), channel_id=1, source_target_pairs={{2,0},{0,2},{3,1},{1,3},{6,4},{4,6},{7,5},{5,7},{10,8},{8,10},{11,... | collective-permute-start | bytes 1179656 | tf_op jit(solution)/shard_map/ppermute | solution.py:17
  74.0 10.2 %collective-permute-start.17 = (bf16[64,2304]{1,0:T(8,128)(2,1)S(1)}, bf16[64,2304]{1,0:T(8,128)(2,1)S(1)}, u32[]{:S(2)}, u32[]{:S(2)}) collective-permute-start(bf16[64,2304]{1,0:T(8,128)(2,1)S(1)} %get-tuple-element.62), channel_id=1, source_target_pairs={{4,0},{0,4},{5,1},{1,5},{6,2},{2,6},{7,3},{3,7},{12,8},{8,12},{13,... | collective-permute-start | bytes 884744 | tf_op jit(solution)/shard_map/ppermute | solution.py:17
  74.8 9.7 %collective-permute-start.18 = (bf16[64,2304]{1,0:T(8,128)(2,1)S(1)}, bf16[64,2304]{1,0:T(8,128)(2,1)S(1)}, u32[]{:S(2)}, u32[]{:S(2)}) collective-permute-start(bf16[64,2304]{1,0:T(8,128)(2,1)S(1)} %get-tuple-element.63), channel_id=1, source_target_pairs={{0,6},{2,4},{4,2},{6,0},{1,7},{3,5},{5,3},{7,1},{8,14},{10,12},{12... | collective-permute-start | bytes 884744 | tf_op jit(solution)/shard_map/ppermute | solution.py:21
  75.3 1.6 %collective-permute-start.22 = (bf16[128,1024]{1,0:T(8,128)(2,1)S(1)}, bf16[128,1024]{1,0:T(8,128)(2,1)S(1)}, u32[]{:S(2)}, u32[]{:S(2)}) collective-permute-start(bf16[128,1024]{1,0:T(8,128)(2,1)S(1)} %get-tuple-element.87), channel_id=1, source_target_pairs={{1,0},{0,1},{3,2},{2,3},{5,4},{4,5},{7,6},{6,7},{9,8},{8,9},{11,10... | collective-permute-start | bytes 786440 | tf_op jit(solution)/shard_map/ppermute | solution.py:17
  75.4 1.9 %collective-permute-start.21 = (bf16[128,1024]{1,0:T(8,128)(2,1)S(1)}, bf16[128,1024]{1,0:T(8,128)(2,1)S(1)}, u32[]{:S(2)}, u32[]{:S(2)}) collective-permute-start(bf16[128,1024]{1,0:T(8,128)(2,1)S(1)} %get-tuple-element.88), channel_id=1, source_target_pairs={{1,0},{0,1},{3,2},{2,3},{5,4},{4,5},{7,6},{6,7},{9,8},{8,9},{11,10... | collective-permute-start | bytes 786440 | tf_op jit(solution)/shard_map/ppermute | solution.py:17
  84.5 12.3 %collective-permute-start.24 = (bf16[64,1792]{1,0:T(8,128)(2,1)S(1)}, bf16[64,1792]{1,0:T(8,128)(2,1)S(1)}, u32[]{:S(2)}, u32[]{:S(2)}) collective-permute-start(bf16[64,1792]{1,0:T(8,128)(2,1)S(1)} %get-tuple-element.72), channel_id=1, source_target_pairs={{4,0},{0,4},{5,1},{1,5},{6,2},{2,6},{7,3},{3,7},{12,8},{8,12},{13,... | collective-permute-start | bytes 688136 | tf_op jit(solution)/shard_map/ppermute | solution.py:17
  85.6 11.1 %collective-permute-start.25 = (bf16[64,1792]{1,0:T(8,128)(2,1)S(1)}, bf16[64,1792]{1,0:T(8,128)(2,1)S(1)}, u32[]{:S(2)}, u32[]{:S(2)}) collective-permute-start(bf16[64,1792]{1,0:T(8,128)(2,1)S(1)} %get-tuple-element.73), channel_id=1, source_target_pairs={{0,6},{2,4},{4,2},{6,0},{1,7},{3,5},{5,3},{7,1},{8,14},{10,12},{12... | collective-permute-start | bytes 688136 | tf_op jit(solution)/shard_map/ppermute | solution.py:21
  87.8 8.9 %collective-permute-start.26 = (bf16[64,1536]{1,0:T(8,128)(2,1)S(1)}, bf16[64,1536]{1,0:T(8,128)(2,1)S(1)}, u32[]{:S(2)}, u32[]{:S(2)}) collective-permute-start(bf16[64,1536]{1,0:T(8,128)(2,1)S(1)} %get-tuple-element.75), channel_id=1, source_target_pairs={{24,0},{0,8},{8,16},{16,24},{25,1},{1,9},{9,17},{17,25},{26,2},{2,... | collective-permute-start | bytes 589832 | tf_op jit(solution)/shard_map/ppermute | solution.py:17
  89.3 7.4 %collective-permute-start.27 = (bf16[64,1536]{1,0:T(8,128)(2,1)S(1)}, bf16[64,1536]{1,0:T(8,128)(2,1)S(1)}, u32[]{:S(2)}, u32[]{:S(2)}) collective-permute-start(bf16[64,1536]{1,0:T(8,128)(2,1)S(1)} %get-tuple-element.76), channel_id=1, source_target_pairs={{8,0},{16,8},{24,16},{0,24},{9,1},{17,9},{25,17},{1,25},{10,2},{18... | collective-permute-start | bytes 589832 | tf_op jit(solution)/shard_map/ppermute | solution.py:17
  89.9 6.8 %collective-permute-start.23 = (bf16[64,1280]{1,0:T(8,128)(2,1)S(1)}, bf16[64,1280]{1,0:T(8,128)(2,1)S(1)}, u32[]{:S(2)}, u32[]{:S(2)}) collective-permute-start(bf16[64,1280]{1,0:T(8,128)(2,1)S(1)} %get-tuple-element.71), channel_id=1, source_target_pairs={{2,0},{0,2},{3,1},{1,3},{6,4},{4,6},{7,5},{5,7},{10,8},{8,10},{11,... | collective-permute-start | bytes 491528 | tf_op jit(solution)/shard_map/ppermute | solution.py:17
  96.9 10.6 %collective-permute-start.30 = (bf16[64,2048]{1,0:T(8,128)(2,1)S(1)}, bf16[64,2048]{1,0:T(8,128)(2,1)S(1)}, u32[]{:S(2)}, u32[]{:S(2)}) collective-permute-start(bf16[64,2048]{1,0:T(8,128)(2,1)S(1)} %get-tuple-element.83), channel_id=1, source_target_pairs={{16,0},{24,8},{0,16},{8,24},{17,1},{25,9},{1,17},{9,25},{18,2},{26... | collective-permute-start | bytes 786440 | tf_op jit(solution)/shard_map/ppermute | solution.py:17
  100.0 6.1 %collective-permute-start.28 = (bf16[64,512]{1,0:T(8,128)(2,1)S(1)}, bf16[64,512]{1,0:T(8,128)(2,1)S(1)}, u32[]{:S(2)}, u32[]{:S(2)}) collective-permute-start(bf16[64,512]{1,0:T(8,128)(2,1)S(1)} %get-tuple-element.81), channel_id=1, source_target_pairs={{24,0},{0,8},{8,16},{16,24},{25,1},{1,9},{9,17},{17,25},{26,2},{2,... | collective-permute-start | bytes 196616 | tf_op jit(solution)/shard_map/ppermute | solution.py:17
  102.0 5.5 %collective-permute-start.29 = (bf16[64,512]{1,0:T(8,128)(2,1)S(1)}, bf16[64,512]{1,0:T(8,128)(2,1)S(1)}, u32[]{:S(2)}, u32[]{:S(2)}) collective-permute-start(bf16[64,512]{1,0:T(8,128)(2,1)S(1)} %get-tuple-element.82), channel_id=1, source_target_pairs={{8,0},{16,8},{24,16},{0,24},{9,1},{17,9},{25,17},{1,25},{10,2},{18... | collective-permute-start | bytes 196616 | tf_op jit(solution)/shard_map/ppermute | solution.py:17

commit v3 on v2

--- a/solution.py
+++ b/solution.py
@@ -266,13 +266,14 @@
     flip = shift(product, "l", 1)
     up, down = shift(product, "x", 1), shift(product, "x", -1)
 
-    flip, up, down, panels[2] = hold((flip, up, down, panels[2]))
+    first = shift(panels[1], "c", 1)
+    flip, up, down, panels[2], first = hold((flip, up, down, panels[2], first))
     panels.append(shift(panels[-1], "z", 1))
     up_flip, down_flip = shift(up, "l", 1), shift(flip, "x", -1)
     far = shift(up, "x", 1)
-    both = [(masked, beside)] + [(p, shift(p, "c", 1)) for p in panels[1:3]]
-
-    up_flip, down_flip, far = hold((up_flip, down_flip, far))
+    both = [(masked, beside), (panels[1], first), (panels[2], shift(panels[2], "c", 1))]
+
+    up_flip, far = hold((up_flip, far))
     far_flip = shift(down_flip, "x", -1)
     fourth = shift(panels[3], "z", 1)
     both.append((panels[3], shift(panels[3], "c", 1)))

time: 111 us -> 110 us (level)
  waiting for transfers between devices: 43.2 us -> 39.5 us
  starting transfers between devices: 37.9 us -> 39.6 us
    ppermute x29, waiting for transfers between devices: 43.1 us -> 39.4 us  [shift(): lax.ppermute(block, axis, [((i + distance) % n, i) for i in range(n)])]
    ppermute x29, starting transfers between devices: 35.4 us -> 36.5 us  [shift(): lax.ppermute(block, axis, [((i + distance) % n, i) for i in range(n)])]
    unnamed x11 -> x7, local copies, waits for them, and re-layouts: 2.66 us -> 3.69 us
  transfers between devices with their start and end apart: 31 -> 31, of which waited for: 17 -> 16; matrix products, arithmetic and copies ran while one was open for 4% -> 4% of each run, Pallas kernels for 14% -> 15%
where the time goes in v3:
time: 110 us; the launch traced here: 108 us
  starting transfers between devices  39.6 us (36%)
  waiting for transfers between devices  39.5 us (36%)
  Pallas kernels  19.4 us (18%)
  local copies, waits for them, and re-layouts  6.64 us (6%)
  matrix products  1.46 us (1%)
  other arithmetic  1.39 us (1%)
    ppermute x29, waiting for transfers between devices, shift(): lax.ppermute(block, axis, [((i + distance) % n, i) for i in range(n)])  39.4 us
    ppermute x29, starting transfers between devices, shift(): lax.ppermute(block, axis, [((i + distance) % n, i) for i in range(n)])  36.5 us
    pallas_call x7, Pallas kernels, call(): pl.pallas_call(kernel, out_shape=out_shape, in_specs=[SMEM] + [VMEM] * (l...  17.8 us
    unnamed x7, local copies, waits for them, and re-layouts  3.69 us
    ppermute x2, starting transfers between devices, across_and_flip(): return lax.ppermute(block, ('l', 'h'), [(i, 3 - i) for i in range(4)])  3.12 us
    dynamic_slice x1, local copies, waits for them, and re-layouts, per_device(): lax.dynamic_slice_in_dim(jacobi_matrix, (1 - h) * 2 * width, 2 * width, 0)  2.8 us
  transfers between devices with their start and end apart: 31, of which 16 were waited for; matrix products, arithmetic and copies ran while one was open for 4% of the time, Pallas kernels for 15%

profile of v3, /device:TPU:6, one launch (start us, length us, event | category | flops | bytes accessed | tf_op | source)
XLA Modules:
  0.0 108.4 jit_solution(3757351566896965360)
XLA Ops:
  0.0 1.2 %compare_select_fusion.refs_4_.refs_3_.refs_8_ = bf16[256,1024]{1,0:T(8,128)(2,1)S(1)} fusion(bf16[256,1024]{1,0:T(8,128)(2,1)} %param.3, s32[1024]{0:T(1024)S(1)} %iota_add_fusion, s32[256]{0:T(256)} %param.5), kind=kLoop, calls=%fused_computation.5 | loop fusion | flops 524288 | bytes 1053696 | tf_op jit(solution)/shard_map/jit(_where)/select_n | solution.py:222
  1.2 5.9 %collective-permute-start.2 = (bf16[256,1024]{1,0:T(8,128)(2,1)S(1)}, bf16[256,1024]{1,0:T(8,128)(2,1)S(1)}, u32[]{:S(2)}, u32[]{:S(2)}) collective-permute-start(bf16[256,1024]{1,0:T(8,128)(2,1)S(1)} %compare_select_fusion.refs_4_.refs_3_.refs_8_), channel_id=1, source_target_pairs={{32,0},{64,32},{96,64},{128,96},{160,128},{192,160},{224,192},{0,2... | collective-permute-start | bytes 1572872 | tf_op jit(solution)/shard_map/ppermute | solution.py:17
  7.2 3.2 %collective-permute-start.1 = (bf16[256,1024]{1,0:T(8,128)(2,1)S(1)}, bf16[256,1024]{1,0:T(8,128)(2,1)S(1)}, u32[]{:S(2)}, u32[]{:S(2)}) collective-permute-start(bf16[256,1024]{1,0:T(8,128)(2,1)S(1)} %compare_select_fusion.refs_4_.refs_3_.refs_8_), channel_id=1, source_target_pairs={{2,0},{0,2},{3,1},{1,3},{6,4},{4,6},{7,5},{5,7},{10,8},{8,10},{11,... | collective-permute-start | bytes 1572872 | tf_op jit(solution)/shard_map/ppermute | solution.py:17
  10.4 2.8 %constant_dynamic-slice_fusion.slab_ref = bf16[2048,1024]{1,0:T(8,128)(2,1)S(1)} fusion(bf16[4096,1024]{1,0:T(8,128)(2,1)} %param.4, s32[]{:T(128)S(6)} %select_n.47), kind=kLoop, calls=%fused_computation.9 | loop fusion | bytes 8388612 | tf_op jit(solution)/shard_map/dynamic_slice | solution.py:233
  13.2 1.8 %copy-done.2 = bf16[4096,1024]{1,0:T(8,128)(2,1)S(1)} copy-done((bf16[4096,1024]{1,0:T(8,128)(2,1)S(1)}, bf16[4096,1024]{1,0:T(8,128)(2,1)}, u32[]{:S(2)}) %copy-start.2) | copy-done | bytes 8388632
  15.0 0.7 fusion.2
  15.8 0.7 fusion.4.total_ref
  16.5 1.9 %collective-permute-done.2.refs_6_.refs_5_.refs_10_ = bf16[256,1024]{1,0:T(8,128)(2,1)S(1)} collective-permute-done((bf16[256,1024]{1,0:T(8,128)(2,1)S(1)}, bf16[256,1024]{1,0:T(8,128)(2,1)S(1)}, u32[]{:S(2)}, u32[]{:S(2)}) %collective-permute-start.2) | collective-permute-done | bytes 524320 | tf_op jit(solution)/shard_map/ppermute | solution.py:17
  18.4 3.7 %collective-permute-done.1.a_ref = bf16[256,1024]{1,0:T(8,128)(2,1)S(1)} collective-permute-done((bf16[256,1024]{1,0:T(8,128)(2,1)S(1)}, bf16[256,1024]{1,0:T(8,128)(2,1)S(1)}, u32[]{:S(2)}, u32[]{:S(2)}) %collective-permute-start.1) | collective-permute-done | bytes 524320 | tf_op jit(solution)/shard_map/ppermute | solution.py:17
  22.1 1.8 %collective-permute-done.3.b_ref = bf16[256,1024]{1,0:T(8,128)(2,1)S(1)} collective-permute-done((bf16[256,1024]{1,0:T(8,128)(2,1)S(1)}, bf16[256,1024]{1,0:T(8,128)(2,1)S(1)}, u32[]{:S(2)}, u32[]{:S(2)}) %collective-permute-start.3) | collective-permute-done | bytes 524320 | tf_op jit(solution)/shard_map/ppermute | solution.py:17
  24.0 1.9 %shard_map.37 = (bf16[128,1024]{1,0:T(8,128)(2,1)S(1)}, bf16[128,1024]{1,0:T(8,128)(2,1)S(1)}) custom-call(s32[2]{0:T(128)S(1)} %pad_add_fusion.1.place_ref, f32[256,1024]{1,0:T(8,128)S(1)} %fusion.4.total_ref, bf16[256,1024]{1,0:T(8,128)(2,1)S(1)} %collective-permute-done.1.a_ref, bf16[256,1024]{1,0:T(8,128)(2,1)S(1)} %collective-permute-done.3.b_ref, ...), custom_call_target="tpu_custom_call" | custom-call | flops 1073741824 | bytes 6291464 | tf_op jit(solution)/shard_map/pallas_call | solution.py:26
  26.4 1.0 collective-permute-start.8
  27.5 0.6 collective-permute-start.7
  28.1 1.5 %collective-permute-start.6 = (bf16[256,1024]{1,0:T(8,128)(2,1)S(1)}, bf16[256,1024]{1,0:T(8,128)(2,1)}, u32[]{:S(2)}, u32[]{:S(2)}) collective-permute-start(bf16[256,1024]{1,0:T(8,128)(2,1)S(1)} %constant_dynamic-update-slice_fusion.refs_0_), channel_id=1, source_target_pairs={{8,0},{16,8},{24,16},{0,24},{9,1},{17,9},{25,17},{1,25},{10,2},{18... | collective-permute-start | bytes 1572872 | tf_op jit(solution)/shard_map/ppermute | solution.py:17
  29.6 1.6 %collective-permute-start.5 = (bf16[256,1024]{1,0:T(8,128)(2,1)S(1)}, bf16[256,1024]{1,0:T(8,128)(2,1)}, u32[]{:S(2)}, u32[]{:S(2)}) collective-permute-start(bf16[256,1024]{1,0:T(8,128)(2,1)S(1)} %constant_dynamic-update-slice_fusion.refs_0_), channel_id=1, source_target_pairs={{4,0},{0,4},{5,1},{1,5},{6,2},{2,6},{7,3},{3,7},{12,8},{8,12},{13,... | collective-permute-start | bytes 1572872 | tf_op jit(solution)/shard_map/ppermute | solution.py:17
  31.2 9.2 %collective-permute-done.8.refs_8_.refs_7_.refs_12_ = bf16[256,1024]{1,0:T(8,128)(2,1)S(1)} collective-permute-done((bf16[256,1024]{1,0:T(8,128)(2,1)S(1)}, bf16[256,1024]{1,0:T(8,128)(2,1)S(1)}, u32[]{:S(2)}, u32[]{:S(2)}) %collective-permute-start.8) | collective-permute-done | bytes 524320 | tf_op jit(solution)/shard_map/ppermute | solution.py:17
  40.4 1.1 %collective-permute-done.7.refs_2_ = bf16[256,1024]{1,0:T(8,128)(2,1)S(1)} collective-permute-done((bf16[256,1024]{1,0:T(8,128)(2,1)S(1)}, bf16[256,1024]{1,0:T(8,128)(2,1)S(1)}, u32[]{:S(2)}, u32[]{:S(2)}) %collective-permute-start.7) | collective-permute-done | bytes 524320 | tf_op jit(solution)/shard_map/ppermute | solution.py:17
  41.5 0.8 copy-done
  42.3 0.7 collective-permute-done.6.refs_1_
  43.1 1.0 collective-permute-start.13
  44.1 0.8 collective-permute-start.11
  44.9 1.6 %collective-permute-start.10 = (bf16[256,1024]{1,0:T(8,128)(2,1)}, bf16[256,1024]{1,0:T(8,128)(2,1)}, u32[]{:S(2)}, u32[]{:S(2)}) collective-permute-start(bf16[256,1024]{1,0:T(8,128)(2,1)} %collective-permute-done.6.refs_1_), channel_id=1, source_target_pairs={{4,0},{0,4},{5,1},{1,5},{6,2},{2,6},{7,3},{3,7},{12,8},{8,12},{13,... | collective-permute-start | bytes 1572872 | tf_op jit(solution)/shard_map/ppermute | solution.py:17
  46.5 2.4 %collective-permute-start.16 = (bf16[256,1024]{1,0:T(8,128)(2,1)}, bf16[256,1024]{1,0:T(8,128)(2,1)}, u32[]{:S(2)}, u32[]{:S(2)}) collective-permute-start(bf16[256,1024]{1,0:T(8,128)(2,1)} %collective-permute-done.5.refs_0_.refs_4_), channel_id=1, source_target_pairs={{24,0},{0,8},{8,16},{16,24},{25,1},{1,9},{9,17},{17,25},{26,2},{2,... | collective-permute-start | bytes 1572872 | tf_op jit(solution)/shard_map/ppermute | solution.py:17
  48.9 7.0 %collective-permute-done.13.refs_10_.refs_9_.refs_14_ = bf16[256,1024]{1,0:T(8,128)(2,1)} collective-permute-done((bf16[256,1024]{1,0:T(8,128)(2,1)S(1)}, bf16[256,1024]{1,0:T(8,128)(2,1)}, u32[]{:S(2)}, u32[]{:S(2)}) %collective-permute-start.13) | collective-permute-done | bytes 524320 | tf_op jit(solution)/shard_map/ppermute | solution.py:17
  56.1 2.0 %collective-permute-done.11.refs_3_ = bf16[256,1024]{1,0:T(8,128)(2,1)} collective-permute-done((bf16[256,1024]{1,0:T(8,128)(2,1)}, bf16[256,1024]{1,0:T(8,128)(2,1)}, u32[]{:S(2)}, u32[]{:S(2)}) %collective-permute-start.11) | collective-permute-done | bytes 524320 | tf_op jit(solution)/shard_map/ppermute | solution.py:17
  58.1 1.0 collective-permute-start.20
  59.1 3.2 %collective-permute-start.19 = (bf16[256,1024]{1,0:T(8,128)(2,1)}, bf16[256,1024]{1,0:T(8,128)(2,1)S(1)}, u32[]{:S(2)}, u32[]{:S(2)}) collective-permute-start(bf16[256,1024]{1,0:T(8,128)(2,1)} %collective-permute-done.16.refs_2_.refs_6_), channel_id=1, source_target_pairs={{24,0},{0,8},{8,16},{16,24},{25,1},{1,9},{9,17},{17,25},{26,2},{2,... | collective-permute-start | bytes 1572872 | tf_op jit(solution)/shard_map/ppermute | solution.py:17
  62.4 1.0 copy-done.1
  63.4 4.2 %shard_map.38 = (bf16[64,3072]{1,0:T(8,128)(2,1)S(1)}, f32[64,3072]{1,0:T(8,128)S(1)}) custom-call(s32[8]{0:T(128)S(1)} %stack.71.late_ref, bf16[256,1024]{1,0:T(8,128)(2,1)S(1)} %constant_dynamic-update-slice_fusion.refs_0_, bf16[256,1024]{1,0:T(8,128)(2,1)} %collective-permute-done.6.refs_1_, bf16[256,1024]{1,0:T(8,128)(2,1)S(1)} %copy-done.1, ...), custom_call_target="tpu_custom_call" | custom-call | flops 12884901888 | bytes 6291488 | tf_op jit(solution)/shard_map/pallas_call | solution.py:26
  67.6 3.0 %collective-permute-start.15 = (bf16[64,3072]{1,0:T(8,128)(2,1)S(1)}, bf16[64,3072]{1,0:T(8,128)(2,1)S(1)}, u32[]{:S(2)}, u32[]{:S(2)}) collective-permute-start(bf16[64,3072]{1,0:T(8,128)(2,1)S(1)} %get-tuple-element.58), channel_id=1, source_target_pairs={{2,0},{0,2},{3,1},{1,3},{6,4},{4,6},{7,5},{5,7},{10,8},{8,10},{11,... | collective-permute-start | bytes 1179656 | tf_op jit(solution)/shard_map/ppermute | solution.py:17
  70.5 3.7 %shard_map.39 = (bf16[64,2304]{1,0:T(8,128)(2,1)S(1)}, bf16[64,2304]{1,0:T(8,128)(2,1)S(1)}) custom-call(s32[8]{0:T(128)S(1)} %stack.71.late_ref, bf16[256,1024]{1,0:T(8,128)(2,1)} %collective-permute-done.5.refs_0_.refs_4_, bf16[256,1024]{1,0:T(8,128)(2,1)} %collective-permute-done.10.refs_1_.refs_5_, ...), custom_call_target="tpu_custom_call" | custom-call | flops 9663676416 | bytes 5767200 | tf_op jit(solution)/shard_map/pallas_call | solution.py:26
  74.5 1.1 collective-permute-start.18
  75.7 0.5 collective-permute-start.21
  76.2 1.0 collective-permute-done.22.refs_18_
  77.6 5.9 %shard_map.40 = (bf16[64,1280]{1,0:T(8,128)(2,1)S(1)}, f32[64,1280]{1,0:T(8,128)S(1)}, bf16[64,1792]{1,0:T(8,128)(2,1)S(1)}, bf16[64,1792]{1,0:T(8,128)(2,1)S(1)}) custom-call(s32[8]{0:T(128)S(1)} %stack.71.late_ref, bf16[256,1024]{1,0:T(8,128)(2,1)S(1)} %constant_dynamic-update-slice_fusion.refs_0_, bf16[256,1024]{1,0:T(8,128)(2,1)} %collective-permute-done.6.refs_1_, ...), custom_call_target="tpu_custom_call" | custom-call | bytes 9437216 | tf_op jit(solution)/shard_map/pallas_call | solution.py:26
  83.5 0.7 collective-permute-done.17.refs_2_
  84.4 1.2 %collective-permute-start.24 = (bf16[64,1792]{1,0:T(8,128)(2,1)S(1)}, bf16[64,1792]{1,0:T(8,128)(2,1)S(1)}, u32[]{:S(2)}, u32[]{:S(2)}) collective-permute-start(bf16[64,1792]{1,0:T(8,128)(2,1)S(1)} %get-tuple-element.72), channel_id=1, source_target_pairs={{4,0},{0,4},{5,1},{1,5},{6,2},{2,6},{7,3},{3,7},{12,8},{8,12},{13,... | collective-permute-start | bytes 688136 | tf_op jit(solution)/shard_map/ppermute | solution.py:17
  85.6 2.1 %collective-permute-start.25 = (bf16[64,1792]{1,0:T(8,128)(2,1)S(1)}, bf16[64,1792]{1,0:T(8,128)(2,1)S(1)}, u32[]{:S(2)}, u32[]{:S(2)}) collective-permute-start(bf16[64,1792]{1,0:T(8,128)(2,1)S(1)} %get-tuple-element.73), channel_id=1, source_target_pairs={{0,6},{2,4},{4,2},{6,0},{1,7},{3,5},{5,3},{7,1},{8,14},{10,12},{12... | collective-permute-start | bytes 688136 | tf_op jit(solution)/shard_map/ppermute | solution.py:21
  87.8 0.4 collective-permute-start.26
  88.2 1.7 %collective-permute-start.27 = (bf16[64,1536]{1,0:T(8,128)(2,1)S(1)}, bf16[64,1536]{1,0:T(8,128)(2,1)S(1)}, u32[]{:S(2)}, u32[]{:S(2)}) collective-permute-start(bf16[64,1536]{1,0:T(8,128)(2,1)S(1)} %get-tuple-element.76), channel_id=1, source_target_pairs={{8,0},{16,8},{24,16},{0,24},{9,1},{17,9},{25,17},{1,25},{10,2},{18... | collective-permute-start | bytes 589832 | tf_op jit(solution)/shard_map/ppermute | solution.py:17
  89.9 0.9 collective-permute-start.23
  90.7 6.0 %collective-permute-done.23.refs_5_ = bf16[64,1280]{1,0:T(8,128)(2,1)S(1)} collective-permute-done((bf16[64,1280]{1,0:T(8,128)(2,1)S(1)}, bf16[64,1280]{1,0:T(8,128)(2,1)S(1)}, u32[]{:S(2)}, u32[]{:S(2)}) %collective-permute-start.23) | collective-permute-done | bytes 163872 | tf_op jit(solution)/shard_map/ppermute | solution.py:17
  96.8 2.0 %collective-permute-start.30 = (bf16[64,2048]{1,0:T(8,128)(2,1)S(1)}, bf16[64,2048]{1,0:T(8,128)(2,1)S(1)}, u32[]{:S(2)}, u32[]{:S(2)}) collective-permute-start(bf16[64,2048]{1,0:T(8,128)(2,1)S(1)} %get-tuple-element.83), channel_id=1, source_target_pairs={{16,0},{24,8},{0,16},{8,24},{17,1},{25,9},{1,17},{9,25},{18,2},{26... | collective-permute-start | bytes 786440 | tf_op jit(solution)/shard_map/ppermute | solution.py:17
  98.9 2.0 %collective-permute-start.28 = (bf16[64,512]{1,0:T(8,128)(2,1)S(1)}, bf16[64,512]{1,0:T(8,128)(2,1)S(1)}, u32[]{:S(2)}, u32[]{:S(2)}) collective-permute-start(bf16[64,512]{1,0:T(8,128)(2,1)S(1)} %get-tuple-element.81), channel_id=1, source_target_pairs={{24,0},{0,8},{8,16},{16,24},{25,1},{1,9},{9,17},{17,25},{26,2},{2,... | collective-permute-start | bytes 196616 | tf_op jit(solution)/shard_map/ppermute | solution.py:17
  101.0 2.0 %shard_map.43.refs_4_ = f32[33,64,256]{2,1,0:T(8,128)} custom-call(s32[2]{0:T(128)S(1)} %pad_add_fusion.place_ref, f32[64,1536]{1,0:T(8,128)S(1)} %get-tuple-element.84.refs_0_, bf16[64,1536]{1,0:T(8,128)(2,1)S(1)} %collective-permute-done.26.refs_1_, bf16[64,1536]{1,0:T(8,128)(2,1)S(1)} %collective-permute-done.27.refs_2_), custom_call_target="tpu_custom_call" | custom-call | bytes 786440 | tf_op jit(solution)/shard_map/pallas_call | solution.py:26
  102.9 2.1 %collective-permute-done.28.refs_1_ = bf16[64,512]{1,0:T(8,128)(2,1)S(1)} collective-permute-done((bf16[64,512]{1,0:T(8,128)(2,1)S(1)}, bf16[64,512]{1,0:T(8,128)(2,1)S(1)}, u32[]{:S(2)}, u32[]{:S(2)}) %collective-permute-start.28) | collective-permute-done | bytes 65568 | tf_op jit(solution)/shard_map/ppermute | solution.py:17
  105.1 1.5 %collective-permute-done.29.refs_2_ = bf16[64,512]{1,0:T(8,128)(2,1)S(1)} collective-permute-done((bf16[64,512]{1,0:T(8,128)(2,1)S(1)}, bf16[64,512]{1,0:T(8,128)(2,1)S(1)}, u32[]{:S(2)}, u32[]{:S(2)}) %collective-permute-start.29) | collective-permute-done | bytes 65568 | tf_op jit(solution)/shard_map/ppermute | solution.py:17
  106.6 1.6 %shard_map.44 = f32[33,64,256]{2,1,0:T(8,128)} custom-call(s32[2]{0:T(128)S(1)} %pad_add_fusion.place_ref, f32[64,768]{1,0:T(8,128)S(1)} %get-tuple-element.80.refs_0_, bf16[64,512]{1,0:T(8,128)(2,1)S(1)} %collective-permute-done.28.refs_1_, bf16[64,512]{1,0:T(8,128)(2,1)S(1)} %collective-permute-done.29.refs_2_, ...), custom_call_target="tpu_custom_call", output_to_operand_aliasing={{}: (5, {})} | custom-call | tf_op jit(solution)/shard_map/pallas_call | solution.py:200
  (40 shorter events, 2.2 us)
Async XLA Ops:
  1.2 17.1 %collective-permute-start.2 = (bf16[256,1024]{1,0:T(8,128)(2,1)S(1)}, bf16[256,1024]{1,0:T(8,128)(2,1)S(1)}, u32[]{:S(2)}, u32[]{:S(2)}) collective-permute-start(bf16[256,1024]{1,0:T(8,128)(2,1)S(1)} %compare_select_fusion.refs_4_.refs_3_.refs_8_), channel_id=1, source_target_pairs={{32,0},{64,32},{96,64},{128,96},{160,128},{192,160},{224,192},{0,2... | collective-permute-start | bytes 1572872 | tf_op jit(solution)/shard_map/ppermute | solution.py:17
  7.2 14.9 %collective-permute-start.1 = (bf16[256,1024]{1,0:T(8,128)(2,1)S(1)}, bf16[256,1024]{1,0:T(8,128)(2,1)S(1)}, u32[]{:S(2)}, u32[]{:S(2)}) collective-permute-start(bf16[256,1024]{1,0:T(8,128)(2,1)S(1)} %compare_select_fusion.refs_4_.refs_3_.refs_8_), channel_id=1, source_target_pairs={{2,0},{0,2},{3,1},{1,3},{6,4},{4,6},{7,5},{5,7},{10,8},{8,10},{11,... | collective-permute-start | bytes 1572872 | tf_op jit(solution)/shard_map/ppermute | solution.py:17
  10.4 5.4 %collective-permute-start = (bf16[256,1024]{1,0:T(8,128)(2,1)S(1)}, bf16[256,1024]{1,0:T(8,128)(2,1)S(1)}, u32[]{:S(2)}, u32[]{:S(2)}) collective-permute-start(bf16[256,1024]{1,0:T(8,128)(2,1)S(1)} %compare_select_fusion.refs_4_.refs_3_.refs_8_), channel_id=1, source_target_pairs={{1,0},{0,1},{3,2},{2,3},{5,4},{4,5},{7,6},{6,7},{9,8},{8,9},{11,10... | collective-permute-start | bytes 1572872 | tf_op jit(solution)/shard_map/ppermute | solution.py:17
  10.4 4.6 %copy-start.2 = (bf16[4096,1024]{1,0:T(8,128)(2,1)S(1)}, bf16[4096,1024]{1,0:T(8,128)(2,1)}, u32[]{:S(2)}) copy-start(bf16[4096,1024]{1,0:T(8,128)(2,1)} %param.4) | copy-start | bytes 25165828
  22.1 1.9 %collective-permute-start.3 = (bf16[256,1024]{1,0:T(8,128)(2,1)S(1)}, bf16[256,1024]{1,0:T(8,128)(2,1)S(1)}, u32[]{:S(2)}, u32[]{:S(2)}) collective-permute-start(bf16[256,1024]{1,0:T(8,128)(2,1)S(1)} %collective-permute-done.1.a_ref), channel_id=1, source_target_pairs={{1,0},{0,1},{3,2},{2,3},{5,4},{4,5},{7,6},{6,7},{9,8},{8,9},{11,10... | collective-permute-start | bytes 1572872 | tf_op jit(solution)/shard_map/ppermute | solution.py:17
  25.8 1.6 %collective-permute-start.4 = (bf16[128,1024]{1,0:T(8,128)(2,1)S(1)}, bf16[128,1024]{1,0:T(8,128)(2,1)S(1)}, u32[]{:S(2)}, u32[]{:S(2)}) collective-permute-start(bf16[128,1024]{1,0:T(8,128)(2,1)S(1)} %get-tuple-element.50), channel_id=1, source_target_pairs={{1,0},{0,1},{3,2},{2,3},{5,4},{4,5},{7,6},{6,7},{9,8},{8,9},{11,10... | collective-permute-start | bytes 786440 | tf_op jit(solution)/shard_map/ppermute | solution.py:17
  26.1 5.1 %collective-permute-start.9 = (bf16[256,1024]{1,0:T(8,128)(2,1)S(1)}, bf16[256,1024]{1,0:T(8,128)(2,1)S(1)}, u32[]{:S(2)}, u32[]{:S(2)}) collective-permute-start(bf16[256,1024]{1,0:T(8,128)(2,1)S(1)} %collective-permute-done.2.refs_6_.refs_5_.refs_10_), channel_id=1, source_target_pairs={{1,0},{0,1},{3,2},{2,3},{5,4},{4,5},{7,6},{6,7},{9,8},{8,9},{11,10... | collective-permute-start | bytes 1572872 | tf_op jit(solution)/shard_map/ppermute | solution.py:17
  26.4 14.0 %collective-permute-start.8 = (bf16[256,1024]{1,0:T(8,128)(2,1)S(1)}, bf16[256,1024]{1,0:T(8,128)(2,1)S(1)}, u32[]{:S(2)}, u32[]{:S(2)}) collective-permute-start(bf16[256,1024]{1,0:T(8,128)(2,1)S(1)} %collective-permute-done.2.refs_6_.refs_5_.refs_10_), channel_id=1, source_target_pairs={{32,0},{64,32},{96,64},{128,96},{160,128},{192,160},{224,192},{0,2... | collective-permute-start | bytes 1572872 | tf_op jit(solution)/shard_map/ppermute | solution.py:17
  27.5 14.0 %collective-permute-start.7 = (bf16[256,1024]{1,0:T(8,128)(2,1)S(1)}, bf16[256,1024]{1,0:T(8,128)(2,1)S(1)}, u32[]{:S(2)}, u32[]{:S(2)}) collective-permute-start(bf16[256,1024]{1,0:T(8,128)(2,1)S(1)} %constant_dynamic-update-slice_fusion.refs_0_), channel_id=1, source_target_pairs={{24,0},{0,8},{8,16},{16,24},{25,1},{1,9},{9,17},{17,25},{26,2},{2,... | collective-permute-start | bytes 1572872 | tf_op jit(solution)/shard_map/ppermute | solution.py:17
  28.1 15.0 %collective-permute-start.6 = (bf16[256,1024]{1,0:T(8,128)(2,1)S(1)}, bf16[256,1024]{1,0:T(8,128)(2,1)}, u32[]{:S(2)}, u32[]{:S(2)}) collective-permute-start(bf16[256,1024]{1,0:T(8,128)(2,1)S(1)} %constant_dynamic-update-slice_fusion.refs_0_), channel_id=1, source_target_pairs={{8,0},{16,8},{24,16},{0,24},{9,1},{17,9},{25,17},{1,25},{10,2},{18... | collective-permute-start | bytes 1572872 | tf_op jit(solution)/shard_map/ppermute | solution.py:17
  29.6 13.5 %collective-permute-start.5 = (bf16[256,1024]{1,0:T(8,128)(2,1)S(1)}, bf16[256,1024]{1,0:T(8,128)(2,1)}, u32[]{:S(2)}, u32[]{:S(2)}) collective-permute-start(bf16[256,1024]{1,0:T(8,128)(2,1)S(1)} %constant_dynamic-update-slice_fusion.refs_0_), channel_id=1, source_target_pairs={{4,0},{0,4},{5,1},{1,5},{6,2},{2,6},{7,3},{3,7},{12,8},{8,12},{13,... | collective-permute-start | bytes 1572872 | tf_op jit(solution)/shard_map/ppermute | solution.py:17
  41.5 0.8 copy-start
  43.1 12.8 %collective-permute-start.13 = (bf16[256,1024]{1,0:T(8,128)(2,1)S(1)}, bf16[256,1024]{1,0:T(8,128)(2,1)}, u32[]{:S(2)}, u32[]{:S(2)}) collective-permute-start(bf16[256,1024]{1,0:T(8,128)(2,1)S(1)} %collective-permute-done.8.refs_8_.refs_7_.refs_12_), channel_id=1, source_target_pairs={{32,0},{64,32},{96,64},{128,96},{160,128},{192,160},{224,192},{0,2... | collective-permute-start | bytes 1572872 | tf_op jit(solution)/shard_map/ppermute | solution.py:17
  44.1 14.0 %collective-permute-start.11 = (bf16[256,1024]{1,0:T(8,128)(2,1)}, bf16[256,1024]{1,0:T(8,128)(2,1)}, u32[]{:S(2)}, u32[]{:S(2)}) collective-permute-start(bf16[256,1024]{1,0:T(8,128)(2,1)} %collective-permute-done.6.refs_1_), channel_id=1, source_target_pairs={{8,0},{16,8},{24,16},{0,24},{9,1},{17,9},{25,17},{1,25},{10,2},{18... | collective-permute-start | bytes 1572872 | tf_op jit(solution)/shard_map/ppermute | solution.py:17
  44.9 13.2 %collective-permute-start.10 = (bf16[256,1024]{1,0:T(8,128)(2,1)}, bf16[256,1024]{1,0:T(8,128)(2,1)}, u32[]{:S(2)}, u32[]{:S(2)}) collective-permute-start(bf16[256,1024]{1,0:T(8,128)(2,1)} %collective-permute-done.6.refs_1_), channel_id=1, source_target_pairs={{4,0},{0,4},{5,1},{1,5},{6,2},{2,6},{7,3},{3,7},{12,8},{8,12},{13,... | collective-permute-start | bytes 1572872 | tf_op jit(solution)/shard_map/ppermute | solution.py:17
  46.5 12.6 %collective-permute-start.16 = (bf16[256,1024]{1,0:T(8,128)(2,1)}, bf16[256,1024]{1,0:T(8,128)(2,1)}, u32[]{:S(2)}, u32[]{:S(2)}) collective-permute-start(bf16[256,1024]{1,0:T(8,128)(2,1)} %collective-permute-done.5.refs_0_.refs_4_), channel_id=1, source_target_pairs={{24,0},{0,8},{8,16},{16,24},{25,1},{1,9},{9,17},{17,25},{26,2},{2,... | collective-permute-start | bytes 1572872 | tf_op jit(solution)/shard_map/ppermute | solution.py:17
  48.9 13.4 %collective-permute-start.12 = (bf16[256,1024]{1,0:T(8,128)(2,1)S(1)}, bf16[256,1024]{1,0:T(8,128)(2,1)}, u32[]{:S(2)}, u32[]{:S(2)}) collective-permute-start(bf16[256,1024]{1,0:T(8,128)(2,1)S(1)} %collective-permute-done.8.refs_8_.refs_7_.refs_12_), channel_id=1, source_target_pairs={{1,0},{0,1},{3,2},{2,3},{5,4},{4,5},{7,6},{6,7},{9,8},{8,9},{11,10... | collective-permute-start | bytes 1572872 | tf_op jit(solution)/shard_map/ppermute | solution.py:17
  55.9 6.4 %collective-permute-start.14 = (bf16[256,1024]{1,0:T(8,128)(2,1)}, bf16[256,1024]{1,0:T(8,128)(2,1)}, u32[]{:S(2)}, u32[]{:S(2)}) collective-permute-start(bf16[256,1024]{1,0:T(8,128)(2,1)} %collective-permute-done.13.refs_10_.refs_9_.refs_14_), channel_id=1, source_target_pairs={{1,0},{0,1},{3,2},{2,3},{5,4},{4,5},{7,6},{6,7},{9,8},{8,9},{11,10... | collective-permute-start | bytes 1572872 | tf_op jit(solution)/shard_map/ppermute | solution.py:17
  58.1 17.5 %collective-permute-start.20 = (bf16[256,1024]{1,0:T(8,128)(2,1)}, bf16[256,1024]{1,0:T(8,128)(2,1)S(1)}, u32[]{:S(2)}, u32[]{:S(2)}) collective-permute-start(bf16[256,1024]{1,0:T(8,128)(2,1)} %collective-permute-done.13.refs_10_.refs_9_.refs_14_), channel_id=1, source_target_pairs={{32,0},{64,32},{96,64},{128,96},{160,128},{192,160},{224,192},{0,2... | collective-permute-start | bytes 1572872 | tf_op jit(solution)/shard_map/ppermute | solution.py:17
  59.1 16.6 %collective-permute-start.19 = (bf16[256,1024]{1,0:T(8,128)(2,1)}, bf16[256,1024]{1,0:T(8,128)(2,1)S(1)}, u32[]{:S(2)}, u32[]{:S(2)}) collective-permute-start(bf16[256,1024]{1,0:T(8,128)(2,1)} %collective-permute-done.16.refs_2_.refs_6_), channel_id=1, source_target_pairs={{24,0},{0,8},{8,16},{16,24},{25,1},{1,9},{9,17},{17,25},{26,2},{2,... | collective-permute-start | bytes 1572872 | tf_op jit(solution)/shard_map/ppermute | solution.py:17
  62.4 1.0 copy-start.1
  67.6 16.9 %collective-permute-start.15 = (bf16[64,3072]{1,0:T(8,128)(2,1)S(1)}, bf16[64,3072]{1,0:T(8,128)(2,1)S(1)}, u32[]{:S(2)}, u32[]{:S(2)}) collective-permute-start(bf16[64,3072]{1,0:T(8,128)(2,1)S(1)} %get-tuple-element.58), channel_id=1, source_target_pairs={{2,0},{0,2},{3,1},{1,3},{6,4},{4,6},{7,5},{5,7},{10,8},{8,10},{11,... | collective-permute-start | bytes 1179656 | tf_op jit(solution)/shard_map/ppermute | solution.py:17
  74.3 9.9 %collective-permute-start.17 = (bf16[64,2304]{1,0:T(8,128)(2,1)S(1)}, bf16[64,2304]{1,0:T(8,128)(2,1)S(1)}, u32[]{:S(2)}, u32[]{:S(2)}) collective-permute-start(bf16[64,2304]{1,0:T(8,128)(2,1)S(1)} %get-tuple-element.62), channel_id=1, source_target_pairs={{4,0},{0,4},{5,1},{1,5},{6,2},{2,6},{7,3},{3,7},{12,8},{8,12},{13,... | collective-permute-start | bytes 884744 | tf_op jit(solution)/shard_map/ppermute | solution.py:17
  74.5 9.9 %collective-permute-start.18 = (bf16[64,2304]{1,0:T(8,128)(2,1)S(1)}, bf16[64,2304]{1,0:T(8,128)(2,1)S(1)}, u32[]{:S(2)}, u32[]{:S(2)}) collective-permute-start(bf16[64,2304]{1,0:T(8,128)(2,1)S(1)} %get-tuple-element.63), channel_id=1, source_target_pairs={{0,6},{2,4},{4,2},{6,0},{1,7},{3,5},{5,3},{7,1},{8,14},{10,12},{12... | collective-permute-start | bytes 884744 | tf_op jit(solution)/shard_map/ppermute | solution.py:21
  75.6 1.6 %collective-permute-start.22 = (bf16[128,1024]{1,0:T(8,128)(2,1)S(1)}, bf16[128,1024]{1,0:T(8,128)(2,1)S(1)}, u32[]{:S(2)}, u32[]{:S(2)}) collective-permute-start(bf16[128,1024]{1,0:T(8,128)(2,1)S(1)} %get-tuple-element.87), channel_id=1, source_target_pairs={{1,0},{0,1},{3,2},{2,3},{5,4},{4,5},{7,6},{6,7},{9,8},{8,9},{11,10... | collective-permute-start | bytes 786440 | tf_op jit(solution)/shard_map/ppermute | solution.py:17
  75.7 1.9 %collective-permute-start.21 = (bf16[128,1024]{1,0:T(8,128)(2,1)S(1)}, bf16[128,1024]{1,0:T(8,128)(2,1)S(1)}, u32[]{:S(2)}, u32[]{:S(2)}) collective-permute-start(bf16[128,1024]{1,0:T(8,128)(2,1)S(1)} %get-tuple-element.88), channel_id=1, source_target_pairs={{1,0},{0,1},{3,2},{2,3},{5,4},{4,5},{7,6},{6,7},{9,8},{8,9},{11,10... | collective-permute-start | bytes 786440 | tf_op jit(solution)/shard_map/ppermute | solution.py:17
  84.4 12.3 %collective-permute-start.24 = (bf16[64,1792]{1,0:T(8,128)(2,1)S(1)}, bf16[64,1792]{1,0:T(8,128)(2,1)S(1)}, u32[]{:S(2)}, u32[]{:S(2)}) collective-permute-start(bf16[64,1792]{1,0:T(8,128)(2,1)S(1)} %get-tuple-element.72), channel_id=1, source_target_pairs={{4,0},{0,4},{5,1},{1,5},{6,2},{2,6},{7,3},{3,7},{12,8},{8,12},{13,... | collective-permute-start | bytes 688136 | tf_op jit(solution)/shard_map/ppermute | solution.py:17
  85.6 11.1 %collective-permute-start.25 = (bf16[64,1792]{1,0:T(8,128)(2,1)S(1)}, bf16[64,1792]{1,0:T(8,128)(2,1)S(1)}, u32[]{:S(2)}, u32[]{:S(2)}) collective-permute-start(bf16[64,1792]{1,0:T(8,128)(2,1)S(1)} %get-tuple-element.73), channel_id=1, source_target_pairs={{0,6},{2,4},{4,2},{6,0},{1,7},{3,5},{5,3},{7,1},{8,14},{10,12},{12... | collective-permute-start | bytes 688136 | tf_op jit(solution)/shard_map/ppermute | solution.py:21
  87.8 8.9 %collective-permute-start.26 = (bf16[64,1536]{1,0:T(8,128)(2,1)S(1)}, bf16[64,1536]{1,0:T(8,128)(2,1)S(1)}, u32[]{:S(2)}, u32[]{:S(2)}) collective-permute-start(bf16[64,1536]{1,0:T(8,128)(2,1)S(1)} %get-tuple-element.75), channel_id=1, source_target_pairs={{24,0},{0,8},{8,16},{16,24},{25,1},{1,9},{9,17},{17,25},{26,2},{2,... | collective-permute-start | bytes 589832 | tf_op jit(solution)/shard_map/ppermute | solution.py:17
  88.2 8.5 %collective-permute-start.27 = (bf16[64,1536]{1,0:T(8,128)(2,1)S(1)}, bf16[64,1536]{1,0:T(8,128)(2,1)S(1)}, u32[]{:S(2)}, u32[]{:S(2)}) collective-permute-start(bf16[64,1536]{1,0:T(8,128)(2,1)S(1)} %get-tuple-element.76), channel_id=1, source_target_pairs={{8,0},{16,8},{24,16},{0,24},{9,1},{17,9},{25,17},{1,25},{10,2},{18... | collective-permute-start | bytes 589832 | tf_op jit(solution)/shard_map/ppermute | solution.py:17
  89.9 6.8 %collective-permute-start.23 = (bf16[64,1280]{1,0:T(8,128)(2,1)S(1)}, bf16[64,1280]{1,0:T(8,128)(2,1)S(1)}, u32[]{:S(2)}, u32[]{:S(2)}) collective-permute-start(bf16[64,1280]{1,0:T(8,128)(2,1)S(1)} %get-tuple-element.71), channel_id=1, source_target_pairs={{2,0},{0,2},{3,1},{1,3},{6,4},{4,6},{7,5},{5,7},{10,8},{8,10},{11,... | collective-permute-start | bytes 491528 | tf_op jit(solution)/shard_map/ppermute | solution.py:17
  96.8 9.8 %collective-permute-start.30 = (bf16[64,2048]{1,0:T(8,128)(2,1)S(1)}, bf16[64,2048]{1,0:T(8,128)(2,1)S(1)}, u32[]{:S(2)}, u32[]{:S(2)}) collective-permute-start(bf16[64,2048]{1,0:T(8,128)(2,1)S(1)} %get-tuple-element.83), channel_id=1, source_target_pairs={{16,0},{24,8},{0,16},{8,24},{17,1},{25,9},{1,17},{9,25},{18,2},{26... | collective-permute-start | bytes 786440 | tf_op jit(solution)/shard_map/ppermute | solution.py:17
  98.9 6.2 %collective-permute-start.28 = (bf16[64,512]{1,0:T(8,128)(2,1)S(1)}, bf16[64,512]{1,0:T(8,128)(2,1)S(1)}, u32[]{:S(2)}, u32[]{:S(2)}) collective-permute-start(bf16[64,512]{1,0:T(8,128)(2,1)S(1)} %get-tuple-element.81), channel_id=1, source_target_pairs={{24,0},{0,8},{8,16},{16,24},{25,1},{1,9},{9,17},{17,25},{26,2},{2,... | collective-permute-start | bytes 196616 | tf_op jit(solution)/shard_map/ppermute | solution.py:17
  100.9 5.7 %collective-permute-start.29 = (bf16[64,512]{1,0:T(8,128)(2,1)S(1)}, bf16[64,512]{1,0:T(8,128)(2,1)S(1)}, u32[]{:S(2)}, u32[]{:S(2)}) collective-permute-start(bf16[64,512]{1,0:T(8,128)(2,1)S(1)} %get-tuple-element.82), channel_id=1, source_target_pairs={{8,0},{16,8},{24,16},{0,24},{9,1},{17,9},{25,17},{1,25},{10,2},{18... | collective-permute-start | bytes 196616 | tf_op jit(solution)/shard_map/ppermute | solution.py:17

commit v4 on v3

--- a/solution.py
+++ b/solution.py
@@ -309,8 +309,8 @@
 
     where = jnp.stack([l, (z < lax.axis_size("z") // 2)]).astype(jnp.int32)
     band = 8 * WIDE + 1
-    out = assemble(where, arrays, plan, band, share, tile)
-    out = assemble(where, more, more_plan, band, share, tile, out)
+    out = assemble(where, [*arrays, more[0]], [*plan, more_plan[0]], band, share, tile)
+    out = assemble(where, more[1:], more_plan[1:], band, share, tile, out)
     return jnp.transpose(out, (1, 0, 2))
 
 

time: 110 us -> 110 us (level)
  no operation moved by 1% of the time
where the time goes in v4:
time: 110 us; the launch traced here: 108 us
  starting transfers between devices  39.6 us (36%)
  waiting for transfers between devices  39.5 us (36%)
  Pallas kernels  19.3 us (18%)
  local copies, waits for them, and re-layouts  6.64 us (6%)
  matrix products  1.46 us (1%)
  other arithmetic  1.39 us (1%)
    ppermute x29, waiting for transfers between devices, shift(): lax.ppermute(block, axis, [((i + distance) % n, i) for i in range(n)])  39.3 us
    ppermute x29, starting transfers between devices, shift(): lax.ppermute(block, axis, [((i + distance) % n, i) for i in range(n)])  36.5 us
    pallas_call x7, Pallas kernels, call(): pl.pallas_call(kernel, out_shape=out_shape, in_specs=[SMEM] + [VMEM] * (l...  17.8 us
    unnamed x7, local copies, waits for them, and re-layouts  3.69 us
    ppermute x2, starting transfers between devices, across_and_flip(): return lax.ppermute(block, ('l', 'h'), [(i, 3 - i) for i in range(4)])  3.12 us
    dynamic_slice x1, local copies, waits for them, and re-layouts, per_device(): lax.dynamic_slice_in_dim(jacobi_matrix, (1 - h) * 2 * width, 2 * width, 0)  2.8 us
  transfers between devices with their start and end apart: 31, of which 16 were waited for; matrix products, arithmetic and copies ran while one was open for 4% of the time, Pallas kernels for 15%

profile of v4, /device:TPU:6, one launch (start us, length us, event | category | flops | bytes accessed | tf_op | source)
XLA Modules:
  0.0 108.3 jit_solution(12193833775566557759)
XLA Ops:
  0.0 1.2 %compare_select_fusion.refs_4_.refs_3_.refs_8_ = bf16[256,1024]{1,0:T(8,128)(2,1)S(1)} fusion(bf16[256,1024]{1,0:T(8,128)(2,1)} %param.3, s32[1024]{0:T(1024)S(1)} %iota_add_fusion, s32[256]{0:T(256)} %param.5), kind=kLoop, calls=%fused_computation.5 | loop fusion | flops 524288 | bytes 1053696 | tf_op jit(solution)/shard_map/jit(_where)/select_n | solution.py:222
  1.2 5.9 %collective-permute-start.2 = (bf16[256,1024]{1,0:T(8,128)(2,1)S(1)}, bf16[256,1024]{1,0:T(8,128)(2,1)S(1)}, u32[]{:S(2)}, u32[]{:S(2)}) collective-permute-start(bf16[256,1024]{1,0:T(8,128)(2,1)S(1)} %compare_select_fusion.refs_4_.refs_3_.refs_8_), channel_id=1, source_target_pairs={{32,0},{64,32},{96,64},{128,96},{160,128},{192,160},{224,192},{0,2... | collective-permute-start | bytes 1572872 | tf_op jit(solution)/shard_map/ppermute | solution.py:17
  7.2 3.2 %collective-permute-start.1 = (bf16[256,1024]{1,0:T(8,128)(2,1)S(1)}, bf16[256,1024]{1,0:T(8,128)(2,1)S(1)}, u32[]{:S(2)}, u32[]{:S(2)}) collective-permute-start(bf16[256,1024]{1,0:T(8,128)(2,1)S(1)} %compare_select_fusion.refs_4_.refs_3_.refs_8_), channel_id=1, source_target_pairs={{2,0},{0,2},{3,1},{1,3},{6,4},{4,6},{7,5},{5,7},{10,8},{8,10},{11,... | collective-permute-start | bytes 1572872 | tf_op jit(solution)/shard_map/ppermute | solution.py:17
  10.4 2.8 %constant_dynamic-slice_fusion.slab_ref = bf16[2048,1024]{1,0:T(8,128)(2,1)S(1)} fusion(bf16[4096,1024]{1,0:T(8,128)(2,1)} %param.4, s32[]{:T(128)S(6)} %select_n.47), kind=kLoop, calls=%fused_computation.9 | loop fusion | bytes 8388612 | tf_op jit(solution)/shard_map/dynamic_slice | solution.py:233
  13.2 1.8 %copy-done.2 = bf16[4096,1024]{1,0:T(8,128)(2,1)S(1)} copy-done((bf16[4096,1024]{1,0:T(8,128)(2,1)S(1)}, bf16[4096,1024]{1,0:T(8,128)(2,1)}, u32[]{:S(2)}) %copy-start.2) | copy-done | bytes 8388632
  15.0 0.7 fusion.2
  15.8 0.7 fusion.4.total_ref
  16.5 1.9 %collective-permute-done.2.refs_6_.refs_5_.refs_10_ = bf16[256,1024]{1,0:T(8,128)(2,1)S(1)} collective-permute-done((bf16[256,1024]{1,0:T(8,128)(2,1)S(1)}, bf16[256,1024]{1,0:T(8,128)(2,1)S(1)}, u32[]{:S(2)}, u32[]{:S(2)}) %collective-permute-start.2) | collective-permute-done | bytes 524320 | tf_op jit(solution)/shard_map/ppermute | solution.py:17
  18.4 3.7 %collective-permute-done.1.a_ref = bf16[256,1024]{1,0:T(8,128)(2,1)S(1)} collective-permute-done((bf16[256,1024]{1,0:T(8,128)(2,1)S(1)}, bf16[256,1024]{1,0:T(8,128)(2,1)S(1)}, u32[]{:S(2)}, u32[]{:S(2)}) %collective-permute-start.1) | collective-permute-done | bytes 524320 | tf_op jit(solution)/shard_map/ppermute | solution.py:17
  22.1 1.8 %collective-permute-done.3.b_ref = bf16[256,1024]{1,0:T(8,128)(2,1)S(1)} collective-permute-done((bf16[256,1024]{1,0:T(8,128)(2,1)S(1)}, bf16[256,1024]{1,0:T(8,128)(2,1)S(1)}, u32[]{:S(2)}, u32[]{:S(2)}) %collective-permute-start.3) | collective-permute-done | bytes 524320 | tf_op jit(solution)/shard_map/ppermute | solution.py:17
  24.0 1.9 %shard_map.37 = (bf16[128,1024]{1,0:T(8,128)(2,1)S(1)}, bf16[128,1024]{1,0:T(8,128)(2,1)S(1)}) custom-call(s32[2]{0:T(128)S(1)} %pad_add_fusion.1.place_ref, f32[256,1024]{1,0:T(8,128)S(1)} %fusion.4.total_ref, bf16[256,1024]{1,0:T(8,128)(2,1)S(1)} %collective-permute-done.1.a_ref, bf16[256,1024]{1,0:T(8,128)(2,1)S(1)} %collective-permute-done.3.b_ref, ...), custom_call_target="tpu_custom_call" | custom-call | flops 1073741824 | bytes 6291464 | tf_op jit(solution)/shard_map/pallas_call | solution.py:26
  26.4 1.0 collective-permute-start.8
  27.5 0.6 collective-permute-start.7
  28.1 1.5 %collective-permute-start.6 = (bf16[256,1024]{1,0:T(8,128)(2,1)S(1)}, bf16[256,1024]{1,0:T(8,128)(2,1)}, u32[]{:S(2)}, u32[]{:S(2)}) collective-permute-start(bf16[256,1024]{1,0:T(8,128)(2,1)S(1)} %constant_dynamic-update-slice_fusion.refs_0_), channel_id=1, source_target_pairs={{8,0},{16,8},{24,16},{0,24},{9,1},{17,9},{25,17},{1,25},{10,2},{18... | collective-permute-start | bytes 1572872 | tf_op jit(solution)/shard_map/ppermute | solution.py:17
  29.6 1.6 %collective-permute-start.5 = (bf16[256,1024]{1,0:T(8,128)(2,1)S(1)}, bf16[256,1024]{1,0:T(8,128)(2,1)}, u32[]{:S(2)}, u32[]{:S(2)}) collective-permute-start(bf16[256,1024]{1,0:T(8,128)(2,1)S(1)} %constant_dynamic-update-slice_fusion.refs_0_), channel_id=1, source_target_pairs={{4,0},{0,4},{5,1},{1,5},{6,2},{2,6},{7,3},{3,7},{12,8},{8,12},{13,... | collective-permute-start | bytes 1572872 | tf_op jit(solution)/shard_map/ppermute | solution.py:17
  31.2 9.2 %collective-permute-done.8.refs_8_.refs_7_.refs_12_ = bf16[256,1024]{1,0:T(8,128)(2,1)S(1)} collective-permute-done((bf16[256,1024]{1,0:T(8,128)(2,1)S(1)}, bf16[256,1024]{1,0:T(8,128)(2,1)S(1)}, u32[]{:S(2)}, u32[]{:S(2)}) %collective-permute-start.8) | collective-permute-done | bytes 524320 | tf_op jit(solution)/shard_map/ppermute | solution.py:17
  40.4 1.1 %collective-permute-done.7.refs_2_ = bf16[256,1024]{1,0:T(8,128)(2,1)S(1)} collective-permute-done((bf16[256,1024]{1,0:T(8,128)(2,1)S(1)}, bf16[256,1024]{1,0:T(8,128)(2,1)S(1)}, u32[]{:S(2)}, u32[]{:S(2)}) %collective-permute-start.7) | collective-permute-done | bytes 524320 | tf_op jit(solution)/shard_map/ppermute | solution.py:17
  41.5 0.8 copy-done
  42.3 0.7 collective-permute-done.6.refs_1_
  43.1 1.0 collective-permute-start.13
  44.1 0.8 collective-permute-start.11
  44.9 1.6 %collective-permute-start.10 = (bf16[256,1024]{1,0:T(8,128)(2,1)}, bf16[256,1024]{1,0:T(8,128)(2,1)}, u32[]{:S(2)}, u32[]{:S(2)}) collective-permute-start(bf16[256,1024]{1,0:T(8,128)(2,1)} %collective-permute-done.6.refs_1_), channel_id=1, source_target_pairs={{4,0},{0,4},{5,1},{1,5},{6,2},{2,6},{7,3},{3,7},{12,8},{8,12},{13,... | collective-permute-start | bytes 1572872 | tf_op jit(solution)/shard_map/ppermute | solution.py:17
  46.5 2.4 %collective-permute-start.16 = (bf16[256,1024]{1,0:T(8,128)(2,1)}, bf16[256,1024]{1,0:T(8,128)(2,1)}, u32[]{:S(2)}, u32[]{:S(2)}) collective-permute-start(bf16[256,1024]{1,0:T(8,128)(2,1)} %collective-permute-done.5.refs_0_.refs_4_), channel_id=1, source_target_pairs={{24,0},{0,8},{8,16},{16,24},{25,1},{1,9},{9,17},{17,25},{26,2},{2,... | collective-permute-start | bytes 1572872 | tf_op jit(solution)/shard_map/ppermute | solution.py:17
  48.9 7.0 %collective-permute-done.13.refs_10_.refs_9_.refs_14_ = bf16[256,1024]{1,0:T(8,128)(2,1)} collective-permute-done((bf16[256,1024]{1,0:T(8,128)(2,1)S(1)}, bf16[256,1024]{1,0:T(8,128)(2,1)}, u32[]{:S(2)}, u32[]{:S(2)}) %collective-permute-start.13) | collective-permute-done | bytes 524320 | tf_op jit(solution)/shard_map/ppermute | solution.py:17
  56.1 2.0 %collective-permute-done.11.refs_3_ = bf16[256,1024]{1,0:T(8,128)(2,1)} collective-permute-done((bf16[256,1024]{1,0:T(8,128)(2,1)}, bf16[256,1024]{1,0:T(8,128)(2,1)}, u32[]{:S(2)}, u32[]{:S(2)}) %collective-permute-start.11) | collective-permute-done | bytes 524320 | tf_op jit(solution)/shard_map/ppermute | solution.py:17
  58.1 1.0 collective-permute-start.20
  59.1 3.2 %collective-permute-start.19 = (bf16[256,1024]{1,0:T(8,128)(2,1)}, bf16[256,1024]{1,0:T(8,128)(2,1)S(1)}, u32[]{:S(2)}, u32[]{:S(2)}) collective-permute-start(bf16[256,1024]{1,0:T(8,128)(2,1)} %collective-permute-done.16.refs_2_.refs_6_), channel_id=1, source_target_pairs={{24,0},{0,8},{8,16},{16,24},{25,1},{1,9},{9,17},{17,25},{26,2},{2,... | collective-permute-start | bytes 1572872 | tf_op jit(solution)/shard_map/ppermute | solution.py:17
  62.4 1.0 copy-done.1
  63.4 4.2 %shard_map.38 = (bf16[64,3072]{1,0:T(8,128)(2,1)S(1)}, f32[64,3072]{1,0:T(8,128)S(1)}) custom-call(s32[8]{0:T(128)S(1)} %stack.71.late_ref, bf16[256,1024]{1,0:T(8,128)(2,1)S(1)} %constant_dynamic-update-slice_fusion.refs_0_, bf16[256,1024]{1,0:T(8,128)(2,1)} %collective-permute-done.6.refs_1_, bf16[256,1024]{1,0:T(8,128)(2,1)S(1)} %copy-done.1, ...), custom_call_target="tpu_custom_call" | custom-call | flops 12884901888 | bytes 6291488 | tf_op jit(solution)/shard_map/pallas_call | solution.py:26
  67.6 3.0 %collective-permute-start.15 = (bf16[64,3072]{1,0:T(8,128)(2,1)S(1)}, bf16[64,3072]{1,0:T(8,128)(2,1)S(1)}, u32[]{:S(2)}, u32[]{:S(2)}) collective-permute-start(bf16[64,3072]{1,0:T(8,128)(2,1)S(1)} %get-tuple-element.58), channel_id=1, source_target_pairs={{2,0},{0,2},{3,1},{1,3},{6,4},{4,6},{7,5},{5,7},{10,8},{8,10},{11,... | collective-permute-start | bytes 1179656 | tf_op jit(solution)/shard_map/ppermute | solution.py:17
  70.5 3.7 %shard_map.39 = (bf16[64,2304]{1,0:T(8,128)(2,1)S(1)}, bf16[64,2304]{1,0:T(8,128)(2,1)S(1)}) custom-call(s32[8]{0:T(128)S(1)} %stack.71.late_ref, bf16[256,1024]{1,0:T(8,128)(2,1)} %collective-permute-done.5.refs_0_.refs_4_, bf16[256,1024]{1,0:T(8,128)(2,1)} %collective-permute-done.10.refs_1_.refs_5_, ...), custom_call_target="tpu_custom_call" | custom-call | flops 9663676416 | bytes 5767200 | tf_op jit(solution)/shard_map/pallas_call | solution.py:26
  74.5 1.1 collective-permute-start.18
  75.7 0.5 collective-permute-start.21
  76.2 1.0 collective-permute-done.22.refs_18_
  77.6 5.9 %shard_map.40 = (bf16[64,1280]{1,0:T(8,128)(2,1)S(1)}, f32[64,1280]{1,0:T(8,128)S(1)}, bf16[64,1792]{1,0:T(8,128)(2,1)S(1)}, bf16[64,1792]{1,0:T(8,128)(2,1)S(1)}) custom-call(s32[8]{0:T(128)S(1)} %stack.71.late_ref, bf16[256,1024]{1,0:T(8,128)(2,1)S(1)} %constant_dynamic-update-slice_fusion.refs_0_, bf16[256,1024]{1,0:T(8,128)(2,1)} %collective-permute-done.6.refs_1_, ...), custom_call_target="tpu_custom_call" | custom-call | bytes 9437216 | tf_op jit(solution)/shard_map/pallas_call | solution.py:26
  83.5 0.7 collective-permute-done.17.refs_2_
  84.4 1.2 %collective-permute-start.24 = (bf16[64,1792]{1,0:T(8,128)(2,1)S(1)}, bf16[64,1792]{1,0:T(8,128)(2,1)S(1)}, u32[]{:S(2)}, u32[]{:S(2)}) collective-permute-start(bf16[64,1792]{1,0:T(8,128)(2,1)S(1)} %get-tuple-element.72), channel_id=1, source_target_pairs={{4,0},{0,4},{5,1},{1,5},{6,2},{2,6},{7,3},{3,7},{12,8},{8,12},{13,... | collective-permute-start | bytes 688136 | tf_op jit(solution)/shard_map/ppermute | solution.py:17
  85.6 2.1 %collective-permute-start.25 = (bf16[64,1792]{1,0:T(8,128)(2,1)S(1)}, bf16[64,1792]{1,0:T(8,128)(2,1)S(1)}, u32[]{:S(2)}, u32[]{:S(2)}) collective-permute-start(bf16[64,1792]{1,0:T(8,128)(2,1)S(1)} %get-tuple-element.73), channel_id=1, source_target_pairs={{0,6},{2,4},{4,2},{6,0},{1,7},{3,5},{5,3},{7,1},{8,14},{10,12},{12... | collective-permute-start | bytes 688136 | tf_op jit(solution)/shard_map/ppermute | solution.py:21
  87.8 0.4 collective-permute-start.26
  88.2 1.7 %collective-permute-start.27 = (bf16[64,1536]{1,0:T(8,128)(2,1)S(1)}, bf16[64,1536]{1,0:T(8,128)(2,1)S(1)}, u32[]{:S(2)}, u32[]{:S(2)}) collective-permute-start(bf16[64,1536]{1,0:T(8,128)(2,1)S(1)} %get-tuple-element.76), channel_id=1, source_target_pairs={{8,0},{16,8},{24,16},{0,24},{9,1},{17,9},{25,17},{1,25},{10,2},{18... | collective-permute-start | bytes 589832 | tf_op jit(solution)/shard_map/ppermute | solution.py:17
  89.9 0.9 collective-permute-start.23
  90.7 6.0 %collective-permute-done.23.refs_5_ = bf16[64,1280]{1,0:T(8,128)(2,1)S(1)} collective-permute-done((bf16[64,1280]{1,0:T(8,128)(2,1)S(1)}, bf16[64,1280]{1,0:T(8,128)(2,1)S(1)}, u32[]{:S(2)}, u32[]{:S(2)}) %collective-permute-start.23) | collective-permute-done | bytes 163872 | tf_op jit(solution)/shard_map/ppermute | solution.py:17
  96.8 2.0 %collective-permute-start.30 = (bf16[64,2048]{1,0:T(8,128)(2,1)S(1)}, bf16[64,2048]{1,0:T(8,128)(2,1)S(1)}, u32[]{:S(2)}, u32[]{:S(2)}) collective-permute-start(bf16[64,2048]{1,0:T(8,128)(2,1)S(1)} %get-tuple-element.82), channel_id=1, source_target_pairs={{16,0},{24,8},{0,16},{8,24},{17,1},{25,9},{1,17},{9,25},{18,2},{26... | collective-permute-start | bytes 786440 | tf_op jit(solution)/shard_map/ppermute | solution.py:17
  98.9 2.0 %collective-permute-start.28 = (bf16[64,512]{1,0:T(8,128)(2,1)S(1)}, bf16[64,512]{1,0:T(8,128)(2,1)S(1)}, u32[]{:S(2)}, u32[]{:S(2)}) collective-permute-start(bf16[64,512]{1,0:T(8,128)(2,1)S(1)} %get-tuple-element.80), channel_id=1, source_target_pairs={{24,0},{0,8},{8,16},{16,24},{25,1},{1,9},{9,17},{17,25},{26,2},{2,... | collective-permute-start | bytes 196616 | tf_op jit(solution)/shard_map/ppermute | solution.py:17
  101.0 2.0 %shard_map.43.refs_3_ = f32[33,64,256]{2,1,0:T(8,128)} custom-call(s32[2]{0:T(128)S(1)} %pad_add_fusion.place_ref, f32[64,1536]{1,0:T(8,128)S(1)} %get-tuple-element.83.refs_0_, bf16[64,1536]{1,0:T(8,128)(2,1)S(1)} %collective-permute-done.26.refs_1_, bf16[64,1536]{1,0:T(8,128)(2,1)S(1)} %collective-permute-done.27.refs_2_, ...), custom_call_target="tpu_custom_call" | custom-call | bytes 983048 | tf_op jit(solution)/shard_map/pallas_call | solution.py:26
  102.9 2.1 %collective-permute-done.28.refs_0_ = bf16[64,512]{1,0:T(8,128)(2,1)S(1)} collective-permute-done((bf16[64,512]{1,0:T(8,128)(2,1)S(1)}, bf16[64,512]{1,0:T(8,128)(2,1)S(1)}, u32[]{:S(2)}, u32[]{:S(2)}) %collective-permute-start.28) | collective-permute-done | bytes 65568 | tf_op jit(solution)/shard_map/ppermute | solution.py:17
  105.1 1.5 %collective-permute-done.29.refs_1_ = bf16[64,512]{1,0:T(8,128)(2,1)S(1)} collective-permute-done((bf16[64,512]{1,0:T(8,128)(2,1)S(1)}, bf16[64,512]{1,0:T(8,128)(2,1)S(1)}, u32[]{:S(2)}, u32[]{:S(2)}) %collective-permute-start.29) | collective-permute-done | bytes 65568 | tf_op jit(solution)/shard_map/ppermute | solution.py:17
  106.6 1.5 %shard_map.44 = f32[33,64,256]{2,1,0:T(8,128)} custom-call(s32[2]{0:T(128)S(1)} %pad_add_fusion.place_ref, bf16[64,512]{1,0:T(8,128)(2,1)S(1)} %collective-permute-done.28.refs_0_, bf16[64,512]{1,0:T(8,128)(2,1)S(1)} %collective-permute-done.29.refs_1_, bf16[64,2048]{1,0:T(8,128)(2,1)S(1)} %collective-permute-done.30.refs_2_, ...), custom_call_target="tpu_custom_call", output_to_operand_aliasing={{}: (4, {})} | custom-call | tf_op jit(solution)/shard_map/pallas_call | solution.py:200
  (40 shorter events, 2.2 us)
Async XLA Ops:
  1.2 17.1 %collective-permute-start.2 = (bf16[256,1024]{1,0:T(8,128)(2,1)S(1)}, bf16[256,1024]{1,0:T(8,128)(2,1)S(1)}, u32[]{:S(2)}, u32[]{:S(2)}) collective-permute-start(bf16[256,1024]{1,0:T(8,128)(2,1)S(1)} %compare_select_fusion.refs_4_.refs_3_.refs_8_), channel_id=1, source_target_pairs={{32,0},{64,32},{96,64},{128,96},{160,128},{192,160},{224,192},{0,2... | collective-permute-start | bytes 1572872 | tf_op jit(solution)/shard_map/ppermute | solution.py:17
  7.2 14.9 %collective-permute-start.1 = (bf16[256,1024]{1,0:T(8,128)(2,1)S(1)}, bf16[256,1024]{1,0:T(8,128)(2,1)S(1)}, u32[]{:S(2)}, u32[]{:S(2)}) collective-permute-start(bf16[256,1024]{1,0:T(8,128)(2,1)S(1)} %compare_select_fusion.refs_4_.refs_3_.refs_8_), channel_id=1, source_target_pairs={{2,0},{0,2},{3,1},{1,3},{6,4},{4,6},{7,5},{5,7},{10,8},{8,10},{11,... | collective-permute-start | bytes 1572872 | tf_op jit(solution)/shard_map/ppermute | solution.py:17
  10.4 5.4 %collective-permute-start = (bf16[256,1024]{1,0:T(8,128)(2,1)S(1)}, bf16[256,1024]{1,0:T(8,128)(2,1)S(1)}, u32[]{:S(2)}, u32[]{:S(2)}) collective-permute-start(bf16[256,1024]{1,0:T(8,128)(2,1)S(1)} %compare_select_fusion.refs_4_.refs_3_.refs_8_), channel_id=1, source_target_pairs={{1,0},{0,1},{3,2},{2,3},{5,4},{4,5},{7,6},{6,7},{9,8},{8,9},{11,10... | collective-permute-start | bytes 1572872 | tf_op jit(solution)/shard_map/ppermute | solution.py:17
  10.4 4.6 %copy-start.2 = (bf16[4096,1024]{1,0:T(8,128)(2,1)S(1)}, bf16[4096,1024]{1,0:T(8,128)(2,1)}, u32[]{:S(2)}) copy-start(bf16[4096,1024]{1,0:T(8,128)(2,1)} %param.4) | copy-start | bytes 25165828
  22.1 1.9 %collective-permute-start.3 = (bf16[256,1024]{1,0:T(8,128)(2,1)S(1)}, bf16[256,1024]{1,0:T(8,128)(2,1)S(1)}, u32[]{:S(2)}, u32[]{:S(2)}) collective-permute-start(bf16[256,1024]{1,0:T(8,128)(2,1)S(1)} %collective-permute-done.1.a_ref), channel_id=1, source_target_pairs={{1,0},{0,1},{3,2},{2,3},{5,4},{4,5},{7,6},{6,7},{9,8},{8,9},{11,10... | collective-permute-start | bytes 1572872 | tf_op jit(solution)/shard_map/ppermute | solution.py:17
  25.8 1.6 %collective-permute-start.4 = (bf16[128,1024]{1,0:T(8,128)(2,1)S(1)}, bf16[128,1024]{1,0:T(8,128)(2,1)S(1)}, u32[]{:S(2)}, u32[]{:S(2)}) collective-permute-start(bf16[128,1024]{1,0:T(8,128)(2,1)S(1)} %get-tuple-element.50), channel_id=1, source_target_pairs={{1,0},{0,1},{3,2},{2,3},{5,4},{4,5},{7,6},{6,7},{9,8},{8,9},{11,10... | collective-permute-start | bytes 786440 | tf_op jit(solution)/shard_map/ppermute | solution.py:17
  26.1 5.1 %collective-permute-start.9 = (bf16[256,1024]{1,0:T(8,128)(2,1)S(1)}, bf16[256,1024]{1,0:T(8,128)(2,1)S(1)}, u32[]{:S(2)}, u32[]{:S(2)}) collective-permute-start(bf16[256,1024]{1,0:T(8,128)(2,1)S(1)} %collective-permute-done.2.refs_6_.refs_5_.refs_10_), channel_id=1, source_target_pairs={{1,0},{0,1},{3,2},{2,3},{5,4},{4,5},{7,6},{6,7},{9,8},{8,9},{11,10... | collective-permute-start | bytes 1572872 | tf_op jit(solution)/shard_map/ppermute | solution.py:17
  26.4 14.0 %collective-permute-start.8 = (bf16[256,1024]{1,0:T(8,128)(2,1)S(1)}, bf16[256,1024]{1,0:T(8,128)(2,1)S(1)}, u32[]{:S(2)}, u32[]{:S(2)}) collective-permute-start(bf16[256,1024]{1,0:T(8,128)(2,1)S(1)} %collective-permute-done.2.refs_6_.refs_5_.refs_10_), channel_id=1, source_target_pairs={{32,0},{64,32},{96,64},{128,96},{160,128},{192,160},{224,192},{0,2... | collective-permute-start | bytes 1572872 | tf_op jit(solution)/shard_map/ppermute | solution.py:17
  27.5 14.0 %collective-permute-start.7 = (bf16[256,1024]{1,0:T(8,128)(2,1)S(1)}, bf16[256,1024]{1,0:T(8,128)(2,1)S(1)}, u32[]{:S(2)}, u32[]{:S(2)}) collective-permute-start(bf16[256,1024]{1,0:T(8,128)(2,1)S(1)} %constant_dynamic-update-slice_fusion.refs_0_), channel_id=1, source_target_pairs={{24,0},{0,8},{8,16},{16,24},{25,1},{1,9},{9,17},{17,25},{26,2},{2,... | collective-permute-start | bytes 1572872 | tf_op jit(solution)/shard_map/ppermute | solution.py:17
  28.1 15.0 %collective-permute-start.6 = (bf16[256,1024]{1,0:T(8,128)(2,1)S(1)}, bf16[256,1024]{1,0:T(8,128)(2,1)}, u32[]{:S(2)}, u32[]{:S(2)}) collective-permute-start(bf16[256,1024]{1,0:T(8,128)(2,1)S(1)} %constant_dynamic-update-slice_fusion.refs_0_), channel_id=1, source_target_pairs={{8,0},{16,8},{24,16},{0,24},{9,1},{17,9},{25,17},{1,25},{10,2},{18... | collective-permute-start | bytes 1572872 | tf_op jit(solution)/shard_map/ppermute | solution.py:17
  29.6 13.5 %collective-permute-start.5 = (bf16[256,1024]{1,0:T(8,128)(2,1)S(1)}, bf16[256,1024]{1,0:T(8,128)(2,1)}, u32[]{:S(2)}, u32[]{:S(2)}) collective-permute-start(bf16[256,1024]{1,0:T(8,128)(2,1)S(1)} %constant_dynamic-update-slice_fusion.refs_0_), channel_id=1, source_target_pairs={{4,0},{0,4},{5,1},{1,5},{6,2},{2,6},{7,3},{3,7},{12,8},{8,12},{13,... | collective-permute-start | bytes 1572872 | tf_op jit(solution)/shard_map/ppermute | solution.py:17
  41.5 0.8 copy-start
  43.1 12.8 %collective-permute-start.13 = (bf16[256,1024]{1,0:T(8,128)(2,1)S(1)}, bf16[256,1024]{1,0:T(8,128)(2,1)}, u32[]{:S(2)}, u32[]{:S(2)}) collective-permute-start(bf16[256,1024]{1,0:T(8,128)(2,1)S(1)} %collective-permute-done.8.refs_8_.refs_7_.refs_12_), channel_id=1, source_target_pairs={{32,0},{64,32},{96,64},{128,96},{160,128},{192,160},{224,192},{0,2... | collective-permute-start | bytes 1572872 | tf_op jit(solution)/shard_map/ppermute | solution.py:17
  44.1 14.0 %collective-permute-start.11 = (bf16[256,1024]{1,0:T(8,128)(2,1)}, bf16[256,1024]{1,0:T(8,128)(2,1)}, u32[]{:S(2)}, u32[]{:S(2)}) collective-permute-start(bf16[256,1024]{1,0:T(8,128)(2,1)} %collective-permute-done.6.refs_1_), channel_id=1, source_target_pairs={{8,0},{16,8},{24,16},{0,24},{9,1},{17,9},{25,17},{1,25},{10,2},{18... | collective-permute-start | bytes 1572872 | tf_op jit(solution)/shard_map/ppermute | solution.py:17
  44.9 13.2 %collective-permute-start.10 = (bf16[256,1024]{1,0:T(8,128)(2,1)}, bf16[256,1024]{1,0:T(8,128)(2,1)}, u32[]{:S(2)}, u32[]{:S(2)}) collective-permute-start(bf16[256,1024]{1,0:T(8,128)(2,1)} %collective-permute-done.6.refs_1_), channel_id=1, source_target_pairs={{4,0},{0,4},{5,1},{1,5},{6,2},{2,6},{7,3},{3,7},{12,8},{8,12},{13,... | collective-permute-start | bytes 1572872 | tf_op jit(solution)/shard_map/ppermute | solution.py:17
  46.5 12.6 %collective-permute-start.16 = (bf16[256,1024]{1,0:T(8,128)(2,1)}, bf16[256,1024]{1,0:T(8,128)(2,1)}, u32[]{:S(2)}, u32[]{:S(2)}) collective-permute-start(bf16[256,1024]{1,0:T(8,128)(2,1)} %collective-permute-done.5.refs_0_.refs_4_), channel_id=1, source_target_pairs={{24,0},{0,8},{8,16},{16,24},{25,1},{1,9},{9,17},{17,25},{26,2},{2,... | collective-permute-start | bytes 1572872 | tf_op jit(solution)/shard_map/ppermute | solution.py:17
  48.9 13.4 %collective-permute-start.12 = (bf16[256,1024]{1,0:T(8,128)(2,1)S(1)}, bf16[256,1024]{1,0:T(8,128)(2,1)}, u32[]{:S(2)}, u32[]{:S(2)}) collective-permute-start(bf16[256,1024]{1,0:T(8,128)(2,1)S(1)} %collective-permute-done.8.refs_8_.refs_7_.refs_12_), channel_id=1, source_target_pairs={{1,0},{0,1},{3,2},{2,3},{5,4},{4,5},{7,6},{6,7},{9,8},{8,9},{11,10... | collective-permute-start | bytes 1572872 | tf_op jit(solution)/shard_map/ppermute | solution.py:17
  55.9 6.4 %collective-permute-start.14 = (bf16[256,1024]{1,0:T(8,128)(2,1)}, bf16[256,1024]{1,0:T(8,128)(2,1)}, u32[]{:S(2)}, u32[]{:S(2)}) collective-permute-start(bf16[256,1024]{1,0:T(8,128)(2,1)} %collective-permute-done.13.refs_10_.refs_9_.refs_14_), channel_id=1, source_target_pairs={{1,0},{0,1},{3,2},{2,3},{5,4},{4,5},{7,6},{6,7},{9,8},{8,9},{11,10... | collective-permute-start | bytes 1572872 | tf_op jit(solution)/shard_map/ppermute | solution.py:17
  58.1 17.5 %collective-permute-start.20 = (bf16[256,1024]{1,0:T(8,128)(2,1)}, bf16[256,1024]{1,0:T(8,128)(2,1)S(1)}, u32[]{:S(2)}, u32[]{:S(2)}) collective-permute-start(bf16[256,1024]{1,0:T(8,128)(2,1)} %collective-permute-done.13.refs_10_.refs_9_.refs_14_), channel_id=1, source_target_pairs={{32,0},{64,32},{96,64},{128,96},{160,128},{192,160},{224,192},{0,2... | collective-permute-start | bytes 1572872 | tf_op jit(solution)/shard_map/ppermute | solution.py:17
  59.1 16.6 %collective-permute-start.19 = (bf16[256,1024]{1,0:T(8,128)(2,1)}, bf16[256,1024]{1,0:T(8,128)(2,1)S(1)}, u32[]{:S(2)}, u32[]{:S(2)}) collective-permute-start(bf16[256,1024]{1,0:T(8,128)(2,1)} %collective-permute-done.16.refs_2_.refs_6_), channel_id=1, source_target_pairs={{24,0},{0,8},{8,16},{16,24},{25,1},{1,9},{9,17},{17,25},{26,2},{2,... | collective-permute-start | bytes 1572872 | tf_op jit(solution)/shard_map/ppermute | solution.py:17
  62.4 1.0 copy-start.1
  67.6 16.9 %collective-permute-start.15 = (bf16[64,3072]{1,0:T(8,128)(2,1)S(1)}, bf16[64,3072]{1,0:T(8,128)(2,1)S(1)}, u32[]{:S(2)}, u32[]{:S(2)}) collective-permute-start(bf16[64,3072]{1,0:T(8,128)(2,1)S(1)} %get-tuple-element.58), channel_id=1, source_target_pairs={{2,0},{0,2},{3,1},{1,3},{6,4},{4,6},{7,5},{5,7},{10,8},{8,10},{11,... | collective-permute-start | bytes 1179656 | tf_op jit(solution)/shard_map/ppermute | solution.py:17
  74.3 9.9 %collective-permute-start.17 = (bf16[64,2304]{1,0:T(8,128)(2,1)S(1)}, bf16[64,2304]{1,0:T(8,128)(2,1)S(1)}, u32[]{:S(2)}, u32[]{:S(2)}) collective-permute-start(bf16[64,2304]{1,0:T(8,128)(2,1)S(1)} %get-tuple-element.62), channel_id=1, source_target_pairs={{4,0},{0,4},{5,1},{1,5},{6,2},{2,6},{7,3},{3,7},{12,8},{8,12},{13,... | collective-permute-start | bytes 884744 | tf_op jit(solution)/shard_map/ppermute | solution.py:17
  74.5 9.9 %collective-permute-start.18 = (bf16[64,2304]{1,0:T(8,128)(2,1)S(1)}, bf16[64,2304]{1,0:T(8,128)(2,1)S(1)}, u32[]{:S(2)}, u32[]{:S(2)}) collective-permute-start(bf16[64,2304]{1,0:T(8,128)(2,1)S(1)} %get-tuple-element.63), channel_id=1, source_target_pairs={{0,6},{2,4},{4,2},{6,0},{1,7},{3,5},{5,3},{7,1},{8,14},{10,12},{12... | collective-permute-start | bytes 884744 | tf_op jit(solution)/shard_map/ppermute | solution.py:21
  75.6 1.6 %collective-permute-start.22 = (bf16[128,1024]{1,0:T(8,128)(2,1)S(1)}, bf16[128,1024]{1,0:T(8,128)(2,1)S(1)}, u32[]{:S(2)}, u32[]{:S(2)}) collective-permute-start(bf16[128,1024]{1,0:T(8,128)(2,1)S(1)} %get-tuple-element.87), channel_id=1, source_target_pairs={{1,0},{0,1},{3,2},{2,3},{5,4},{4,5},{7,6},{6,7},{9,8},{8,9},{11,10... | collective-permute-start | bytes 786440 | tf_op jit(solution)/shard_map/ppermute | solution.py:17
  75.7 1.9 %collective-permute-start.21 = (bf16[128,1024]{1,0:T(8,128)(2,1)S(1)}, bf16[128,1024]{1,0:T(8,128)(2,1)S(1)}, u32[]{:S(2)}, u32[]{:S(2)}) collective-permute-start(bf16[128,1024]{1,0:T(8,128)(2,1)S(1)} %get-tuple-element.88), channel_id=1, source_target_pairs={{1,0},{0,1},{3,2},{2,3},{5,4},{4,5},{7,6},{6,7},{9,8},{8,9},{11,10... | collective-permute-start | bytes 786440 | tf_op jit(solution)/shard_map/ppermute | solution.py:17
  84.4 12.3 %collective-permute-start.24 = (bf16[64,1792]{1,0:T(8,128)(2,1)S(1)}, bf16[64,1792]{1,0:T(8,128)(2,1)S(1)}, u32[]{:S(2)}, u32[]{:S(2)}) collective-permute-start(bf16[64,1792]{1,0:T(8,128)(2,1)S(1)} %get-tuple-element.72), channel_id=1, source_target_pairs={{4,0},{0,4},{5,1},{1,5},{6,2},{2,6},{7,3},{3,7},{12,8},{8,12},{13,... | collective-permute-start | bytes 688136 | tf_op jit(solution)/shard_map/ppermute | solution.py:17
  85.6 11.1 %collective-permute-start.25 = (bf16[64,1792]{1,0:T(8,128)(2,1)S(1)}, bf16[64,1792]{1,0:T(8,128)(2,1)S(1)}, u32[]{:S(2)}, u32[]{:S(2)}) collective-permute-start(bf16[64,1792]{1,0:T(8,128)(2,1)S(1)} %get-tuple-element.73), channel_id=1, source_target_pairs={{0,6},{2,4},{4,2},{6,0},{1,7},{3,5},{5,3},{7,1},{8,14},{10,12},{12... | collective-permute-start | bytes 688136 | tf_op jit(solution)/shard_map/ppermute | solution.py:21
  87.8 8.9 %collective-permute-start.26 = (bf16[64,1536]{1,0:T(8,128)(2,1)S(1)}, bf16[64,1536]{1,0:T(8,128)(2,1)S(1)}, u32[]{:S(2)}, u32[]{:S(2)}) collective-permute-start(bf16[64,1536]{1,0:T(8,128)(2,1)S(1)} %get-tuple-element.75), channel_id=1, source_target_pairs={{24,0},{0,8},{8,16},{16,24},{25,1},{1,9},{9,17},{17,25},{26,2},{2,... | collective-permute-start | bytes 589832 | tf_op jit(solution)/shard_map/ppermute | solution.py:17
  88.2 8.5 %collective-permute-start.27 = (bf16[64,1536]{1,0:T(8,128)(2,1)S(1)}, bf16[64,1536]{1,0:T(8,128)(2,1)S(1)}, u32[]{:S(2)}, u32[]{:S(2)}) collective-permute-start(bf16[64,1536]{1,0:T(8,128)(2,1)S(1)} %get-tuple-element.76), channel_id=1, source_target_pairs={{8,0},{16,8},{24,16},{0,24},{9,1},{17,9},{25,17},{1,25},{10,2},{18... | collective-permute-start | bytes 589832 | tf_op jit(solution)/shard_map/ppermute | solution.py:17
  89.9 6.8 %collective-permute-start.23 = (bf16[64,1280]{1,0:T(8,128)(2,1)S(1)}, bf16[64,1280]{1,0:T(8,128)(2,1)S(1)}, u32[]{:S(2)}, u32[]{:S(2)}) collective-permute-start(bf16[64,1280]{1,0:T(8,128)(2,1)S(1)} %get-tuple-element.71), channel_id=1, source_target_pairs={{2,0},{0,2},{3,1},{1,3},{6,4},{4,6},{7,5},{5,7},{10,8},{8,10},{11,... | collective-permute-start | bytes 491528 | tf_op jit(solution)/shard_map/ppermute | solution.py:17
  96.8 9.8 %collective-permute-start.30 = (bf16[64,2048]{1,0:T(8,128)(2,1)S(1)}, bf16[64,2048]{1,0:T(8,128)(2,1)S(1)}, u32[]{:S(2)}, u32[]{:S(2)}) collective-permute-start(bf16[64,2048]{1,0:T(8,128)(2,1)S(1)} %get-tuple-element.82), channel_id=1, source_target_pairs={{16,0},{24,8},{0,16},{8,24},{17,1},{25,9},{1,17},{9,25},{18,2},{26... | collective-permute-start | bytes 786440 | tf_op jit(solution)/shard_map/ppermute | solution.py:17
  98.9 6.2 %collective-permute-start.28 = (bf16[64,512]{1,0:T(8,128)(2,1)S(1)}, bf16[64,512]{1,0:T(8,128)(2,1)S(1)}, u32[]{:S(2)}, u32[]{:S(2)}) collective-permute-start(bf16[64,512]{1,0:T(8,128)(2,1)S(1)} %get-tuple-element.80), channel_id=1, source_target_pairs={{24,0},{0,8},{8,16},{16,24},{25,1},{1,9},{9,17},{17,25},{26,2},{2,... | collective-permute-start | bytes 196616 | tf_op jit(solution)/shard_map/ppermute | solution.py:17
  100.9 5.7 %collective-permute-start.29 = (bf16[64,512]{1,0:T(8,128)(2,1)S(1)}, bf16[64,512]{1,0:T(8,128)(2,1)S(1)}, u32[]{:S(2)}, u32[]{:S(2)}) collective-permute-start(bf16[64,512]{1,0:T(8,128)(2,1)S(1)} %get-tuple-element.81), channel_id=1, source_target_pairs={{8,0},{16,8},{24,16},{0,24},{9,1},{17,9},{25,17},{1,25},{10,2},{18... | collective-permute-start | bytes 196616 | tf_op jit(solution)/shard_map/ppermute | solution.py:17

commit v5 on v3

--- a/solution.py
+++ b/solution.py
@@ -92,9 +92,10 @@
                     ]
             for i, step in enumerate((*steps, steps[-1] + 1)):
                 halves = [panel_refs[2 * (step - first) + part] for part in range(2)]
-                held_ref[:rows, i * tile : (i + 1) * tile] = sum(
+                low = half if members[0] == 0 and step not in steps and (0, WIDE) not in same else 0
+                held_ref[low:rows, i * tile : (i + 1) * tile] = sum(
                     lax.dot_general(
-                        stack_ref[part, :rows, :],
+                        stack_ref[part, low:rows, :],
                         half_refs[0][...]
                         if len(half_refs) == 1
                         else jnp.concatenate([ref[...] for ref in half_refs]),

time: 110 us -> 109 us (level)
  no operation moved by 1% of the time
where the time goes in v5:
time: 109 us; the launch traced here: 108 us
  starting transfers between devices  39.6 us (36%)
  waiting for transfers between devices  39.5 us (36%)
  Pallas kernels  19.3 us (18%)
  local copies, waits for them, and re-layouts  6.64 us (6%)
  matrix products  1.46 us (1%)
  other arithmetic  1.39 us (1%)
    ppermute x29, waiting for transfers between devices, shift(): lax.ppermute(block, axis, [((i + distance) % n, i) for i in range(n)])  39.4 us
    ppermute x29, starting transfers between devices, shift(): lax.ppermute(block, axis, [((i + distance) % n, i) for i in range(n)])  36.5 us
    pallas_call x7, Pallas kernels, call(): pl.pallas_call(kernel, out_shape=out_shape, in_specs=[SMEM] + [VMEM] * (l...  17.7 us
    unnamed x7, local copies, waits for them, and re-layouts  3.69 us
    ppermute x2, starting transfers between devices, across_and_flip(): return lax.ppermute(block, ('l', 'h'), [(i, 3 - i) for i in range(4)])  3.12 us
    dynamic_slice x1, local copies, waits for them, and re-layouts, per_device(): lax.dynamic_slice_in_dim(jacobi_matrix, (1 - h) * 2 * width, 2 * width, 0)  2.8 us
  transfers between devices with their start and end apart: 31, of which 16 were waited for; matrix products, arithmetic and copies ran while one was open for 4% of the time, Pallas kernels for 15%

profile of v5, /device:TPU:6, one launch (start us, length us, event | category | flops | bytes accessed | tf_op | source)
XLA Modules:
  0.0 108.3 jit_solution(7997051119123098560)
XLA Ops:
  0.0 1.2 %compare_select_fusion.refs_4_.refs_3_.refs_8_ = bf16[256,1024]{1,0:T(8,128)(2,1)S(1)} fusion(bf16[256,1024]{1,0:T(8,128)(2,1)} %param.3, s32[1024]{0:T(1024)S(1)} %iota_add_fusion, s32[256]{0:T(256)} %param.5), kind=kLoop, calls=%fused_computation.5 | loop fusion | flops 524288 | bytes 1053696 | tf_op jit(solution)/shard_map/jit(_where)/select_n | solution.py:223
  1.2 5.9 %collective-permute-start.2 = (bf16[256,1024]{1,0:T(8,128)(2,1)S(1)}, bf16[256,1024]{1,0:T(8,128)(2,1)S(1)}, u32[]{:S(2)}, u32[]{:S(2)}) collective-permute-start(bf16[256,1024]{1,0:T(8,128)(2,1)S(1)} %compare_select_fusion.refs_4_.refs_3_.refs_8_), channel_id=1, source_target_pairs={{32,0},{64,32},{96,64},{128,96},{160,128},{192,160},{224,192},{0,2... | collective-permute-start | bytes 1572872 | tf_op jit(solution)/shard_map/ppermute | solution.py:17
  7.2 3.2 %collective-permute-start.1 = (bf16[256,1024]{1,0:T(8,128)(2,1)S(1)}, bf16[256,1024]{1,0:T(8,128)(2,1)S(1)}, u32[]{:S(2)}, u32[]{:S(2)}) collective-permute-start(bf16[256,1024]{1,0:T(8,128)(2,1)S(1)} %compare_select_fusion.refs_4_.refs_3_.refs_8_), channel_id=1, source_target_pairs={{2,0},{0,2},{3,1},{1,3},{6,4},{4,6},{7,5},{5,7},{10,8},{8,10},{11,... | collective-permute-start | bytes 1572872 | tf_op jit(solution)/shard_map/ppermute | solution.py:17
  10.4 2.8 %constant_dynamic-slice_fusion.slab_ref = bf16[2048,1024]{1,0:T(8,128)(2,1)S(1)} fusion(bf16[4096,1024]{1,0:T(8,128)(2,1)} %param.4, s32[]{:T(128)S(6)} %select_n.47), kind=kLoop, calls=%fused_computation.9 | loop fusion | bytes 8388612 | tf_op jit(solution)/shard_map/dynamic_slice | solution.py:234
  13.2 1.8 %copy-done.2 = bf16[4096,1024]{1,0:T(8,128)(2,1)S(1)} copy-done((bf16[4096,1024]{1,0:T(8,128)(2,1)S(1)}, bf16[4096,1024]{1,0:T(8,128)(2,1)}, u32[]{:S(2)}) %copy-start.2) | copy-done | bytes 8388632
  15.0 0.7 fusion.2
  15.8 0.7 fusion.4.total_ref
  16.5 1.9 %collective-permute-done.2.refs_6_.refs_5_.refs_10_ = bf16[256,1024]{1,0:T(8,128)(2,1)S(1)} collective-permute-done((bf16[256,1024]{1,0:T(8,128)(2,1)S(1)}, bf16[256,1024]{1,0:T(8,128)(2,1)S(1)}, u32[]{:S(2)}, u32[]{:S(2)}) %collective-permute-start.2) | collective-permute-done | bytes 524320 | tf_op jit(solution)/shard_map/ppermute | solution.py:17
  18.4 3.7 %collective-permute-done.1.a_ref = bf16[256,1024]{1,0:T(8,128)(2,1)S(1)} collective-permute-done((bf16[256,1024]{1,0:T(8,128)(2,1)S(1)}, bf16[256,1024]{1,0:T(8,128)(2,1)S(1)}, u32[]{:S(2)}, u32[]{:S(2)}) %collective-permute-start.1) | collective-permute-done | bytes 524320 | tf_op jit(solution)/shard_map/ppermute | solution.py:17
  22.1 1.8 %collective-permute-done.3.b_ref = bf16[256,1024]{1,0:T(8,128)(2,1)S(1)} collective-permute-done((bf16[256,1024]{1,0:T(8,128)(2,1)S(1)}, bf16[256,1024]{1,0:T(8,128)(2,1)S(1)}, u32[]{:S(2)}, u32[]{:S(2)}) %collective-permute-start.3) | collective-permute-done | bytes 524320 | tf_op jit(solution)/shard_map/ppermute | solution.py:17
  24.0 1.9 %shard_map.37 = (bf16[128,1024]{1,0:T(8,128)(2,1)S(1)}, bf16[128,1024]{1,0:T(8,128)(2,1)S(1)}) custom-call(s32[2]{0:T(128)S(1)} %pad_add_fusion.1.place_ref, f32[256,1024]{1,0:T(8,128)S(1)} %fusion.4.total_ref, bf16[256,1024]{1,0:T(8,128)(2,1)S(1)} %collective-permute-done.1.a_ref, bf16[256,1024]{1,0:T(8,128)(2,1)S(1)} %collective-permute-done.3.b_ref, ...), custom_call_target="tpu_custom_call" | custom-call | flops 1073741824 | bytes 6291464 | tf_op jit(solution)/shard_map/pallas_call | solution.py:26
  26.4 1.0 collective-permute-start.8
  27.5 0.6 collective-permute-start.7
  28.1 1.5 %collective-permute-start.6 = (bf16[256,1024]{1,0:T(8,128)(2,1)S(1)}, bf16[256,1024]{1,0:T(8,128)(2,1)}, u32[]{:S(2)}, u32[]{:S(2)}) collective-permute-start(bf16[256,1024]{1,0:T(8,128)(2,1)S(1)} %constant_dynamic-update-slice_fusion.refs_0_), channel_id=1, source_target_pairs={{8,0},{16,8},{24,16},{0,24},{9,1},{17,9},{25,17},{1,25},{10,2},{18... | collective-permute-start | bytes 1572872 | tf_op jit(solution)/shard_map/ppermute | solution.py:17
  29.6 1.6 %collective-permute-start.5 = (bf16[256,1024]{1,0:T(8,128)(2,1)S(1)}, bf16[256,1024]{1,0:T(8,128)(2,1)}, u32[]{:S(2)}, u32[]{:S(2)}) collective-permute-start(bf16[256,1024]{1,0:T(8,128)(2,1)S(1)} %constant_dynamic-update-slice_fusion.refs_0_), channel_id=1, source_target_pairs={{4,0},{0,4},{5,1},{1,5},{6,2},{2,6},{7,3},{3,7},{12,8},{8,12},{13,... | collective-permute-start | bytes 1572872 | tf_op jit(solution)/shard_map/ppermute | solution.py:17
  31.2 9.2 %collective-permute-done.8.refs_8_.refs_7_.refs_12_ = bf16[256,1024]{1,0:T(8,128)(2,1)S(1)} collective-permute-done((bf16[256,1024]{1,0:T(8,128)(2,1)S(1)}, bf16[256,1024]{1,0:T(8,128)(2,1)S(1)}, u32[]{:S(2)}, u32[]{:S(2)}) %collective-permute-start.8) | collective-permute-done | bytes 524320 | tf_op jit(solution)/shard_map/ppermute | solution.py:17
  40.4 1.1 %collective-permute-done.7.refs_2_ = bf16[256,1024]{1,0:T(8,128)(2,1)S(1)} collective-permute-done((bf16[256,1024]{1,0:T(8,128)(2,1)S(1)}, bf16[256,1024]{1,0:T(8,128)(2,1)S(1)}, u32[]{:S(2)}, u32[]{:S(2)}) %collective-permute-start.7) | collective-permute-done | bytes 524320 | tf_op jit(solution)/shard_map/ppermute | solution.py:17
  41.5 0.8 copy-done
  42.3 0.7 collective-permute-done.6.refs_1_
  43.1 1.0 collective-permute-start.13
  44.1 0.8 collective-permute-start.11
  44.9 1.6 %collective-permute-start.10 = (bf16[256,1024]{1,0:T(8,128)(2,1)}, bf16[256,1024]{1,0:T(8,128)(2,1)}, u32[]{:S(2)}, u32[]{:S(2)}) collective-permute-start(bf16[256,1024]{1,0:T(8,128)(2,1)} %collective-permute-done.6.refs_1_), channel_id=1, source_target_pairs={{4,0},{0,4},{5,1},{1,5},{6,2},{2,6},{7,3},{3,7},{12,8},{8,12},{13,... | collective-permute-start | bytes 1572872 | tf_op jit(solution)/shard_map/ppermute | solution.py:17
  46.5 2.4 %collective-permute-start.16 = (bf16[256,1024]{1,0:T(8,128)(2,1)}, bf16[256,1024]{1,0:T(8,128)(2,1)}, u32[]{:S(2)}, u32[]{:S(2)}) collective-permute-start(bf16[256,1024]{1,0:T(8,128)(2,1)} %collective-permute-done.5.refs_0_.refs_4_), channel_id=1, source_target_pairs={{24,0},{0,8},{8,16},{16,24},{25,1},{1,9},{9,17},{17,25},{26,2},{2,... | collective-permute-start | bytes 1572872 | tf_op jit(solution)/shard_map/ppermute | solution.py:17
  48.9 7.0 %collective-permute-done.13.refs_10_.refs_9_.refs_14_ = bf16[256,1024]{1,0:T(8,128)(2,1)} collective-permute-done((bf16[256,1024]{1,0:T(8,128)(2,1)S(1)}, bf16[256,1024]{1,0:T(8,128)(2,1)}, u32[]{:S(2)}, u32[]{:S(2)}) %collective-permute-start.13) | collective-permute-done | bytes 524320 | tf_op jit(solution)/shard_map/ppermute | solution.py:17
  56.1 2.0 %collective-permute-done.11.refs_3_ = bf16[256,1024]{1,0:T(8,128)(2,1)} collective-permute-done((bf16[256,1024]{1,0:T(8,128)(2,1)}, bf16[256,1024]{1,0:T(8,128)(2,1)}, u32[]{:S(2)}, u32[]{:S(2)}) %collective-permute-start.11) | collective-permute-done | bytes 524320 | tf_op jit(solution)/shard_map/ppermute | solution.py:17
  58.1 1.0 collective-permute-start.20
  59.1 3.2 %collective-permute-start.19 = (bf16[256,1024]{1,0:T(8,128)(2,1)}, bf16[256,1024]{1,0:T(8,128)(2,1)S(1)}, u32[]{:S(2)}, u32[]{:S(2)}) collective-permute-start(bf16[256,1024]{1,0:T(8,128)(2,1)} %collective-permute-done.16.refs_2_.refs_6_), channel_id=1, source_target_pairs={{24,0},{0,8},{8,16},{16,24},{25,1},{1,9},{9,17},{17,25},{26,2},{2,... | collective-permute-start | bytes 1572872 | tf_op jit(solution)/shard_map/ppermute | solution.py:17
  62.4 1.0 copy-done.1
  63.4 4.0 %shard_map.38 = (bf16[64,3072]{1,0:T(8,128)(2,1)S(1)}, f32[64,3072]{1,0:T(8,128)S(1)}) custom-call(s32[8]{0:T(128)S(1)} %stack.71.late_ref, bf16[256,1024]{1,0:T(8,128)(2,1)S(1)} %constant_dynamic-update-slice_fusion.refs_0_, bf16[256,1024]{1,0:T(8,128)(2,1)} %collective-permute-done.6.refs_1_, bf16[256,1024]{1,0:T(8,128)(2,1)S(1)} %copy-done.1, ...), custom_call_target="tpu_custom_call" | custom-call | flops 12884901888 | bytes 6291488 | tf_op jit(solution)/shard_map/pallas_call | solution.py:26
  67.4 3.0 %collective-permute-start.15 = (bf16[64,3072]{1,0:T(8,128)(2,1)S(1)}, bf16[64,3072]{1,0:T(8,128)(2,1)S(1)}, u32[]{:S(2)}, u32[]{:S(2)}) collective-permute-start(bf16[64,3072]{1,0:T(8,128)(2,1)S(1)} %get-tuple-element.58), channel_id=1, source_target_pairs={{2,0},{0,2},{3,1},{1,3},{6,4},{4,6},{7,5},{5,7},{10,8},{8,10},{11,... | collective-permute-start | bytes 1179656 | tf_op jit(solution)/shard_map/ppermute | solution.py:17
  70.4 3.7 %shard_map.39 = (bf16[64,2304]{1,0:T(8,128)(2,1)S(1)}, bf16[64,2304]{1,0:T(8,128)(2,1)S(1)}) custom-call(s32[8]{0:T(128)S(1)} %stack.71.late_ref, bf16[256,1024]{1,0:T(8,128)(2,1)} %collective-permute-done.5.refs_0_.refs_4_, bf16[256,1024]{1,0:T(8,128)(2,1)} %collective-permute-done.10.refs_1_.refs_5_, ...), custom_call_target="tpu_custom_call" | custom-call | flops 9663676416 | bytes 5767200 | tf_op jit(solution)/shard_map/pallas_call | solution.py:26
  74.4 1.1 collective-permute-start.18
  75.6 0.5 collective-permute-start.21
  76.1 1.0 collective-permute-done.22.refs_18_
  77.5 5.9 %shard_map.40 = (bf16[64,1280]{1,0:T(8,128)(2,1)S(1)}, f32[64,1280]{1,0:T(8,128)S(1)}, bf16[64,1792]{1,0:T(8,128)(2,1)S(1)}, bf16[64,1792]{1,0:T(8,128)(2,1)S(1)}) custom-call(s32[8]{0:T(128)S(1)} %stack.71.late_ref, bf16[256,1024]{1,0:T(8,128)(2,1)S(1)} %constant_dynamic-update-slice_fusion.refs_0_, bf16[256,1024]{1,0:T(8,128)(2,1)} %collective-permute-done.6.refs_1_, ...), custom_call_target="tpu_custom_call" | custom-call | bytes 9437216 | tf_op jit(solution)/shard_map/pallas_call | solution.py:26
  83.4 0.7 collective-permute-done.17.refs_2_
  84.3 1.2 %collective-permute-start.24 = (bf16[64,1792]{1,0:T(8,128)(2,1)S(1)}, bf16[64,1792]{1,0:T(8,128)(2,1)S(1)}, u32[]{:S(2)}, u32[]{:S(2)}) collective-permute-start(bf16[64,1792]{1,0:T(8,128)(2,1)S(1)} %get-tuple-element.72), channel_id=1, source_target_pairs={{4,0},{0,4},{5,1},{1,5},{6,2},{2,6},{7,3},{3,7},{12,8},{8,12},{13,... | collective-permute-start | bytes 688136 | tf_op jit(solution)/shard_map/ppermute | solution.py:17
  85.5 2.1 %collective-permute-start.25 = (bf16[64,1792]{1,0:T(8,128)(2,1)S(1)}, bf16[64,1792]{1,0:T(8,128)(2,1)S(1)}, u32[]{:S(2)}, u32[]{:S(2)}) collective-permute-start(bf16[64,1792]{1,0:T(8,128)(2,1)S(1)} %get-tuple-element.73), channel_id=1, source_target_pairs={{0,6},{2,4},{4,2},{6,0},{1,7},{3,5},{5,3},{7,1},{8,14},{10,12},{12... | collective-permute-start | bytes 688136 | tf_op jit(solution)/shard_map/ppermute | solution.py:21
  87.6 0.6 collective-permute-start.26
  88.3 1.7 %collective-permute-start.27 = (bf16[64,1536]{1,0:T(8,128)(2,1)S(1)}, bf16[64,1536]{1,0:T(8,128)(2,1)S(1)}, u32[]{:S(2)}, u32[]{:S(2)}) collective-permute-start(bf16[64,1536]{1,0:T(8,128)(2,1)S(1)} %get-tuple-element.76), channel_id=1, source_target_pairs={{8,0},{16,8},{24,16},{0,24},{9,1},{17,9},{25,17},{1,25},{10,2},{18... | collective-permute-start | bytes 589832 | tf_op jit(solution)/shard_map/ppermute | solution.py:17
  90.0 0.9 collective-permute-start.23
  90.8 6.0 %collective-permute-done.23.refs_5_ = bf16[64,1280]{1,0:T(8,128)(2,1)S(1)} collective-permute-done((bf16[64,1280]{1,0:T(8,128)(2,1)S(1)}, bf16[64,1280]{1,0:T(8,128)(2,1)S(1)}, u32[]{:S(2)}, u32[]{:S(2)}) %collective-permute-start.23) | collective-permute-done | bytes 163872 | tf_op jit(solution)/shard_map/ppermute | solution.py:17
  96.9 1.8 %collective-permute-start.30 = (bf16[64,2048]{1,0:T(8,128)(2,1)S(1)}, bf16[64,2048]{1,0:T(8,128)(2,1)S(1)}, u32[]{:S(2)}, u32[]{:S(2)}) collective-permute-start(bf16[64,2048]{1,0:T(8,128)(2,1)S(1)} %get-tuple-element.83), channel_id=1, source_target_pairs={{16,0},{24,8},{0,16},{8,24},{17,1},{25,9},{1,17},{9,25},{18,2},{26... | collective-permute-start | bytes 786440 | tf_op jit(solution)/shard_map/ppermute | solution.py:17
  98.7 2.0 %collective-permute-start.28 = (bf16[64,512]{1,0:T(8,128)(2,1)S(1)}, bf16[64,512]{1,0:T(8,128)(2,1)S(1)}, u32[]{:S(2)}, u32[]{:S(2)}) collective-permute-start(bf16[64,512]{1,0:T(8,128)(2,1)S(1)} %get-tuple-element.81), channel_id=1, source_target_pairs={{24,0},{0,8},{8,16},{16,24},{25,1},{1,9},{9,17},{17,25},{26,2},{2,... | collective-permute-start | bytes 196616 | tf_op jit(solution)/shard_map/ppermute | solution.py:17
  100.8 2.0 %shard_map.43.refs_4_ = f32[33,64,256]{2,1,0:T(8,128)} custom-call(s32[2]{0:T(128)S(1)} %pad_add_fusion.place_ref, f32[64,1536]{1,0:T(8,128)S(1)} %get-tuple-element.84.refs_0_, bf16[64,1536]{1,0:T(8,128)(2,1)S(1)} %collective-permute-done.26.refs_1_, bf16[64,1536]{1,0:T(8,128)(2,1)S(1)} %collective-permute-done.27.refs_2_), custom_call_target="tpu_custom_call" | custom-call | bytes 786440 | tf_op jit(solution)/shard_map/pallas_call | solution.py:26
  102.8 1.9 %collective-permute-done.28.refs_1_ = bf16[64,512]{1,0:T(8,128)(2,1)S(1)} collective-permute-done((bf16[64,512]{1,0:T(8,128)(2,1)S(1)}, bf16[64,512]{1,0:T(8,128)(2,1)S(1)}, u32[]{:S(2)}, u32[]{:S(2)}) %collective-permute-start.28) | collective-permute-done | bytes 65568 | tf_op jit(solution)/shard_map/ppermute | solution.py:17
  104.7 1.8 %collective-permute-done.29.refs_2_ = bf16[64,512]{1,0:T(8,128)(2,1)S(1)} collective-permute-done((bf16[64,512]{1,0:T(8,128)(2,1)S(1)}, bf16[64,512]{1,0:T(8,128)(2,1)S(1)}, u32[]{:S(2)}, u32[]{:S(2)}) %collective-permute-start.29) | collective-permute-done | bytes 65568 | tf_op jit(solution)/shard_map/ppermute | solution.py:17
  106.5 1.6 %shard_map.44 = f32[33,64,256]{2,1,0:T(8,128)} custom-call(s32[2]{0:T(128)S(1)} %pad_add_fusion.place_ref, f32[64,768]{1,0:T(8,128)S(1)} %get-tuple-element.80.refs_0_, bf16[64,512]{1,0:T(8,128)(2,1)S(1)} %collective-permute-done.28.refs_1_, bf16[64,512]{1,0:T(8,128)(2,1)S(1)} %collective-permute-done.29.refs_2_, ...), custom_call_target="tpu_custom_call", output_to_operand_aliasing={{}: (5, {})} | custom-call | tf_op jit(solution)/shard_map/pallas_call | solution.py:201
  (40 shorter events, 2.2 us)
Async XLA Ops:
  1.2 17.1 %collective-permute-start.2 = (bf16[256,1024]{1,0:T(8,128)(2,1)S(1)}, bf16[256,1024]{1,0:T(8,128)(2,1)S(1)}, u32[]{:S(2)}, u32[]{:S(2)}) collective-permute-start(bf16[256,1024]{1,0:T(8,128)(2,1)S(1)} %compare_select_fusion.refs_4_.refs_3_.refs_8_), channel_id=1, source_target_pairs={{32,0},{64,32},{96,64},{128,96},{160,128},{192,160},{224,192},{0,2... | collective-permute-start | bytes 1572872 | tf_op jit(solution)/shard_map/ppermute | solution.py:17
  7.2 14.9 %collective-permute-start.1 = (bf16[256,1024]{1,0:T(8,128)(2,1)S(1)}, bf16[256,1024]{1,0:T(8,128)(2,1)S(1)}, u32[]{:S(2)}, u32[]{:S(2)}) collective-permute-start(bf16[256,1024]{1,0:T(8,128)(2,1)S(1)} %compare_select_fusion.refs_4_.refs_3_.refs_8_), channel_id=1, source_target_pairs={{2,0},{0,2},{3,1},{1,3},{6,4},{4,6},{7,5},{5,7},{10,8},{8,10},{11,... | collective-permute-start | bytes 1572872 | tf_op jit(solution)/shard_map/ppermute | solution.py:17
  10.4 5.4 %collective-permute-start = (bf16[256,1024]{1,0:T(8,128)(2,1)S(1)}, bf16[256,1024]{1,0:T(8,128)(2,1)S(1)}, u32[]{:S(2)}, u32[]{:S(2)}) collective-permute-start(bf16[256,1024]{1,0:T(8,128)(2,1)S(1)} %compare_select_fusion.refs_4_.refs_3_.refs_8_), channel_id=1, source_target_pairs={{1,0},{0,1},{3,2},{2,3},{5,4},{4,5},{7,6},{6,7},{9,8},{8,9},{11,10... | collective-permute-start | bytes 1572872 | tf_op jit(solution)/shard_map/ppermute | solution.py:17
  10.4 4.6 %copy-start.2 = (bf16[4096,1024]{1,0:T(8,128)(2,1)S(1)}, bf16[4096,1024]{1,0:T(8,128)(2,1)}, u32[]{:S(2)}) copy-start(bf16[4096,1024]{1,0:T(8,128)(2,1)} %param.4) | copy-start | bytes 25165828
  22.1 1.9 %collective-permute-start.3 = (bf16[256,1024]{1,0:T(8,128)(2,1)S(1)}, bf16[256,1024]{1,0:T(8,128)(2,1)S(1)}, u32[]{:S(2)}, u32[]{:S(2)}) collective-permute-start(bf16[256,1024]{1,0:T(8,128)(2,1)S(1)} %collective-permute-done.1.a_ref), channel_id=1, source_target_pairs={{1,0},{0,1},{3,2},{2,3},{5,4},{4,5},{7,6},{6,7},{9,8},{8,9},{11,10... | collective-permute-start | bytes 1572872 | tf_op jit(solution)/shard_map/ppermute | solution.py:17
  25.8 1.6 %collective-permute-start.4 = (bf16[128,1024]{1,0:T(8,128)(2,1)S(1)}, bf16[128,1024]{1,0:T(8,128)(2,1)S(1)}, u32[]{:S(2)}, u32[]{:S(2)}) collective-permute-start(bf16[128,1024]{1,0:T(8,128)(2,1)S(1)} %get-tuple-element.50), channel_id=1, source_target_pairs={{1,0},{0,1},{3,2},{2,3},{5,4},{4,5},{7,6},{6,7},{9,8},{8,9},{11,10... | collective-permute-start | bytes 786440 | tf_op jit(solution)/shard_map/ppermute | solution.py:17
  26.1 5.1 %collective-permute-start.9 = (bf16[256,1024]{1,0:T(8,128)(2,1)S(1)}, bf16[256,1024]{1,0:T(8,128)(2,1)S(1)}, u32[]{:S(2)}, u32[]{:S(2)}) collective-permute-start(bf16[256,1024]{1,0:T(8,128)(2,1)S(1)} %collective-permute-done.2.refs_6_.refs_5_.refs_10_), channel_id=1, source_target_pairs={{1,0},{0,1},{3,2},{2,3},{5,4},{4,5},{7,6},{6,7},{9,8},{8,9},{11,10... | collective-permute-start | bytes 1572872 | tf_op jit(solution)/shard_map/ppermute | solution.py:17
  26.4 14.0 %collective-permute-start.8 = (bf16[256,1024]{1,0:T(8,128)(2,1)S(1)}, bf16[256,1024]{1,0:T(8,128)(2,1)S(1)}, u32[]{:S(2)}, u32[]{:S(2)}) collective-permute-start(bf16[256,1024]{1,0:T(8,128)(2,1)S(1)} %collective-permute-done.2.refs_6_.refs_5_.refs_10_), channel_id=1, source_target_pairs={{32,0},{64,32},{96,64},{128,96},{160,128},{192,160},{224,192},{0,2... | collective-permute-start | bytes 1572872 | tf_op jit(solution)/shard_map/ppermute | solution.py:17
  27.5 14.0 %collective-permute-start.7 = (bf16[256,1024]{1,0:T(8,128)(2,1)S(1)}, bf16[256,1024]{1,0:T(8,128)(2,1)S(1)}, u32[]{:S(2)}, u32[]{:S(2)}) collective-permute-start(bf16[256,1024]{1,0:T(8,128)(2,1)S(1)} %constant_dynamic-update-slice_fusion.refs_0_), channel_id=1, source_target_pairs={{24,0},{0,8},{8,16},{16,24},{25,1},{1,9},{9,17},{17,25},{26,2},{2,... | collective-permute-start | bytes 1572872 | tf_op jit(solution)/shard_map/ppermute | solution.py:17
  28.1 15.0 %collective-permute-start.6 = (bf16[256,1024]{1,0:T(8,128)(2,1)S(1)}, bf16[256,1024]{1,0:T(8,128)(2,1)}, u32[]{:S(2)}, u32[]{:S(2)}) collective-permute-start(bf16[256,1024]{1,0:T(8,128)(2,1)S(1)} %constant_dynamic-update-slice_fusion.refs_0_), channel_id=1, source_target_pairs={{8,0},{16,8},{24,16},{0,24},{9,1},{17,9},{25,17},{1,25},{10,2},{18... | collective-permute-start | bytes 1572872 | tf_op jit(solution)/shard_map/ppermute | solution.py:17
  29.6 13.5 %collective-permute-start.5 = (bf16[256,1024]{1,0:T(8,128)(2,1)S(1)}, bf16[256,1024]{1,0:T(8,128)(2,1)}, u32[]{:S(2)}, u32[]{:S(2)}) collective-permute-start(bf16[256,1024]{1,0:T(8,128)(2,1)S(1)} %constant_dynamic-update-slice_fusion.refs_0_), channel_id=1, source_target_pairs={{4,0},{0,4},{5,1},{1,5},{6,2},{2,6},{7,3},{3,7},{12,8},{8,12},{13,... | collective-permute-start | bytes 1572872 | tf_op jit(solution)/shard_map/ppermute | solution.py:17
  41.5 0.8 copy-start
  43.1 12.8 %collective-permute-start.13 = (bf16[256,1024]{1,0:T(8,128)(2,1)S(1)}, bf16[256,1024]{1,0:T(8,128)(2,1)}, u32[]{:S(2)}, u32[]{:S(2)}) collective-permute-start(bf16[256,1024]{1,0:T(8,128)(2,1)S(1)} %collective-permute-done.8.refs_8_.refs_7_.refs_12_), channel_id=1, source_target_pairs={{32,0},{64,32},{96,64},{128,96},{160,128},{192,160},{224,192},{0,2... | collective-permute-start | bytes 1572872 | tf_op jit(solution)/shard_map/ppermute | solution.py:17
  44.1 14.0 %collective-permute-start.11 = (bf16[256,1024]{1,0:T(8,128)(2,1)}, bf16[256,1024]{1,0:T(8,128)(2,1)}, u32[]{:S(2)}, u32[]{:S(2)}) collective-permute-start(bf16[256,1024]{1,0:T(8,128)(2,1)} %collective-permute-done.6.refs_1_), channel_id=1, source_target_pairs={{8,0},{16,8},{24,16},{0,24},{9,1},{17,9},{25,17},{1,25},{10,2},{18... | collective-permute-start | bytes 1572872 | tf_op jit(solution)/shard_map/ppermute | solution.py:17
  44.9 13.2 %collective-permute-start.10 = (bf16[256,1024]{1,0:T(8,128)(2,1)}, bf16[256,1024]{1,0:T(8,128)(2,1)}, u32[]{:S(2)}, u32[]{:S(2)}) collective-permute-start(bf16[256,1024]{1,0:T(8,128)(2,1)} %collective-permute-done.6.refs_1_), channel_id=1, source_target_pairs={{4,0},{0,4},{5,1},{1,5},{6,2},{2,6},{7,3},{3,7},{12,8},{8,12},{13,... | collective-permute-start | bytes 1572872 | tf_op jit(solution)/shard_map/ppermute | solution.py:17
  46.5 12.6 %collective-permute-start.16 = (bf16[256,1024]{1,0:T(8,128)(2,1)}, bf16[256,1024]{1,0:T(8,128)(2,1)}, u32[]{:S(2)}, u32[]{:S(2)}) collective-permute-start(bf16[256,1024]{1,0:T(8,128)(2,1)} %collective-permute-done.5.refs_0_.refs_4_), channel_id=1, source_target_pairs={{24,0},{0,8},{8,16},{16,24},{25,1},{1,9},{9,17},{17,25},{26,2},{2,... | collective-permute-start | bytes 1572872 | tf_op jit(solution)/shard_map/ppermute | solution.py:17
  48.9 13.4 %collective-permute-start.12 = (bf16[256,1024]{1,0:T(8,128)(2,1)S(1)}, bf16[256,1024]{1,0:T(8,128)(2,1)}, u32[]{:S(2)}, u32[]{:S(2)}) collective-permute-start(bf16[256,1024]{1,0:T(8,128)(2,1)S(1)} %collective-permute-done.8.refs_8_.refs_7_.refs_12_), channel_id=1, source_target_pairs={{1,0},{0,1},{3,2},{2,3},{5,4},{4,5},{7,6},{6,7},{9,8},{8,9},{11,10... | collective-permute-start | bytes 1572872 | tf_op jit(solution)/shard_map/ppermute | solution.py:17
  55.9 6.4 %collective-permute-start.14 = (bf16[256,1024]{1,0:T(8,128)(2,1)}, bf16[256,1024]{1,0:T(8,128)(2,1)}, u32[]{:S(2)}, u32[]{:S(2)}) collective-permute-start(bf16[256,1024]{1,0:T(8,128)(2,1)} %collective-permute-done.13.refs_10_.refs_9_.refs_14_), channel_id=1, source_target_pairs={{1,0},{0,1},{3,2},{2,3},{5,4},{4,5},{7,6},{6,7},{9,8},{8,9},{11,10... | collective-permute-start | bytes 1572872 | tf_op jit(solution)/shard_map/ppermute | solution.py:17
  58.1 17.4 %collective-permute-start.20 = (bf16[256,1024]{1,0:T(8,128)(2,1)}, bf16[256,1024]{1,0:T(8,128)(2,1)S(1)}, u32[]{:S(2)}, u32[]{:S(2)}) collective-permute-start(bf16[256,1024]{1,0:T(8,128)(2,1)} %collective-permute-done.13.refs_10_.refs_9_.refs_14_), channel_id=1, source_target_pairs={{32,0},{64,32},{96,64},{128,96},{160,128},{192,160},{224,192},{0,2... | collective-permute-start | bytes 1572872 | tf_op jit(solution)/shard_map/ppermute | solution.py:17
  59.1 16.5 %collective-permute-start.19 = (bf16[256,1024]{1,0:T(8,128)(2,1)}, bf16[256,1024]{1,0:T(8,128)(2,1)S(1)}, u32[]{:S(2)}, u32[]{:S(2)}) collective-permute-start(bf16[256,1024]{1,0:T(8,128)(2,1)} %collective-permute-done.16.refs_2_.refs_6_), channel_id=1, source_target_pairs={{24,0},{0,8},{8,16},{16,24},{25,1},{1,9},{9,17},{17,25},{26,2},{2,... | collective-permute-start | bytes 1572872 | tf_op jit(solution)/shard_map/ppermute | solution.py:17
  62.4 1.0 copy-start.1
  67.4 16.9 %collective-permute-start.15 = (bf16[64,3072]{1,0:T(8,128)(2,1)S(1)}, bf16[64,3072]{1,0:T(8,128)(2,1)S(1)}, u32[]{:S(2)}, u32[]{:S(2)}) collective-permute-start(bf16[64,3072]{1,0:T(8,128)(2,1)S(1)} %get-tuple-element.58), channel_id=1, source_target_pairs={{2,0},{0,2},{3,1},{1,3},{6,4},{4,6},{7,5},{5,7},{10,8},{8,10},{11,... | collective-permute-start | bytes 1179656 | tf_op jit(solution)/shard_map/ppermute | solution.py:17
  74.2 9.9 %collective-permute-start.17 = (bf16[64,2304]{1,0:T(8,128)(2,1)S(1)}, bf16[64,2304]{1,0:T(8,128)(2,1)S(1)}, u32[]{:S(2)}, u32[]{:S(2)}) collective-permute-start(bf16[64,2304]{1,0:T(8,128)(2,1)S(1)} %get-tuple-element.62), channel_id=1, source_target_pairs={{4,0},{0,4},{5,1},{1,5},{6,2},{2,6},{7,3},{3,7},{12,8},{8,12},{13,... | collective-permute-start | bytes 884744 | tf_op jit(solution)/shard_map/ppermute | solution.py:17
  74.4 9.9 %collective-permute-start.18 = (bf16[64,2304]{1,0:T(8,128)(2,1)S(1)}, bf16[64,2304]{1,0:T(8,128)(2,1)S(1)}, u32[]{:S(2)}, u32[]{:S(2)}) collective-permute-start(bf16[64,2304]{1,0:T(8,128)(2,1)S(1)} %get-tuple-element.63), channel_id=1, source_target_pairs={{0,6},{2,4},{4,2},{6,0},{1,7},{3,5},{5,3},{7,1},{8,14},{10,12},{12... | collective-permute-start | bytes 884744 | tf_op jit(solution)/shard_map/ppermute | solution.py:21
  75.5 1.6 %collective-permute-start.22 = (bf16[128,1024]{1,0:T(8,128)(2,1)S(1)}, bf16[128,1024]{1,0:T(8,128)(2,1)S(1)}, u32[]{:S(2)}, u32[]{:S(2)}) collective-permute-start(bf16[128,1024]{1,0:T(8,128)(2,1)S(1)} %get-tuple-element.87), channel_id=1, source_target_pairs={{1,0},{0,1},{3,2},{2,3},{5,4},{4,5},{7,6},{6,7},{9,8},{8,9},{11,10... | collective-permute-start | bytes 786440 | tf_op jit(solution)/shard_map/ppermute | solution.py:17
  75.6 1.9 %collective-permute-start.21 = (bf16[128,1024]{1,0:T(8,128)(2,1)S(1)}, bf16[128,1024]{1,0:T(8,128)(2,1)S(1)}, u32[]{:S(2)}, u32[]{:S(2)}) collective-permute-start(bf16[128,1024]{1,0:T(8,128)(2,1)S(1)} %get-tuple-element.88), channel_id=1, source_target_pairs={{1,0},{0,1},{3,2},{2,3},{5,4},{4,5},{7,6},{6,7},{9,8},{8,9},{11,10... | collective-permute-start | bytes 786440 | tf_op jit(solution)/shard_map/ppermute | solution.py:17
  84.3 12.5 %collective-permute-start.24 = (bf16[64,1792]{1,0:T(8,128)(2,1)S(1)}, bf16[64,1792]{1,0:T(8,128)(2,1)S(1)}, u32[]{:S(2)}, u32[]{:S(2)}) collective-permute-start(bf16[64,1792]{1,0:T(8,128)(2,1)S(1)} %get-tuple-element.72), channel_id=1, source_target_pairs={{4,0},{0,4},{5,1},{1,5},{6,2},{2,6},{7,3},{3,7},{12,8},{8,12},{13,... | collective-permute-start | bytes 688136 | tf_op jit(solution)/shard_map/ppermute | solution.py:17
  85.5 11.3 %collective-permute-start.25 = (bf16[64,1792]{1,0:T(8,128)(2,1)S(1)}, bf16[64,1792]{1,0:T(8,128)(2,1)S(1)}, u32[]{:S(2)}, u32[]{:S(2)}) collective-permute-start(bf16[64,1792]{1,0:T(8,128)(2,1)S(1)} %get-tuple-element.73), channel_id=1, source_target_pairs={{0,6},{2,4},{4,2},{6,0},{1,7},{3,5},{5,3},{7,1},{8,14},{10,12},{12... | collective-permute-start | bytes 688136 | tf_op jit(solution)/shard_map/ppermute | solution.py:21
  87.6 9.2 %collective-permute-start.26 = (bf16[64,1536]{1,0:T(8,128)(2,1)S(1)}, bf16[64,1536]{1,0:T(8,128)(2,1)S(1)}, u32[]{:S(2)}, u32[]{:S(2)}) collective-permute-start(bf16[64,1536]{1,0:T(8,128)(2,1)S(1)} %get-tuple-element.75), channel_id=1, source_target_pairs={{24,0},{0,8},{8,16},{16,24},{25,1},{1,9},{9,17},{17,25},{26,2},{2,... | collective-permute-start | bytes 589832 | tf_op jit(solution)/shard_map/ppermute | solution.py:17
  88.3 8.5 %collective-permute-start.27 = (bf16[64,1536]{1,0:T(8,128)(2,1)S(1)}, bf16[64,1536]{1,0:T(8,128)(2,1)S(1)}, u32[]{:S(2)}, u32[]{:S(2)}) collective-permute-start(bf16[64,1536]{1,0:T(8,128)(2,1)S(1)} %get-tuple-element.76), channel_id=1, source_target_pairs={{8,0},{16,8},{24,16},{0,24},{9,1},{17,9},{25,17},{1,25},{10,2},{18... | collective-permute-start | bytes 589832 | tf_op jit(solution)/shard_map/ppermute | solution.py:17
  90.0 6.8 %collective-permute-start.23 = (bf16[64,1280]{1,0:T(8,128)(2,1)S(1)}, bf16[64,1280]{1,0:T(8,128)(2,1)S(1)}, u32[]{:S(2)}, u32[]{:S(2)}) collective-permute-start(bf16[64,1280]{1,0:T(8,128)(2,1)S(1)} %get-tuple-element.71), channel_id=1, source_target_pairs={{2,0},{0,2},{3,1},{1,3},{6,4},{4,6},{7,5},{5,7},{10,8},{8,10},{11,... | collective-permute-start | bytes 491528 | tf_op jit(solution)/shard_map/ppermute | solution.py:17
  96.9 9.6 %collective-permute-start.30 = (bf16[64,2048]{1,0:T(8,128)(2,1)S(1)}, bf16[64,2048]{1,0:T(8,128)(2,1)S(1)}, u32[]{:S(2)}, u32[]{:S(2)}) collective-permute-start(bf16[64,2048]{1,0:T(8,128)(2,1)S(1)} %get-tuple-element.83), channel_id=1, source_target_pairs={{16,0},{24,8},{0,16},{8,24},{17,1},{25,9},{1,17},{9,25},{18,2},{26... | collective-permute-start | bytes 786440 | tf_op jit(solution)/shard_map/ppermute | solution.py:17
  98.7 6.0 %collective-permute-start.28 = (bf16[64,512]{1,0:T(8,128)(2,1)S(1)}, bf16[64,512]{1,0:T(8,128)(2,1)S(1)}, u32[]{:S(2)}, u32[]{:S(2)}) collective-permute-start(bf16[64,512]{1,0:T(8,128)(2,1)S(1)} %get-tuple-element.81), channel_id=1, source_target_pairs={{24,0},{0,8},{8,16},{16,24},{25,1},{1,9},{9,17},{17,25},{26,2},{2,... | collective-permute-start | bytes 196616 | tf_op jit(solution)/shard_map/ppermute | solution.py:17
  100.7 5.7 %collective-permute-start.29 = (bf16[64,512]{1,0:T(8,128)(2,1)S(1)}, bf16[64,512]{1,0:T(8,128)(2,1)S(1)}, u32[]{:S(2)}, u32[]{:S(2)}) collective-permute-start(bf16[64,512]{1,0:T(8,128)(2,1)S(1)} %get-tuple-element.82), channel_id=1, source_target_pairs={{8,0},{16,8},{24,16},{0,24},{9,1},{17,9},{25,17},{1,25},{10,2},{18... | collective-permute-start | bytes 196616 | tf_op jit(solution)/shard_map/ppermute | solution.py:17
